TPU v7x, 32 devices: a whole 2x2x4 slice. The times are simulated.
32 devices in a mesh: row: 4 (over y, core), col: 8 (over z, x).
Axes of the slice: x: 2, y: 2, z: 4, core: 2. Of those that a mesh axis runs over, the one named last changes fastest.
Arguments:
- kkt: float32 [2048, 2048], P('row', 'col'), may hold values from -4 to 4, as said below
- swaps: int32 [2, 2, 128], replicated, may hold values from 0 to 2047, as said below
- inverses: float32 [2, 256, 256], replicated
- pivots: float32 [2, 256], replicated, may hold values from -0.12 to 0.12
- couplings: float32 [2, 256], replicated, may hold values from -0.12 to 0.12
- pattern: int32 [2, 256], replicated, may hold values from 0 to 1, as said below
Outputs:
- factored: float32 [2048, 2048], P('row', 'col')
Inputs may be any that keep to these rules, and one draw needn't show every extreme that they name: For panel k, swaps[k, 0, :] holds 128 distinct rows among k * 256 to k * 256 + 255, both ends of that range among them, and swaps[k, 1, :] holds 128 distinct rows among (k + 1) * 256 to 2047, both ends of that range among them. pattern[k, i] = 1 makes rows i and i + 1 one 2 x 2 block of D; no two neighbouring entries are both 1 and the last entry is 0. kkt is the stored order of a symmetric matrix.
All inputs are finite; a program needn't handle non-finite values.
Results may differ from a plain program's by a relative error of at most 0.00014.
Values sent between devices are 32-bit elements; how exact they have to be, the bound alone decides.
No kernel may reach another device: no remote copies, remote signals or barrier semaphores. Data moves between devices by JAX's collectives and lax.ppermute only.
A program may use at most 64 MiB of HBM per device.

v0:
```python
import jax
import jax.numpy as jnp
from jax import lax
from jax.sharding import PartitionSpec as P

highest_prec = lax.Precision.HIGHEST


def spread(shard, axis, root):
    mine = lax.axis_index(axis) == root
    return lax.psum(jnp.where(mine, shard, jnp.zeros_like(shard)), axis)


def scale_cols(lower_rows, pivot_row, coupling_row, pattern_row):
    links = coupling_row * pattern_row.astype(jnp.float32)
    zero_col = jnp.zeros((lower_rows.shape[0], 1), lower_rows.dtype)
    after = jnp.concatenate([lower_rows[:, 1:], zero_col], axis=1)
    before = jnp.concatenate([zero_col, lower_rows[:, :-1]], axis=1)
    links_before = jnp.concatenate([jnp.zeros((1,), links.dtype), links[:-1]])
    return lower_rows * pivot_row + after * links + before * links_before


def pick_lines(local_block, sources, group_count, my_index, tile_width, along):
    tile_idx = sources // tile_width
    is_owned = tile_idx % group_count == my_index
    local_idx = jnp.where(is_owned, tile_idx // group_count * tile_width + sources % tile_width, 0)
    taken = jnp.take(local_block, local_idx, axis=along)
    if along == 0:
        return jnp.where(is_owned[:, None], taken, 0.0)
    return jnp.where(is_owned[None, :], taken, 0.0)


def place_lines(local_block, targets, arrived, group_count, my_index, tile_width, along):
    tile_idx = targets // tile_width
    is_owned = tile_idx % group_count == my_index
    local_idx = jnp.where(
        is_owned,
        tile_idx // group_count * tile_width + targets % tile_width,
        local_block.shape[along],
    )
    if along == 0:
        return local_block.at[local_idx].set(arrived, mode="drop")
    return local_block.at[:, local_idx].set(arrived, mode="drop")


def shards(kkt, swaps, inverses, pivots, couplings, pattern):
    rows_dev, cols_dev = kkt.shape
    tile_width = inverses.shape[1]
    row_groups = lax.axis_size("row")
    col_groups = lax.axis_size("col")
    row_index = lax.axis_index("row")
    col_index = lax.axis_index("col")
    tiles_row = rows_dev // tile_width
    tiles_col = cols_dev // tile_width
    row_positions = jnp.arange(rows_dev, dtype=jnp.int32)
    col_positions = jnp.arange(cols_dev, dtype=jnp.int32)
    row_tiles = row_positions // tile_width * row_groups + row_index
    col_tiles = col_positions // tile_width * col_groups + col_index
    matrix = kkt
    for panel in range(2):
        have_panel = False
        leads = swaps[panel, 0]
        partners = swaps[panel, 1]
        targets = jnp.concatenate([leads, partners])
        sources = jnp.concatenate([partners, leads])
        arrived = lax.psum(pick_lines(matrix, sources, row_groups, row_index, tile_width, 0), "row")
        matrix = place_lines(matrix, targets, arrived, row_groups, row_index, tile_width, 0)
        have_panel = True
        before_tile = spread(matrix, "col", panel % col_groups)
        partner_lines = lax.psum(
            pick_lines(matrix, partners, col_groups, col_index, tile_width, 1), "col"
        )
        lead_offsets = leads - panel * tile_width
        lead_lines = jnp.take(before_tile, lead_offsets, axis=1)
        matrix = place_lines(matrix, leads, partner_lines, col_groups, col_index, tile_width, 1)
        matrix = place_lines(matrix, partners, lead_lines, col_groups, col_index, tile_width, 1)
        panel_cols = before_tile.at[:, lead_offsets].set(partner_lines)
        row_tail = row_tiles > panel
        col_tail = col_tiles > panel
        product = jnp.dot(
            panel_cols, inverses[panel], precision=highest_prec, preferred_element_type=jnp.float32
        )
        lower_rows = jnp.where(row_tail[:, None], product, 0.0)
        held_tiles = (jnp.arange(tiles_col, dtype=jnp.int32) * col_groups + col_index) // row_groups
        picked = jnp.take(
            lower_rows.reshape(tiles_row, tile_width, tile_width), held_tiles, axis=0
        ).reshape(cols_dev, tile_width)
        lower_cols = spread(picked, "row", col_index % row_groups)
        scaled_cols = scale_cols(lower_cols, pivots[panel], couplings[panel], pattern[panel])
        update = lax.dot_general(
            lower_rows,
            scaled_cols,
            (((1,), (1,)), ((), ())),
            precision=highest_prec,
            preferred_element_type=jnp.float32,
        )
        matrix = matrix - update
        panel_block = jnp.where(
            (col_index == panel % col_groups) & row_tail[:, None], lower_rows, matrix
        )
        matrix = matrix.at[:, 0:tile_width].set(panel_block)
        top_block = jnp.where(
            (row_index == panel % row_groups) & col_tail[None, :],
            scaled_cols.T,
            matrix[0:tile_width, :],
        )
        matrix = matrix.at[0:tile_width, :].set(top_block)
    return matrix


def solution(mesh):
    return jax.shard_map(
        shards,
        mesh=mesh,
        in_specs=(P("row", "col"), P(), P(), P(), P(), P()),
        out_specs=P("row", "col"),
        check_vma=False,
    )
```

profile of v0, /device:TPU:0, one launch (start us, length us, event | category | flops | bytes accessed | tf_op | source)
XLA Modules:
  0.0 328.6 jit_solution(16383741696120624056)
XLA Ops:
  6.5 1.0 copy.50
  7.6 0.7 copy-done.5
  8.3 1.0 gather_fusion
  9.3 0.8 select_select_fusion.3
  10.3 0.6 copy-done.6
  11.0 34.0 %all-reduce.13.cloned.1.call-done = f32[256,256]{1,0:T(8,128)} async-done(((f32[256,256]{1,0:T(8,128)}), f32[256,256]{1,0:T(8,128)}) %all-reduce.13.cloned.1.call-update) | async-done | bytes 262160 | tf_op jit(solution)/shard_map/psum | solution.py:66
  45.0 2.0 scatter_fusion
  47.0 0.2 copy.17
  47.2 0.8 broadcast_select_fusion.1
  48.1 0.8 gather_fusion.1
  48.8 0.8 bitcast_select_fusion.1
  49.7 0.1 pad_maximum_fusion.1
  49.9 0.6 copy-done.8
  50.5 74.2 %all-reduce.23.cloned.1.call-done = (f32[512,256]{1,0:T(8,128)}, f32[512,128]{0,1:T(8,128)}) async-done(((f32[512,256]{1,0:T(8,128)}, f32[512,128]{0,1:T(8,128)}), (f32[512,256]{1,0:T(8,128)}, f32[512,128]{0,1:T(8,128)})) %all-reduce.23.cloned.1.call-update) | async-done | bytes 786448 | tf_op jit(solution)/shard_map/psum | solution.py:11
  124.7 1.3 copy.18
  126.0 1.2 scatter_custom_fusion.2
  127.3 1.7 scatter_custom_fusion.3
  129.0 1.2 scatter_custom_fusion.1
  130.2 1.0 convolution_select_fusion.1
  131.3 0.1 copy.29
  131.4 0.7 fusion.17
  132.2 0.2 copy.22
  132.4 30.8 %all-reduce.15.cloned.1.call-done = f32[256,256]{0,1:T(8,128)} async-done(((f32[256,256]{0,1:T(8,128)}), f32[256,256]{0,1:T(8,128)}) %all-reduce.15.cloned.1.call-update) | async-done | bytes 262160 | tf_op jit(solution)/shard_map/psum | solution.py:11
  163.3 1.1 fusion.64
  164.4 0.2 multiply_add_fusion.1
  164.6 0.6 fusion.1
  165.2 1.0 gather_fusion.2
  166.2 0.8 select_select_fusion.1
  167.2 32.0 %all-reduce.17.cloned.1.call-done = f32[256,256]{1,0:T(8,128)} async-done(((f32[256,256]{1,0:T(8,128)}), f32[256,256]{1,0:T(8,128)}) %all-reduce.17.cloned.1.call-update) | async-done | bytes 262160 | tf_op jit(solution)/shard_map/psum | solution.py:66
  199.2 2.0 scatter_fusion.1
  201.2 0.2 copy.23
  201.4 0.8 broadcast_select_fusion
  202.3 0.8 gather_fusion.3
  203.0 0.8 bitcast_select_fusion
  203.9 74.9 %all-reduce.21.cloned.1.call-done = (f32[512,256]{1,0:T(8,128)}, f32[512,128]{0,1:T(8,128)}) async-done(((f32[512,256]{1,0:T(8,128)}, f32[512,128]{0,1:T(8,128)}), (f32[512,256]{1,0:T(8,128)}, f32[512,128]{0,1:T(8,128)})) %all-reduce.21.cloned.1.call-update) | async-done | bytes 786448 | tf_op jit(solution)/shard_map/psum | solution.py:11
  278.9 1.3 copy.24
  280.2 1.2 scatter_custom_fusion.6
  281.4 1.7 scatter_custom_fusion.7
  283.1 1.2 scatter_custom_fusion.5
  284.4 1.0 convolution_select_fusion
  285.4 0.1 copy.30
  285.5 0.7 fusion.14
  286.4 0.2 copy.28
  286.6 30.8 %all-reduce.19.cloned.1.call-done = f32[256,256]{0,1:T(8,128)} async-done(((f32[256,256]{0,1:T(8,128)}), f32[256,256]{0,1:T(8,128)}) %all-reduce.19.cloned.1.call-update) | async-done | bytes 262160 | tf_op jit(solution)/shard_map/psum | solution.py:11
  317.4 1.1 fusion.63
  318.6 0.2 multiply_add_fusion
  318.7 1.4 fusion
  320.1 1.7 fusion.2
  (53 shorter events, 0.8 us)
Async XLA Ops:
  6.5 38.4 %all-reduce.13.cloned.1.call-start = ((), (), s32[]{:S(2)}) async-start(), calls=%async_computation | async-start | bytes 524288 | tf_op jit(solution)/shard_map/psum | solution.py:66
  7.6 0.7 copy-start.5
  10.2 114.5 %all-reduce.23.cloned.1.call-start = ((), (), s32[]{:S(2)}) async-start(), calls=%async_computation.5 | async-start | bytes 1572864 | tf_op jit(solution)/shard_map/psum | solution.py:11
  10.3 0.7 copy-start.6
  10.3 0.7 copy-start.7
  49.6 113.6 %all-reduce.15.cloned.1.call-start = ((), (), s32[]{:S(2)}) async-start(), calls=%async_computation.1 | async-start | bytes 524288 | tf_op jit(solution)/shard_map/psum | solution.py:11
  49.9 0.7 copy-start.8
  124.7 1.3 copy-start.2
  128.9 1.3 copy-start.4
  132.2 67.0 %all-reduce.17.cloned.1.call-start = ((), (), s32[]{:S(2)}) async-start(), calls=%async_computation.2 | async-start | bytes 524288 | tf_op jit(solution)/shard_map/psum | solution.py:66
  163.3 1.1 copy-start
  167.1 111.8 %all-reduce.21.cloned.1.call-start = ((), (), s32[]{:S(2)}) async-start(), calls=%async_computation.4 | async-start | bytes 1572864 | tf_op jit(solution)/shard_map/psum | solution.py:11
  203.9 113.6 %all-reduce.19.cloned.1.call-start = ((), (), s32[]{:S(2)}) async-start(), calls=%async_computation.3 | async-start | bytes 524288 | tf_op jit(solution)/shard_map/psum | solution.py:11
  278.9 1.3 copy-start.3
  317.4 1.1 copy-start.1
Sparse Core Ops, SparseCore 0:
  10.3 34.6 all-reduce.12
  49.8 74.8 all-reduce.22
  132.3 30.9 all-reduce.14
  167.2 31.9 all-reduce.16
  204.0 74.8 all-reduce.20
  286.4 30.9 all-reduce.18
where the time goes:
time: 329 us
  waiting for transfers between devices  277 us (84%)
  local copies, waits for them, and re-layouts  21.5 us (7%)
  between operations  13.9 us (4%)
  other arithmetic  12.3 us (4%)
  matrix products  3.96 us (1%)
    psum x4, waiting for transfers between devices, spread(): return lax.psum(jnp.where(mine, shard, jnp.zeros_like(shard)), axis)  211 us
    psum x2, waiting for transfers between devices, shards(): lax.psum(pick_lines(matrix, sources, row_groups, row_index, tile_width, 0...  66 us
  transfers between devices with their start and end apart: 6, of which 6 were waited for; matrix products, arithmetic and copies ran while one was open for 0% of the time, Pallas kernels for 0%

commit v1 on v0

v1 whole, which is shorter than its diff:
```python
import functools

import jax
import jax.numpy as jnp
from jax import lax
from jax.experimental import pallas as pl
from jax.experimental.pallas import tpu as pltpu
from jax.sharding import PartitionSpec as P

f32 = jnp.float32
bf16 = jnp.bfloat16
VMEM_LIMIT = 48 * 1024 * 1024


def split(value):
    high = value.astype(bf16)
    return high, (value - high.astype(f32)).astype(bf16)


def mm(left, right, dims=(((1,), (0,)), ((), ()))):
    left_high, left_low = split(left)
    right_high, right_low = split(right)
    dot = functools.partial(lax.dot_general, dimension_numbers=dims, preferred_element_type=f32)
    return dot(left_high, right_high) + (dot(left_high, right_low) + dot(left_low, right_high))


def mm_nt(left, right):
    return mm(left, right, (((1,), (1,)), ((), ())))


def pick_rows(chosen, value):
    width = value.shape[1]
    both = jnp.dot(chosen, jnp.concatenate(split(value), axis=1), preferred_element_type=f32)
    return both[:, :width] + both[:, width:]


def pick_cols(value, chosen):
    height = value.shape[0]
    both = jnp.dot(jnp.concatenate(split(value), axis=0), chosen, preferred_element_type=f32)
    return both[:height] + both[height:]


def ones_where(mask):
    return jnp.where(mask, 1.0, 0.0).astype(bf16)


def scale(lower, factors, panel):
    pivot, link, link_before = (factors[3 * panel + i : 3 * panel + i + 1, :] for i in range(3))
    width = lower.shape[1]
    after = pltpu.roll(lower, width - 1, 1)
    before = pltpu.roll(lower, 1, 1)
    return lower * pivot + after * link + before * link_before


def call(body, outs, *args, smem=0, scratch=()):
    vmem = pl.BlockSpec(memory_space=pltpu.VMEM)
    return pl.pallas_call(
        body,
        out_shape=[jax.ShapeDtypeStruct(shape, f32) for shape in outs],
        in_specs=[pl.BlockSpec(memory_space=pltpu.SMEM)] * smem + [vmem] * (len(args) - smem),
        out_specs=[vmem] * len(outs),
        scratch_shapes=list(scratch),
        compiler_params=pltpu.CompilerParams(vmem_limit_bytes=VMEM_LIMIT),
    )(*args)


def gather_moved(me, source, row_ids, block, keep, send):
    rows = pick_rows(ones_where(source[...] == row_ids[...]), block[...])
    half = keep.shape[0]
    odd = me[2] == 1
    keep[...] = jnp.where(odd, rows[half:], rows[:half])
    send[...] = jnp.where(odd, rows[:half], rows[half:])


def place_moved(me, target, row_ids, block, mine, other, out):
    odd = me[2] == 1
    first = jnp.where(odd, other[...], mine[...])
    second = jnp.where(odd, mine[...], other[...])
    hit = row_ids[...] == target[...]
    moved = jnp.max(jnp.where(hit, 1, 0), axis=1, keepdims=True) > 0
    rows = pick_rows(ones_where(hit), jnp.concatenate([first, second], axis=0))
    out[...] = jnp.where(moved, rows, block[...])


def pick_columns(lead_tiles, source, whole, out):
    piece = out.shape[0]
    tile = whole.shape[1]
    lead = lead_tiles * tile
    wanted = source[...]
    index = lax.broadcasted_iota(jnp.int32, (tile, 1), 0)
    total = None
    for t in range(whole.shape[0] // piece):
        block = jnp.concatenate(split(whole[t * piece : (t + 1) * piece, :]), axis=0)
        part = wanted if t < lead_tiles else wanted[:, :lead]
        term = jnp.dot(block, ones_where(index + t * tile == part), preferred_element_type=f32)
        if total is None:
            total = term
        elif t < lead_tiles:
            total = total + term
        else:
            total = jnp.concatenate([total[:, :lead] + term, total[:, lead:]], axis=1)
    out[...] = total[:piece] + total[piece:]


def assemble(order, *refs):
    out = refs[-1]
    piece = refs[0].shape[0]
    for i, ref in enumerate(refs[:-1]):
        out[pl.ds(pl.multiple_of(order[i] * piece, piece), piece), :] = ref[...]


def first_panel(me, rows, target, col_ids, row_ids, block, own, inverse, factors, out, lower, lower_own):
    tile = own.shape[0]
    row, col = me[0], me[1]
    first = rows[:, :tile]
    second = rows[:, tile : 2 * tile]
    hit = target[...] == col_ids[...]
    moved = jnp.max(jnp.where(hit, 1, 0), axis=0, keepdims=True) > 0
    swapped = pick_cols(rows[:, 2 * tile :], ones_where(hit))
    matrix = jnp.where(moved, swapped, block[...])
    matrix = jnp.where(col == 0, first, jnp.where(col == 1, second, matrix))
    tail = row_ids[...] >= tile
    low = jnp.where(tail, mm(first, inverse[...]), 0.0)
    low_own = jnp.where(col > 0, mm(own[:, :tile], inverse[...]), 0.0)
    scaled = scale(low_own, factors, 0)
    matrix = matrix - mm_nt(low, scaled)
    matrix = jnp.where(jnp.logical_and(tail, col == 0), low, matrix)
    lower[...] = low
    lower_own[...] = low_own
    out[...] = matrix

    @pl.when(jnp.logical_and(row == 0, col > 0))
    def _():
        out[:tile, :] = scaled.T


def second_panel(
    me, rows, row_ids, matrix, own, lower, lower_own, corner, inverse0, inverse1, factors, out
):
    tile = own.shape[0]
    row, col = me[0], me[1]
    scaled_corner = scale(mm(corner[...], inverse0[...]), factors, 0)
    tail = row_ids[...] >= 2 * tile
    low = rows[:, tile : 2 * tile] - mm_nt(lower[...], scaled_corner)
    low = jnp.where(tail, mm(low, inverse1[...]), 0.0)
    low_own = own[:, tile : 2 * tile] - mm_nt(lower_own[...], scaled_corner)
    low_own = jnp.where(col > 1, mm(low_own, inverse1[...]), 0.0)
    scaled = scale(low_own, factors, 1)
    result = matrix[...] - mm_nt(low, scaled)
    out[...] = jnp.where(jnp.logical_and(tail, col == 1), low, result)

    @pl.when(jnp.logical_and(row == 1, col > 1))
    def _():
        out[:tile, :] = scaled.T


def through(values, leads, partners):
    hit = values[:, None] == partners[None, :]
    return jnp.where(jnp.any(hit, 1), jnp.sum(jnp.where(hit, leads[None, :], 0), 1), values)


def shards(kkt, swaps, inverses, pivots, couplings, pattern):
    height, tile = kkt.shape
    panels, _, amount = swaps.shape
    rows_axis = lax.axis_size("row")
    cols_axis = lax.axis_size("col")
    row = lax.axis_index("row")
    col = lax.axis_index("col")
    piece = height // cols_axis
    lead = panels * tile

    lead0, partner0 = swaps[0, 0], swaps[0, 1]
    lead1, partner1 = swaps[1, 0], swaps[1, 1]
    target = jnp.concatenate([lead0, partner0, lead1, partner1])
    source = jnp.concatenate(
        [partner0, lead0, through(partner1, lead0, partner0), through(lead1, lead0, partner0)]
    )
    again = jnp.any(partner0[:, None] == jnp.concatenate([lead1, partner1])[None, :], 1)
    none = jnp.full((amount,), -1, jnp.int32)
    target = jnp.concatenate([lead0, jnp.where(again, none, partner0), lead1, partner1])

    lead_ids = jnp.arange(lead, dtype=jnp.int32)
    hit = lead_ids[:, None] == target[None, :]
    lead_source = jnp.where(jnp.any(hit, 1), jnp.sum(jnp.where(hit, source[None, :], 0), 1), lead_ids)
    moved_source = jnp.concatenate([source[amount : 2 * amount], source[3 * amount :]])
    col_source = jnp.concatenate([lead_source, moved_source])[None, :]
    col_target = jnp.concatenate([target[amount : 2 * amount], target[3 * amount :]])[:, None]

    position = jnp.arange(height, dtype=jnp.int32)
    row_ids = (position // tile * rows_axis + row) * tile + position % tile
    col_ids = (col * tile + jnp.arange(tile, dtype=jnp.int32))[None, :]
    links = couplings * pattern.astype(f32)
    ends = jnp.zeros((panels, 1), f32)
    links_after = jnp.concatenate([links[:, :-1], ends], axis=1)
    links_before = jnp.concatenate([ends, links[:, :-1]], axis=1)
    factors = jnp.stack([pivots, links_after, links_before], axis=1).reshape(3 * panels, tile)
    me = jnp.stack([row, col, row % 2]).astype(jnp.int32)

    def flip(value, bit):
        return lax.ppermute(value, "row", [(i, i ^ bit) for i in range(rows_axis)])

    half = panels * amount
    keep, send = call(
        gather_moved,
        [(half, tile)] * 2,
        me,
        source[:, None],
        row_ids[None, :],
        kkt,
        smem=1,
    )
    mine = keep + flip(send, 1)
    bit = 2
    while bit < rows_axis:
        mine = mine + flip(mine, bit)
        bit *= 2
    other = flip(mine, 1)
    (block,) = call(
        place_moved,
        [(height, tile)],
        me,
        target[None, :],
        row_ids[:, None],
        kkt,
        mine,
        other,
        smem=1,
    )

    whole = lax.all_to_all(block, "col", 0, 0, tiled=True)
    (part,) = call(
        functools.partial(pick_columns, panels), [(piece, col_source.shape[1])], col_source, whole
    )
    ring = list(range(0, cols_axis, 2)) + list(range(cols_axis - 1, 0, -2))
    after = [(ring[i], ring[(i + 1) % cols_axis]) for i in range(cols_axis)]
    before = [(b, a) for a, b in after]
    right, left = part, part
    parts, steps = [part], [0]
    for step in range(1, cols_axis // 2 + 1):
        right = lax.ppermute(right, "col", after)
        parts.append(right)
        steps.append(-step)
        if step < cols_axis // 2:
            left = lax.ppermute(left, "col", before)
            parts.append(left)
            steps.append(step)
    place = jnp.where(col % 2 == 0, col // 2, cols_axis - 1 - col // 2)
    order = (place + jnp.array(steps, jnp.int32)) % cols_axis
    order = jnp.where(order < cols_axis // 2, 2 * order, 2 * (cols_axis - 1 - order) + 1)
    (rows,) = call(assemble, [(height, col_source.shape[1])], order, *parts, smem=1)

    pieces = tile // piece
    own = lax.ppermute(
        part[:, :lead],
        ("row", "col"),
        [
            (t % rows_axis * cols_axis + t // rows_axis * pieces + i, i * cols_axis + t)
            for t in range(cols_axis)
            for i in range(pieces)
        ],
    )
    own = lax.all_gather(own, "row", tiled=True)

    corner = jnp.where(row == 1, rows[:tile, :tile], 0.0)
    bit = 2
    holders = [1]
    while bit < rows_axis:
        corner = corner + lax.ppermute(corner, "row", [(i, i ^ bit) for i in holders])
        holders += [i ^ bit for i in holders]
        bit *= 2
    corner = corner + lax.ppermute(corner, "row", [(i, i ^ 1) for i in holders])

    matrix, lower, lower_own = call(
        first_panel,
        [(height, tile), (height, tile), (tile, tile)],
        me,
        rows,
        col_target,
        col_ids,
        row_ids[:, None],
        block,
        own,
        inverses[0],
        factors,
        smem=1,
    )
    (out,) = call(
        second_panel,
        [(height, tile)],
        me,
        rows,
        row_ids[:, None],
        matrix,
        own,
        lower,
        lower_own,
        corner,
        inverses[0],
        inverses[1],
        factors,
        smem=1,
    )
    return out


def solution(mesh):
    return jax.shard_map(
        shards,
        mesh=mesh,
        in_specs=(P("row", "col"), P(), P(), P(), P(), P()),
        out_specs=P("row", "col"),
        check_vma=False,
    )
```

time: 329 us -> 89.2 us (0.27)
  waiting for transfers between devices: 277 us -> 39.6 us
  starting transfers between devices: 0.21 us -> 20.3 us
  local copies, waits for them, and re-layouts: 21.5 us -> 2.25 us
  blocking collectives: 0 us -> 14 us
  between operations: 13.9 us -> 0.31 us
  other arithmetic: 12.3 us -> 2.08 us
  Pallas kernels: 0 us -> 10.2 us
  matrix products: 3.96 us -> 0 us
    psum x6 -> x0, waiting for transfers between devices: 277 us -> none  [the longest x4 211 us: spread(): return lax.psum(jnp.where(mine, shard, jnp.zeros_like(shard)), axis)]
    ppermute x0 -> x13, waiting for transfers between devices: none -> 25.2 us  [the longest x4 16 us: shards(): right = lax.ppermute(right, 'col', after)]
    all_to_all x0 -> x1, waiting for transfers between devices: none -> 14.4 us  [shards(): whole = lax.all_to_all(block, 'col', 0, 0, tiled=True)]
    ppermute x0 -> x13, starting transfers between devices: none -> 14.3 us  [the longest x4 4.4 us: shards(): right = lax.ppermute(right, 'col', after)]
    all_gather x0 -> x1, blocking collectives: none -> 14 us  [shards(): own = lax.all_gather(own, 'row', tiled=True)]
    pallas_call x0 -> x6, Pallas kernels: none -> 10.2 us  [call(): pl.pallas_call(body, out_shape=[jax.ShapeDtypeStruct(shape, f32) for shap...]
    scatter x10 -> x0, local copies, waits for them, and re-layouts: 9.86 us -> none  [the longest x4 4.47 us: place_lines(): return local_block.at[local_idx].set(arrived, mode='drop')]
    all_to_all x0 -> x1, starting transfers between devices: none -> 6.03 us  [shards(): whole = lax.all_to_all(block, 'col', 0, 0, tiled=True)]
  transfers between devices with their start and end apart: 6 -> 14, of which waited for: 6 -> 8; matrix products, arithmetic and copies ran while one was open for 0% -> 1% of each run, Pallas kernels for 0% -> 3%
where the time goes in v1:
time: 89.2 us; the launch traced here: 88.8 us
  waiting for transfers between devices  39.6 us (44%)
  starting transfers between devices  20.3 us (23%)
  blocking collectives  14 us (16%)
  Pallas kernels  10.2 us (11%)
  local copies, waits for them, and re-layouts  2.25 us (3%)
  other arithmetic  2.08 us (2%)
    ppermute x4, waiting for transfers between devices, shards(): right = lax.ppermute(right, 'col', after)  16 us
    all_to_all x1, waiting for transfers between devices, shards(): whole = lax.all_to_all(block, 'col', 0, 0, tiled=True)  14.4 us
    all_gather x1, blocking collectives, shards(): own = lax.all_gather(own, 'row', tiled=True)  14 us
    pallas_call x6, Pallas kernels, call(): pl.pallas_call(body, out_shape=[jax.ShapeDtypeStruct(shape, f32) for shap...  10.2 us
    ppermute x3, waiting for transfers between devices, flip(): return lax.ppermute(value, 'row', [(i, i ^ bit) for i in range(rows_axis)])  9.22 us
    all_to_all x1, starting transfers between devices, shards(): whole = lax.all_to_all(block, 'col', 0, 0, tiled=True)  6.03 us
    ppermute x4, starting transfers between devices, shards(): right = lax.ppermute(right, 'col', after)  4.4 us
    ppermute x3, starting transfers between devices, shards(): left = lax.ppermute(left, 'col', before)  3.73 us
  transfers between devices with their start and end apart: 14, of which 8 were waited for; matrix products, arithmetic and copies ran while one was open for 1% of the time, Pallas kernels for 3%

profile of v1, /device:TPU:0, one launch (start us, length us, event | category | flops | bytes accessed | tf_op | source)
XLA Modules:
  0.0 88.8 jit_solution(3806413049027264337)
XLA Ops:
  0.0 0.8 slice_bitcast_fusion.5
  0.8 0.2 compare_reduce_fusion.2
  1.0 0.2 fusion.12
  1.2 0.2 compare_reduce_fusion
  1.3 0.8 fusion.20
  2.1 0.1 copy.12.source
  2.3 0.1 pad_add_fusion.5.me
  2.4 1.0 %copy-done = f32[512,256]{1,0:T(8,128)S(1)} copy-done((f32[512,256]{1,0:T(8,128)S(1)}, f32[512,256]{1,0:T(8,128)}, u32[]{:S(2)}) %copy-start) | copy-done | bytes 524312
  3.4 1.0 %shard_map.73 = (f32[256,256]{1,0:T(8,128)S(1)}, f32[256,256]{1,0:T(8,128)S(1)}) custom-call(s32[3]{0:T(128)S(1)} %pad_add_fusion.5.me, s32[512,1]{1,0:T(8,128)S(1)} %copy.12.source, s32[1,512]{1,0:T(1,128)S(1)} %fusion.14.row_ids, f32[512,256]{1,0:T(8,128)S(1)} %copy-done), custom_call_target="tpu_custom_call" | custom-call | tf_op jit(solution)/shard_map/pallas_call | solution.py:57
  4.4 0.5 collective-permute-start
  5.0 1.2 %collective-permute-done = f32[256,256]{1,0:T(8,128)S(1)} collective-permute-done((f32[256,256]{1,0:T(8,128)S(1)}, f32[256,256]{1,0:T(8,128)S(1)}, u32[]{:S(2)}, u32[]{:S(2)}) %collective-permute-start) | collective-permute-done | bytes 262176 | tf_op jit(solution)/shard_map/ppermute | solution.py:200
  6.2 3.0 %collective-permute-start.1 = (f32[256,256]{1,0:T(8,128)S(1)}, f32[256,256]{1,0:T(8,128)S(1)}, u32[]{:S(2)}, u32[]{:S(2)}) collective-permute-start(f32[256,256]{1,0:T(8,128)S(1)} %add.144), channel_id=1, source_target_pairs={{0,16},{8,24},{16,0},{24,8},{1,17},{9,25},{17,1},{25,9},{2,18},{10... | collective-permute-start | bytes 786440 | tf_op jit(solution)/shard_map/ppermute | solution.py:200
  9.1 6.6 %collective-permute-done.1 = f32[256,256]{1,0:T(8,128)S(1)} collective-permute-done((f32[256,256]{1,0:T(8,128)S(1)}, f32[256,256]{1,0:T(8,128)S(1)}, u32[]{:S(2)}, u32[]{:S(2)}) %collective-permute-start.1) | collective-permute-done | bytes 262176 | tf_op jit(solution)/shard_map/ppermute | solution.py:200
  15.8 0.1 collective-permute-start.2
  15.8 0.1 fusion.10.row_ids
  15.9 1.4 %collective-permute-done.2.other = f32[256,256]{1,0:T(8,128)S(1)} collective-permute-done((f32[256,256]{1,0:T(8,128)S(1)}, f32[256,256]{1,0:T(8,128)S(1)}, u32[]{:S(2)}, u32[]{:S(2)}) %collective-permute-start.2) | collective-permute-done | bytes 262176 | tf_op jit(solution)/shard_map/ppermute | solution.py:200
  17.4 0.0 copy-start.5
  17.4 0.0 copy-start.7
  17.4 1.9 %shard_map.74.block = f32[512,256]{1,0:T(8,128)} custom-call(s32[3]{0:T(128)S(1)} %pad_add_fusion.5.me, s32[1,512]{1,0:T(1,128)S(1)} %bitcast.33, s32[512,1]{1,0:T(8,128)S(1)} %fusion.10.row_ids, f32[512,256]{1,0:T(8,128)S(1)} %copy-done.1, f32[256,256]{1,0:T(8,128)S(1)} %add.145.mine, f32[256,256]{1,0:T(8,128)S(1)} %collective-permute-done.2.other), custom_call_target="tpu_custom_call" | custom-call | tf_op jit(solution)/shard_map/pallas_call | solution.py:57
  19.3 6.0 %all-to-all-start = ((f32[8,64,256]{2,1,0:T(8,128)}), f32[8,64,256]{2,1,0:T(8,128)S(1)}, u32[]{:S(2)}, u32[]{:S(2)}) async-start(f32[8,64,256]{2,1,0:T(8,128)} %bitcast.9), calls=%async_computation | async-start | bytes 1048576 | tf_op jit(solution)/shard_map/all_to_all | solution.py:230
  25.3 0.2 fusion
  25.5 0.2 select_reduce_fusion
  25.7 14.4 %all-to-all-done = f32[8,64,256]{2,1,0:T(8,128)S(1)} async-done(((f32[8,64,256]{2,1,0:T(8,128)}), f32[8,64,256]{2,1,0:T(8,128)S(1)}, u32[]{:S(2)}, u32[]{:S(2)}) %all-to-all-start) | async-done | bytes 524320 | tf_op jit(solution)/shard_map/all_to_all | solution.py:230
  40.1 0.5 shard_map.75.refs_0_
  40.6 0.8 collective-permute-start.3
  41.4 1.3 %collective-permute-start.4 = (f32[64,768]{1,0:T(8,128)S(1)}, f32[64,768]{1,0:T(8,128)S(1)}, u32[]{:S(2)}, u32[]{:S(2)}) collective-permute-start(f32[64,768]{1,0:T(8,128)S(1)} %shard_map.75.refs_0_), channel_id=1, source_target_pairs={{2,0},{4,2},{6,4},{7,6},{5,7},{3,5},{1,3},{0,1},{10,8},{12,10},{14... | collective-permute-start | bytes 589832 | tf_op jit(solution)/shard_map/ppermute | solution.py:244
  42.7 3.6 %collective-permute-done.3.refs_1_ = f32[64,768]{1,0:T(8,128)S(1)} collective-permute-done((f32[64,768]{1,0:T(8,128)S(1)}, f32[64,768]{1,0:T(8,128)S(1)}, u32[]{:S(2)}, u32[]{:S(2)}) %collective-permute-start.3) | collective-permute-done | bytes 196640 | tf_op jit(solution)/shard_map/ppermute | solution.py:240
  46.3 0.8 collective-permute-start.5
  47.1 0.0 collective-permute-done.4.refs_2_
  47.1 1.3 %collective-permute-start.6 = (f32[64,768]{1,0:T(8,128)S(1)}, f32[64,768]{1,0:T(8,128)S(1)}, u32[]{:S(2)}, u32[]{:S(2)}) collective-permute-start(f32[64,768]{1,0:T(8,128)S(1)} %collective-permute-done.4.refs_2_), channel_id=1, source_target_pairs={{2,0},{4,2},{6,4},{7,6},{5,7},{3,5},{1,3},{0,1},{10,8},{12,10},{14... | collective-permute-start | bytes 589832 | tf_op jit(solution)/shard_map/ppermute | solution.py:244
  48.4 3.9 %collective-permute-done.5.refs_3_ = f32[64,768]{1,0:T(8,128)S(1)} collective-permute-done((f32[64,768]{1,0:T(8,128)S(1)}, f32[64,768]{1,0:T(8,128)S(1)}, u32[]{:S(2)}, u32[]{:S(2)}) %collective-permute-start.5) | collective-permute-done | bytes 196640 | tf_op jit(solution)/shard_map/ppermute | solution.py:240
  52.3 1.1 %collective-permute-start.7 = (f32[64,768]{1,0:T(8,128)S(1)}, f32[64,768]{1,0:T(8,128)S(1)}, u32[]{:S(2)}, u32[]{:S(2)}) collective-permute-start(f32[64,768]{1,0:T(8,128)S(1)} %collective-permute-done.5.refs_3_), channel_id=1, source_target_pairs={{0,2},{2,4},{4,6},{6,7},{7,5},{5,3},{3,1},{1,0},{8,10},{10,12},{12... | collective-permute-start | bytes 589832 | tf_op jit(solution)/shard_map/ppermute | solution.py:240
  53.4 0.1 pad_bitcast_fusion
  53.5 1.1 %collective-permute-start.8 = (f32[64,768]{1,0:T(8,128)S(1)}, f32[64,768]{1,0:T(8,128)S(1)}, u32[]{:S(2)}, u32[]{:S(2)}) collective-permute-start(f32[64,768]{1,0:T(8,128)S(1)} %collective-permute-done.6.refs_4_), channel_id=1, source_target_pairs={{2,0},{4,2},{6,4},{7,6},{5,7},{3,5},{1,3},{0,1},{10,8},{12,10},{14... | collective-permute-start | bytes 589832 | tf_op jit(solution)/shard_map/ppermute | solution.py:244
  54.7 4.5 %collective-permute-done.7.refs_5_ = f32[64,768]{1,0:T(8,128)S(1)} collective-permute-done((f32[64,768]{1,0:T(8,128)S(1)}, f32[64,768]{1,0:T(8,128)S(1)}, u32[]{:S(2)}, u32[]{:S(2)}) %collective-permute-start.7) | collective-permute-done | bytes 196640 | tf_op jit(solution)/shard_map/ppermute | solution.py:240
  59.2 1.7 %collective-permute-start.9 = (f32[64,768]{1,0:T(8,128)S(1)}, f32[64,768]{1,0:T(8,128)S(1)}, u32[]{:S(2)}, u32[]{:S(2)}) collective-permute-start(f32[64,768]{1,0:T(8,128)S(1)} %collective-permute-done.7.refs_5_), channel_id=1, source_target_pairs={{0,2},{2,4},{4,6},{6,7},{7,5},{5,3},{3,1},{1,0},{8,10},{10,12},{12... | collective-permute-start | bytes 589832 | tf_op jit(solution)/shard_map/ppermute | solution.py:240
  60.9 0.0 collective-permute-done.8.refs_6_
  61.0 3.9 %collective-permute-done.9.refs_7_ = f32[64,768]{1,0:T(8,128)S(1)} collective-permute-done((f32[64,768]{1,0:T(8,128)S(1)}, f32[64,768]{1,0:T(8,128)S(1)}, u32[]{:S(2)}, u32[]{:S(2)}) %collective-permute-start.9) | collective-permute-done | bytes 196640 | tf_op jit(solution)/shard_map/ppermute | solution.py:240
  64.8 0.6 shard_map.76.rows
  65.5 0.7 collective-permute-start.11
  66.2 0.1 copy.14.target
  66.5 0.7 collective-permute-start.10
  67.1 0.0 collective-permute-done.11
  67.2 1.3 %collective-permute-start.12 = (f32[256,256]{1,0:T(8,128)S(1)}, f32[256,256]{1,0:T(8,128)S(1)}, u32[]{:S(2)}, u32[]{:S(2)}) collective-permute-start(f32[256,256]{1,0:T(8,128)S(1)} %fusion.21), channel_id=1, source_target_pairs={{8,0},{24,16},{9,1},{25,17},{10,2},{26,18},{11,3},{27,19},{12,4},{... | collective-permute-start | bytes 786440 | tf_op jit(solution)/shard_map/ppermute | solution.py:271
  68.5 14.0 %all_gather.3.own = f32[256,512]{1,0:T(8,128)S(1)} all-gather(f32[64,512]{1,0:T(8,128)S(1)} %collective-permute-done.10), channel_id=1, replica_groups=mesh['row'=4,'col'=8] {'row'}, dimensions={0}, use_global_device_ids=true | all-gather | bytes 655360 | tf_op jit(solution)/shard_map/all_gather | solution.py:262
  82.6 2.6 %shard_map.77 = (f32[512,256]{1,0:T(8,128)S(1)}, f32[512,256]{1,0:T(8,128)S(1)}, f32[256,256]{1,0:T(8,128)S(1)}) custom-call(s32[3]{0:T(128)S(1)} %pad_add_fusion.5.me, f32[512,768]{1,0:T(8,128)S(1)} %shard_map.76.rows, s32[256,1]{1,0:T(8,128)S(1)} %copy.14.target, s32[1,256]{1,0:T(1,128)S(1)} %iota_add_fusion.col_ids, s32[512,1]{1,0:T(8,128)S(1)} %fusion.10.row_ids, ...), custom_call_target="tpu_custom_call" | custom-call | tf_op jit(solution)/shard_map/pallas_call | solution.py:57
  85.2 0.0 collective-permute-done.12
  85.2 3.6 %shard_map.78 = f32[512,256]{1,0:T(8,128)} custom-call(s32[3]{0:T(128)S(1)} %pad_add_fusion.5.me, f32[512,768]{1,0:T(8,128)S(1)} %shard_map.76.rows, s32[512,1]{1,0:T(8,128)S(1)} %fusion.10.row_ids, f32[512,256]{1,0:T(8,128)S(1)} %get-tuple-element.12.matrix, f32[256,512]{1,0:T(8,128)S(1)} %all_gather.3.own, f32[512,256]{1,0:T(8,128)S(1)} %get-tuple-element.13.lower, ...), custom_call_target="tpu_custom_call" | custom-call | tf_op jit(solution)/shard_map/pallas_call | solution.py:57
  (35 shorter events, 0.3 us)
Async XLA Ops:
  2.4 1.0 %copy-start = (f32[512,256]{1,0:T(8,128)S(1)}, f32[512,256]{1,0:T(8,128)}, u32[]{:S(2)}) copy-start(f32[512,256]{1,0:T(8,128)} %block.3) | copy-start | bytes 1572868
  3.4 14.0 %copy-start.1 = (f32[512,256]{1,0:T(8,128)S(1)}, f32[512,256]{1,0:T(8,128)}, u32[]{:S(2)}) copy-start(f32[512,256]{1,0:T(8,128)} %block.3) | copy-start | bytes 1572868
  4.4 1.7 %collective-permute-start = (f32[256,256]{1,0:T(8,128)S(1)}, f32[256,256]{1,0:T(8,128)S(1)}, u32[]{:S(2)}, u32[]{:S(2)}) collective-permute-start(f32[256,256]{1,0:T(8,128)S(1)} %get-tuple-element.11), channel_id=1, source_target_pairs={{0,8},{8,0},{16,24},{24,16},{1,9},{9,1},{17,25},{25,17},{2,10},{10... | collective-permute-start | bytes 786440 | tf_op jit(solution)/shard_map/ppermute | solution.py:200
  6.2 9.6 %collective-permute-start.1 = (f32[256,256]{1,0:T(8,128)S(1)}, f32[256,256]{1,0:T(8,128)S(1)}, u32[]{:S(2)}, u32[]{:S(2)}) collective-permute-start(f32[256,256]{1,0:T(8,128)S(1)} %add.144), channel_id=1, source_target_pairs={{0,16},{8,24},{16,0},{24,8},{1,17},{9,25},{17,1},{25,9},{2,18},{10... | collective-permute-start | bytes 786440 | tf_op jit(solution)/shard_map/ppermute | solution.py:200
  15.8 1.6 %collective-permute-start.2 = (f32[256,256]{1,0:T(8,128)S(1)}, f32[256,256]{1,0:T(8,128)S(1)}, u32[]{:S(2)}, u32[]{:S(2)}) collective-permute-start(f32[256,256]{1,0:T(8,128)S(1)} %add.145.mine), channel_id=1, source_target_pairs={{0,8},{8,0},{16,24},{24,16},{1,9},{9,1},{17,25},{25,17},{2,10},{10... | collective-permute-start | bytes 786440 | tf_op jit(solution)/shard_map/ppermute | solution.py:200
  17.4 29.7 %copy-start.3 = (f32[2,256]{1,0:T(2,128)S(1)}, f32[2,256]{1,0:T(2,128)}, u32[]{:S(2)}) copy-start(f32[2,256]{1,0:T(2,128)} %param.11) | copy-start | bytes 6148
  17.4 29.7 %copy-start.4 = (s32[2,256]{1,0:T(2,128)S(1)}, s32[2,256]{1,0:T(2,128)}, u32[]{:S(2)}) copy-start(s32[2,256]{1,0:T(2,128)} %param.12) | copy-start | bytes 6148
  17.4 29.7 %copy-start.6 = (pred[256]{0:T(512)(128)(4,1)S(1)}, pred[256]{0:T(512)(128)(4,1)}, u32[]{:S(2)}) copy-start(pred[256]{0:T(512)(128)(4,1)} %constant.102.clone.1) | copy-start | bytes 772
  17.4 36.1 %copy-start.5 = (f32[2,256]{1,0:T(2,128)S(1)}, f32[2,256]{1,0:T(2,128)}, u32[]{:S(2)}) copy-start(f32[2,256]{1,0:T(2,128)} %param.10) | copy-start | bytes 6148
  17.4 43.5 %copy-start.7 = (s32[8]{0:T(128)S(1)}, s32[8]{0:T(128)}, u32[]{:S(2)}) copy-start(s32[8]{0:T(128)} %constant.104.clone) | copy-start | bytes 100
  19.3 20.8 %all-to-all-start = ((f32[8,64,256]{2,1,0:T(8,128)}), f32[8,64,256]{2,1,0:T(8,128)S(1)}, u32[]{:S(2)}, u32[]{:S(2)}) async-start(f32[8,64,256]{2,1,0:T(8,128)} %bitcast.9), calls=%async_computation | async-start | bytes 1048576 | tf_op jit(solution)/shard_map/all_to_all | solution.py:230
  40.6 5.7 %collective-permute-start.3 = (f32[64,768]{1,0:T(8,128)S(1)}, f32[64,768]{1,0:T(8,128)S(1)}, u32[]{:S(2)}, u32[]{:S(2)}) collective-permute-start(f32[64,768]{1,0:T(8,128)S(1)} %shard_map.75.refs_0_), channel_id=1, source_target_pairs={{0,2},{2,4},{4,6},{6,7},{7,5},{5,3},{3,1},{1,0},{8,10},{10,12},{12... | collective-permute-start | bytes 589832 | tf_op jit(solution)/shard_map/ppermute | solution.py:240
  41.4 5.7 %collective-permute-start.4 = (f32[64,768]{1,0:T(8,128)S(1)}, f32[64,768]{1,0:T(8,128)S(1)}, u32[]{:S(2)}, u32[]{:S(2)}) collective-permute-start(f32[64,768]{1,0:T(8,128)S(1)} %shard_map.75.refs_0_), channel_id=1, source_target_pairs={{2,0},{4,2},{6,4},{7,6},{5,7},{3,5},{1,3},{0,1},{10,8},{12,10},{14... | collective-permute-start | bytes 589832 | tf_op jit(solution)/shard_map/ppermute | solution.py:244
  46.3 6.0 %collective-permute-start.5 = (f32[64,768]{1,0:T(8,128)S(1)}, f32[64,768]{1,0:T(8,128)S(1)}, u32[]{:S(2)}, u32[]{:S(2)}) collective-permute-start(f32[64,768]{1,0:T(8,128)S(1)} %collective-permute-done.3.refs_1_), channel_id=1, source_target_pairs={{0,2},{2,4},{4,6},{6,7},{7,5},{5,3},{3,1},{1,0},{8,10},{10,12},{12... | collective-permute-start | bytes 589832 | tf_op jit(solution)/shard_map/ppermute | solution.py:240
  47.1 6.4 %collective-permute-start.6 = (f32[64,768]{1,0:T(8,128)S(1)}, f32[64,768]{1,0:T(8,128)S(1)}, u32[]{:S(2)}, u32[]{:S(2)}) collective-permute-start(f32[64,768]{1,0:T(8,128)S(1)} %collective-permute-done.4.refs_2_), channel_id=1, source_target_pairs={{2,0},{4,2},{6,4},{7,6},{5,7},{3,5},{1,3},{0,1},{10,8},{12,10},{14... | collective-permute-start | bytes 589832 | tf_op jit(solution)/shard_map/ppermute | solution.py:244
  52.3 6.8 %collective-permute-start.7 = (f32[64,768]{1,0:T(8,128)S(1)}, f32[64,768]{1,0:T(8,128)S(1)}, u32[]{:S(2)}, u32[]{:S(2)}) collective-permute-start(f32[64,768]{1,0:T(8,128)S(1)} %collective-permute-done.5.refs_3_), channel_id=1, source_target_pairs={{0,2},{2,4},{4,6},{6,7},{7,5},{5,3},{3,1},{1,0},{8,10},{10,12},{12... | collective-permute-start | bytes 589832 | tf_op jit(solution)/shard_map/ppermute | solution.py:240
  53.5 7.4 %collective-permute-start.8 = (f32[64,768]{1,0:T(8,128)S(1)}, f32[64,768]{1,0:T(8,128)S(1)}, u32[]{:S(2)}, u32[]{:S(2)}) collective-permute-start(f32[64,768]{1,0:T(8,128)S(1)} %collective-permute-done.6.refs_4_), channel_id=1, source_target_pairs={{2,0},{4,2},{6,4},{7,6},{5,7},{3,5},{1,3},{0,1},{10,8},{12,10},{14... | collective-permute-start | bytes 589832 | tf_op jit(solution)/shard_map/ppermute | solution.py:244
  59.2 5.7 %collective-permute-start.9 = (f32[64,768]{1,0:T(8,128)S(1)}, f32[64,768]{1,0:T(8,128)S(1)}, u32[]{:S(2)}, u32[]{:S(2)}) collective-permute-start(f32[64,768]{1,0:T(8,128)S(1)} %collective-permute-done.7.refs_5_), channel_id=1, source_target_pairs={{0,2},{2,4},{4,6},{6,7},{7,5},{5,3},{3,1},{1,0},{8,10},{10,12},{12... | collective-permute-start | bytes 589832 | tf_op jit(solution)/shard_map/ppermute | solution.py:240
  60.9 5.5 %copy-start.2 = (f32[2,256,256]{2,1,0:T(8,128)S(1)}, f32[2,256,256]{2,1,0:T(8,128)}, u32[]{:S(2)}) copy-start(f32[2,256,256]{2,1,0:T(8,128)} %param.9) | copy-start | bytes 1572868
  65.5 1.6 %collective-permute-start.11 = (f32[256,256]{1,0:T(8,128)S(1)}, f32[256,256]{1,0:T(8,128)S(1)}, u32[]{:S(2)}, u32[]{:S(2)}) collective-permute-start(f32[256,256]{1,0:T(8,128)S(1)} %slice_select_fusion), channel_id=1, source_target_pairs={{8,24},{9,25},{10,26},{11,27},{12,28},{13,29},{14,30},{15,31}} | collective-permute-start | bytes 786440 | tf_op jit(solution)/shard_map/ppermute | solution.py:268
  66.5 2.0 %collective-permute-start.10 = (f32[64,512]{1,0:T(8,128)S(1)}, f32[64,512]{1,0:T(8,128)S(1)}, u32[]{:S(2)}, u32[]{:S(2)}) collective-permute-start(f32[64,512]{1,0:T(8,128)S(1)} %slice.39), channel_id=1, source_target_pairs={{0,0},{1,8},{2,16},{3,24},{8,1},{9,9},{10,17},{11,25},{16,2},{17,1... | collective-permute-start | bytes 393224 | tf_op jit(solution)/shard_map/ppermute | solution.py:253
  67.2 18.0 %collective-permute-start.12 = (f32[256,256]{1,0:T(8,128)S(1)}, f32[256,256]{1,0:T(8,128)S(1)}, u32[]{:S(2)}, u32[]{:S(2)}) collective-permute-start(f32[256,256]{1,0:T(8,128)S(1)} %fusion.21), channel_id=1, source_target_pairs={{8,0},{24,16},{9,1},{25,17},{10,2},{26,18},{11,3},{27,19},{12,4},{... | collective-permute-start | bytes 786440 | tf_op jit(solution)/shard_map/ppermute | solution.py:271

commit v2 on v1

v2 whole, which is shorter than its diff:
```python
import functools

import jax
import jax.numpy as jnp
from jax import lax
from jax.experimental import pallas as pl
from jax.experimental.pallas import tpu as pltpu
from jax.sharding import PartitionSpec as P

f32 = jnp.float32
bf16 = jnp.bfloat16
VMEM_LIMIT = 20 * 1024 * 1024


def split(value):
    high = value.astype(bf16)
    return high, (value - high.astype(f32)).astype(bf16)


def mm(left, right, dims=(((1,), (0,)), ((), ()))):
    left_high, left_low = split(left)
    right_high, right_low = split(right)
    dot = functools.partial(lax.dot_general, dimension_numbers=dims, preferred_element_type=f32)
    return dot(left_high, right_high) + (dot(left_high, right_low) + dot(left_low, right_high))


def mm_nt(left, right):
    return mm(left, right, (((1,), (1,)), ((), ())))


def pick_rows(chosen, value):
    width = value.shape[1]
    both = jnp.dot(chosen, jnp.concatenate(split(value), axis=1), preferred_element_type=f32)
    return both[:, :width] + both[:, width:]


def pick_cols(value, chosen):
    height = value.shape[0]
    both = jnp.dot(jnp.concatenate(split(value), axis=0), chosen, preferred_element_type=f32)
    return both[:height] + both[height:]


def ones_where(mask):
    return jnp.where(mask, 1.0, 0.0).astype(bf16)


def scale(lower, factors, panel):
    pivot, link, link_before = (factors[3 * panel + i : 3 * panel + i + 1, :] for i in range(3))
    width = lower.shape[1]
    after = pltpu.roll(lower, width - 1, 1)
    before = pltpu.roll(lower, 1, 1)
    return lower * pivot + after * link + before * link_before


def call(body, outs, *args, smem=0, scratch=()):
    vmem = pl.BlockSpec(memory_space=pltpu.VMEM)
    return pl.pallas_call(
        body,
        out_shape=[
            jax.ShapeDtypeStruct(*out) if isinstance(out[1], type) else jax.ShapeDtypeStruct(out, f32)
            for out in outs
        ],
        in_specs=[pl.BlockSpec(memory_space=pltpu.SMEM)] * smem + [vmem] * (len(args) - smem),
        out_specs=[vmem] * len(outs),
        scratch_shapes=list(scratch),
        compiler_params=pltpu.CompilerParams(vmem_limit_bytes=VMEM_LIMIT),
    )(*args)


def row_ids(row, rows_axis, height, tile, axis):
    ids = []
    for t in range(height // tile):
        shape = (tile, 1) if axis == 0 else (1, tile)
        ids.append((t * rows_axis + row) * tile + lax.broadcasted_iota(jnp.int32, shape, axis))
    return jnp.concatenate(ids, axis=axis)


def gather_moved(rows_axis, me, swaps, block, keep, send, target_out, source_out):
    lines = swaps[...]
    height, tile = block.shape
    amount = lines.shape[1]
    upright = jnp.concatenate([lines, lines], axis=0).T
    lead0, partner0, lead1, partner1 = (lines[i : i + 1, :] for i in range(4))
    lead0_up, partner0_up, lead1_up, partner1_up = (upright[:, i : i + 1] for i in range(4))

    def through(values):
        hit = partner0_up == values
        return jnp.where(
            jnp.max(jnp.where(hit, 1, 0), axis=0, keepdims=True) > 0,
            jnp.sum(jnp.where(hit, lead0_up, 0), axis=0, keepdims=True),
            values,
        )

    def through_up(values):
        hit = values == partner0
        return jnp.where(
            jnp.max(jnp.where(hit, 1, 0), axis=1, keepdims=True) > 0,
            jnp.sum(jnp.where(hit, lead0, 0), axis=1, keepdims=True),
            values,
        )

    odd = me[2] == 1
    source1, source1_lead = through(lead1), through(partner1)
    source1_up, source1_lead_up = through_up(lead1_up), through_up(partner1_up)
    wanted = jnp.concatenate([lead0_up, partner0_up, source1_up, source1_lead_up], axis=0)
    ids = row_ids(me[0], rows_axis, height, tile, 1)
    rows = pick_rows(ones_where(wanted == ids), block[...])
    half = keep.shape[0]
    keep[...] = jnp.where(odd, rows[half:], rows[:half])
    send[...] = jnp.where(odd, rows[:half], rows[half:])

    hit = jnp.logical_or(lead1_up == partner0, partner1_up == partner0)
    again = jnp.max(jnp.where(hit, 1, 0), axis=0, keepdims=True) > 0
    target_out[...] = jnp.concatenate([lead0, jnp.where(again, -1, partner0), lead1, partner1], axis=1)

    index = lax.broadcasted_iota(jnp.int32, (1, tile), 1)

    def lead_source(ids, leads_up, sources_up):
        hit = leads_up == ids
        return jnp.where(
            jnp.max(jnp.where(hit, 1, 0), axis=0, keepdims=True) > 0,
            jnp.sum(jnp.where(hit, sources_up, 0), axis=0, keepdims=True),
            ids,
        )

    first = lead_source(index, lead0_up, partner0_up)
    second = through(lead_source(index + tile, lead1_up, partner1_up))
    source_out[...] = jnp.concatenate([first, second, lead0, source1], axis=1)


def place_moved(rows_axis, me, target, block, lead_rows, mine, other, out):
    height, tile = block.shape
    amount = target.shape[1] // 4
    odd = me[2] == 1
    first = jnp.where(odd, other[...], mine[...])
    second = jnp.where(odd, mine[...], other[...])
    aims = target[...]
    lead0, partner0, lead1, partner1 = (aims[:, i * amount : (i + 1) * amount] for i in range(4))
    lead = jnp.where(odd, lead1, lead0)
    ids = row_ids(me[0], rows_axis, height, tile, 0)
    hit = ids == jnp.concatenate([lead, partner0, partner1], axis=1)
    moved = jnp.max(jnp.where(hit, 1, 0), axis=1, keepdims=True) > 0
    rows = pick_rows(ones_where(hit), jnp.concatenate([lead_rows[...], first, second], axis=0))
    out[...] = jnp.where(moved, rows, block[...])


def pick_columns(lead_tiles, source, whole, out):
    piece = out.shape[0]
    tile = whole.shape[1]
    lead = lead_tiles * tile
    wanted = source[...]
    index = lax.broadcasted_iota(jnp.int32, (tile, 1), 0)
    total = None
    for t in range(whole.shape[0] // piece):
        block = jnp.concatenate(split(whole[t * piece : (t + 1) * piece, :]), axis=0)
        part = wanted if t < lead_tiles else wanted[:, :lead]
        term = jnp.dot(block, ones_where(index + t * tile == part), preferred_element_type=f32)
        if total is None:
            total = term
        elif t < lead_tiles:
            total = total + term
        else:
            total = jnp.concatenate([total[:, :lead] + term, total[:, lead:]], axis=1)
    out[...] = total[:piece] + total[piece:]


def first_corner(order, me, *refs):
    *pieces, out = refs
    piece = pieces[0].shape[0]
    tile = out.shape[0]
    holder = me[0] == 1

    @pl.when(jnp.logical_not(holder))
    def _():
        out[...] = jnp.zeros_like(out)

    for i, ref in enumerate(pieces):

        @pl.when(jnp.logical_and(holder, order[i] < tile // piece))
        def _(i=i, ref=ref):
            out[pl.ds(pl.multiple_of(order[i] * piece, piece), piece), :] = ref[:, :tile]


def finish(rows_axis, order, own_order, me, target, block, corner, inverses, factors, *refs):
    *pieces, out, rows, own = refs
    height, tile = block.shape
    piece = pieces[0].shape[0]
    count = height // piece
    for i, ref in enumerate(pieces):
        to, rank = (rows, order[i]) if i < count else (own, own_order[i - count])
        to[pl.ds(pl.multiple_of(rank * piece, piece), piece), :] = ref[...]

    amount = target.shape[1] // 4
    row, col = me[0], me[1]
    ids = row_ids(row, rows_axis, height, tile, 0)
    nt = (((1,), (1,)), ((), ()))

    aims = target[...]
    aims = jnp.concatenate([aims[:, amount : 2 * amount], aims[:, 3 * amount :]], axis=1)
    chosen = ones_where(col * tile + lax.broadcasted_iota(jnp.int32, (tile, 1), 0) == aims)
    ones = jnp.ones((8, 2 * amount), bf16)
    moved = lax.dot_general(ones, chosen, nt, preferred_element_type=f32)[:1] > 0.5
    swapped = jnp.concatenate(split(rows[:, 2 * tile :]), axis=0)
    swapped = lax.dot_general(swapped, chosen, nt, preferred_element_type=f32)
    swapped = swapped[:height] + swapped[height:]
    first, second = rows[:, :tile], rows[:, tile : 2 * tile]
    matrix = jnp.where(moved, swapped, block[...])
    matrix = jnp.where(col == 0, first, jnp.where(col == 1, second, matrix))

    low0 = jnp.where(ids >= tile, mm(first, inverses[0]), 0.0)
    low0_own = jnp.where(col > 0, mm(own[:, :tile], inverses[0]), 0.0)
    scaled0 = scale(low0_own, factors, 0)
    matrix = matrix - mm_nt(low0, scaled0)
    matrix = jnp.where(jnp.logical_and(ids >= tile, col == 0), low0, matrix)

    scaled_corner = scale(mm(corner[...], inverses[0]), factors, 0)
    low1 = mm(second - mm_nt(low0, scaled_corner), inverses[1])
    low1 = jnp.where(ids >= 2 * tile, low1, 0.0)
    low1_own = mm(own[:, tile : 2 * tile] - mm_nt(low0_own, scaled_corner), inverses[1])
    low1_own = jnp.where(col > 1, low1_own, 0.0)
    scaled1 = scale(low1_own, factors, 1)
    matrix = matrix - mm_nt(low1, scaled1)
    out[...] = jnp.where(jnp.logical_and(ids >= 2 * tile, col == 1), low1, matrix)

    @pl.when(jnp.logical_and(row == 0, col > 0))
    def _():
        out[:tile, :] = scaled0.T

    @pl.when(jnp.logical_and(row == 1, col > 1))
    def _():
        out[:tile, :] = scaled1.T


def shards(kkt, swaps, inverses, pivots, couplings, pattern):
    height, tile = kkt.shape
    panels, _, amount = swaps.shape
    rows_axis = lax.axis_size("row")
    cols_axis = lax.axis_size("col")
    row = lax.axis_index("row")
    col = lax.axis_index("col")
    piece = height // cols_axis
    lead = panels * tile

    links = couplings * pattern.astype(f32)
    ends = jnp.zeros((panels, 1), f32)
    links_after = jnp.concatenate([links[:, :-1], ends], axis=1)
    links_before = jnp.concatenate([ends, links[:, :-1]], axis=1)
    factors = jnp.stack([pivots, links_after, links_before], axis=1).reshape(3 * panels, tile)
    me = jnp.stack([row, col, row % 2]).astype(jnp.int32)

    def flip(value, bit):
        return lax.ppermute(value, "row", [(i, i ^ bit) for i in range(rows_axis)])

    half = 2 * amount
    keep, send, target, source = call(
        functools.partial(gather_moved, rows_axis),
        [(half, tile), (half, tile), ((1, 2 * half), jnp.int32), ((1, lead + half), jnp.int32)],
        me,
        swaps.reshape(2 * panels, amount),
        kkt,
        smem=1,
    )
    mine = keep + flip(send, 1)
    if rows_axis == 4:
        near = row < 2
        come = flip(jnp.where(near, mine[:amount], mine[amount:]), 2)
        lead_rows = mine[amount:] + come
        mine = jnp.where(near, mine[:amount], come)
    else:
        bit = 2
        while bit < rows_axis:
            mine = mine + flip(mine, bit)
            bit *= 2
        lead_rows = mine[amount:]
        mine = mine[:amount]
    other = flip(mine, 1)
    (block,) = call(
        functools.partial(place_moved, rows_axis),
        [(height, tile)],
        me,
        target,
        kkt,
        lead_rows,
        mine,
        other,
        smem=1,
    )

    whole = lax.all_to_all(block, "col", 0, 0, tiled=True)
    (part,) = call(functools.partial(pick_columns, panels), [(piece, lead + half)], source, whole)
    ring = list(range(0, cols_axis, 2)) + list(range(cols_axis - 1, 0, -2))
    after = [(ring[i], ring[(i + 1) % cols_axis]) for i in range(cols_axis)]
    before = [(b, a) for a, b in after]
    pieces = tile // piece
    right, left = part, part
    parts, steps = [part], [0]
    last = cols_axis // 2
    for step in range(1, last + 1):
        right = lax.ppermute(right, "col", after)
        parts.append(right)
        steps.append(-step)
        if step < last:
            left = lax.ppermute(left, "col", before)
            parts.append(left)
            steps.append(step)
    place = jnp.where(col % 2 == 0, col // 2, cols_axis - 1 - col // 2)
    order = (place + jnp.array(steps, jnp.int32)) % cols_axis
    order = jnp.where(order < last, 2 * order, 2 * (cols_axis - 1 - order) + 1)

    near_parts = [
        lax.ppermute(
            part[:, :lead],
            ("row", "col"),
            [
                (t % rows_axis * cols_axis + t // rows_axis * pieces + i, (i ^ bits) * cols_axis + t)
                for t in range(cols_axis)
                for i in range(pieces)
            ],
        )
        for bits in range(0, rows_axis, 2)
    ]
    own_parts = near_parts + [flip(near_part, 1) for near_part in near_parts]
    own_bits = [bits + core for core in range(2) for bits in range(0, rows_axis, 2)]
    own_order = row ^ jnp.array(own_bits, jnp.int32)

    (corner,) = call(first_corner, [(tile, tile)], order, me, *parts, smem=2)
    bit = 2
    holders = [1]
    while bit < rows_axis:
        corner = corner + lax.ppermute(corner, "row", [(i, i ^ bit) for i in holders])
        holders += [i ^ bit for i in holders]
        bit *= 2
    corner = corner + lax.ppermute(corner, "row", [(i, i ^ 1) for i in holders])

    (out,) = call(
        functools.partial(finish, rows_axis),
        [(height, tile)],
        order,
        own_order,
        me,
        target,
        block,
        corner,
        inverses,
        factors,
        *parts,
        *own_parts,
        smem=3,
        scratch=[pltpu.VMEM((height, lead + half), f32), pltpu.VMEM((tile, lead), f32)],
    )
    return out


def solution(mesh):
    return jax.shard_map(
        shards,
        mesh=mesh,
        in_specs=(P("row", "col"), P(), P(), P(), P(), P()),
        out_specs=P("row", "col"),
        check_vma=False,
    )
```

time: 89.2 us -> 79.2 us (0.89)
  waiting for transfers between devices: 39.6 us -> 26.5 us
  blocking collectives: 14 us -> 20.6 us
  Pallas kernels: 10.2 us -> 8.3 us
  other arithmetic: 2.08 us -> 0.26 us
    all_to_all x0 -> x1, blocking collectives: none -> 20.6 us  [shards(): whole = lax.all_to_all(block, 'col', 0, 0, tiled=True)]
    all_to_all x1 -> x0, waiting for transfers between devices: 14.4 us -> none  [shards(): whole = lax.all_to_all(block, 'col', 0, 0, tiled=True)]
    all_gather x1 -> x0, blocking collectives: 14 us -> none  [shards(): own = lax.all_gather(own, 'row', tiled=True)]
    all_to_all x1 -> x0, starting transfers between devices: 6.03 us -> none  [shards(): whole = lax.all_to_all(block, 'col', 0, 0, tiled=True)]
    ppermute x3 -> x5, starting transfers between devices: 3.54 us -> 7.87 us  [flip(): return lax.ppermute(value, 'row', [(i, i ^ bit) for i in range(rows_axis)])]
    ppermute x1 -> x2, starting transfers between devices: 0.67 us -> 3.07 us  [shards(): lax.ppermute(part[:, :lead], ('row', 'col'), [(t % rows_axis * cols_axis...]
    ppermute x3 -> x5, waiting for transfers between devices: 9.22 us -> 7.22 us  [flip(): return lax.ppermute(value, 'row', [(i, i ^ bit) for i in range(rows_axis)])]
    pallas_call x6 -> x5, Pallas kernels: 10.2 us -> 8.3 us  [call(): pl.pallas_call(body, out_shape=[jax.ShapeDtypeStruct(*out) if isinstance(...]
  transfers between devices with their start and end apart: 14 -> 16, of which waited for: 8 -> 9; matrix products, arithmetic and copies ran while one was open for 1% -> 1% of each run, Pallas kernels for 3% -> 0%
where the time goes in v2:
time: 79.2 us; the launch traced here: 78.9 us
  waiting for transfers between devices  26.5 us (33%)
  starting transfers between devices  20.7 us (26%)
  blocking collectives  20.6 us (26%)
  Pallas kernels  8.3 us (10%)
  local copies, waits for them, and re-layouts  2.44 us (3%)
    all_to_all x1, blocking collectives, shards(): whole = lax.all_to_all(block, 'col', 0, 0, tiled=True)  20.6 us
    ppermute x4, waiting for transfers between devices, shards(): right = lax.ppermute(right, 'col', after)  17.8 us
    pallas_call x5, Pallas kernels, call(): pl.pallas_call(body, out_shape=[jax.ShapeDtypeStruct(*out) if isinstance(...  8.3 us
    ppermute x5, starting transfers between devices, flip(): return lax.ppermute(value, 'row', [(i, i ^ bit) for i in range(rows_axis)])  7.87 us
    ppermute x5, waiting for transfers between devices, flip(): return lax.ppermute(value, 'row', [(i, i ^ bit) for i in range(rows_axis)])  7.22 us
    ppermute x4, starting transfers between devices, shards(): right = lax.ppermute(right, 'col', after)  5.19 us
    ppermute x2, starting transfers between devices, shards(): lax.ppermute(part[:, :lead], ('row', 'col'), [(t % rows_axis * cols_axis...  3.07 us
    ppermute x3, starting transfers between devices, shards(): left = lax.ppermute(left, 'col', before)  2.43 us
  transfers between devices with their start and end apart: 16, of which 9 were waited for; matrix products, arithmetic and copies ran while one was open for 1% of the time, Pallas kernels for 0%

profile of v2, /device:TPU:0, one launch (start us, length us, event | category | flops | bytes accessed | tf_op | source)
XLA Modules:
  0.0 78.9 jit_solution(10962752498631729534)
XLA Ops:
  0.0 0.1 pad_add_fusion.me
  0.1 0.6 copy-done.3
  0.7 1.0 %copy-done = f32[512,256]{1,0:T(8,128)S(1)} copy-done((f32[512,256]{1,0:T(8,128)S(1)}, f32[512,256]{1,0:T(8,128)}, u32[]{:S(2)}) %copy-start) | copy-done | bytes 524312
  1.7 1.9 %shard_map.82 = (f32[256,256]{1,0:T(8,128)S(1)}, f32[256,256]{1,0:T(8,128)S(1)}, s32[1,512]{1,0:T(1,128)S(1)}, s32[1,768]{1,0:T(1,128)S(1)}) custom-call(s32[3]{0:T(128)S(1)} %pad_add_fusion.me, s32[4,128]{1,0:T(4,128)S(1)} %bitcast.14, f32[512,256]{1,0:T(8,128)S(1)} %copy-done), custom_call_target="tpu_custom_call" | custom-call | tf_op jit(solution)/shard_map/pallas_call | solution.py:57
  3.6 0.5 collective-permute-start
  4.1 1.2 %collective-permute-done = f32[256,256]{1,0:T(8,128)S(1)} collective-permute-done((f32[256,256]{1,0:T(8,128)S(1)}, f32[256,256]{1,0:T(8,128)S(1)}, u32[]{:S(2)}, u32[]{:S(2)}) %collective-permute-start) | collective-permute-done | bytes 262176 | tf_op jit(solution)/shard_map/ppermute | solution.py:252
  5.3 0.0 copy-start.1
  5.4 3.0 %collective-permute-start.1 = (f32[128,256]{1,0:T(8,128)S(1)}, f32[128,256]{1,0:T(8,128)S(1)}, u32[]{:S(2)}, u32[]{:S(2)}) collective-permute-start(f32[128,256]{1,0:T(8,128)S(1)} %slice_select_fusion.1), channel_id=1, source_target_pairs={{0,16},{8,24},{16,0},{24,8},{1,17},{9,25},{17,1},{25,9},{2,18},{10... | collective-permute-start | bytes 393224 | tf_op jit(solution)/shard_map/ppermute | solution.py:252
  8.3 3.8 %collective-permute-done.1 = f32[128,256]{1,0:T(8,128)S(1)} collective-permute-done((f32[128,256]{1,0:T(8,128)S(1)}, f32[128,256]{1,0:T(8,128)S(1)}, u32[]{:S(2)}, u32[]{:S(2)}) %collective-permute-start.1) | collective-permute-done | bytes 131104 | tf_op jit(solution)/shard_map/ppermute | solution.py:252
  12.1 0.1 collective-permute-start.2
  12.2 1.3 %collective-permute-done.2.other = f32[128,256]{1,0:T(8,128)S(1)} collective-permute-done((f32[128,256]{1,0:T(8,128)S(1)}, f32[128,256]{1,0:T(8,128)S(1)}, u32[]{:S(2)}, u32[]{:S(2)}) %collective-permute-start.2) | collective-permute-done | bytes 131104 | tf_op jit(solution)/shard_map/ppermute | solution.py:252
  13.6 1.1 %shard_map.83.block = f32[512,256]{1,0:T(8,128)S(1)} custom-call(s32[3]{0:T(128)S(1)} %pad_add_fusion.me, s32[1,512]{1,0:T(1,128)S(1)} %get-tuple-element.9.target, f32[512,256]{1,0:T(8,128)S(1)} %copy-done.1, f32[128,256]{1,0:T(8,128)S(1)} %get-tuple-element.16.lead_rows, f32[128,256]{1,0:T(8,128)S(1)} %get-tuple-element.15.mine, ...), custom_call_target="tpu_custom_call" | custom-call | tf_op jit(solution)/shard_map/pallas_call | solution.py:57
  14.6 20.6 %all_to_all.11 = f32[8,64,256]{2,1,0:T(8,128)S(1)} all-to-all(f32[8,64,256]{2,1,0:T(8,128)S(1)} %bitcast.12), channel_id=1, replica_groups=mesh['row'=4,'col'=8] {'col'}, dimensions={0} | all-to-all | bytes 1048576 | tf_op jit(solution)/shard_map/all_to_all | solution.py:289
  35.3 0.5 shard_map.84.refs_0_
  35.8 1.2 %collective-permute-start.3 = (f32[64,768]{1,0:T(8,128)S(1)}, f32[64,768]{1,0:T(8,128)S(1)}, u32[]{:S(2)}, u32[]{:S(2)}) collective-permute-start(f32[64,768]{1,0:T(8,128)S(1)} %shard_map.84.refs_0_), channel_id=1, source_target_pairs={{0,2},{2,4},{4,6},{6,7},{7,5},{5,3},{3,1},{1,0},{8,10},{10,12},{12... | collective-permute-start | bytes 589832 | tf_op jit(solution)/shard_map/ppermute | solution.py:299
  36.9 0.9 %collective-permute-start.4 = (f32[64,768]{1,0:T(8,128)S(1)}, f32[64,768]{1,0:T(8,128)S(1)}, u32[]{:S(2)}, u32[]{:S(2)}) collective-permute-start(f32[64,768]{1,0:T(8,128)S(1)} %shard_map.84.refs_0_), channel_id=1, source_target_pairs={{2,0},{4,2},{6,4},{7,6},{5,7},{3,5},{1,3},{0,1},{10,8},{12,10},{14... | collective-permute-start | bytes 589832 | tf_op jit(solution)/shard_map/ppermute | solution.py:303
  37.8 3.6 %collective-permute-done.3.refs_1_ = f32[64,768]{1,0:T(8,128)S(1)} collective-permute-done((f32[64,768]{1,0:T(8,128)S(1)}, f32[64,768]{1,0:T(8,128)S(1)}, u32[]{:S(2)}, u32[]{:S(2)}) %collective-permute-start.3) | collective-permute-done | bytes 196640 | tf_op jit(solution)/shard_map/ppermute | solution.py:299
  41.5 1.1 %collective-permute-start.5 = (f32[64,768]{1,0:T(8,128)S(1)}, f32[64,768]{1,0:T(8,128)S(1)}, u32[]{:S(2)}, u32[]{:S(2)}) collective-permute-start(f32[64,768]{1,0:T(8,128)S(1)} %collective-permute-done.3.refs_1_), channel_id=1, source_target_pairs={{0,2},{2,4},{4,6},{6,7},{7,5},{5,3},{3,1},{1,0},{8,10},{10,12},{12... | collective-permute-start | bytes 589832 | tf_op jit(solution)/shard_map/ppermute | solution.py:299
  42.6 0.0 collective-permute-done.4.refs_2_
  42.6 0.9 %collective-permute-start.6 = (f32[64,768]{1,0:T(8,128)S(1)}, f32[64,768]{1,0:T(8,128)S(1)}, u32[]{:S(2)}, u32[]{:S(2)}) collective-permute-start(f32[64,768]{1,0:T(8,128)S(1)} %collective-permute-done.4.refs_2_), channel_id=1, source_target_pairs={{2,0},{4,2},{6,4},{7,6},{5,7},{3,5},{1,3},{0,1},{10,8},{12,10},{14... | collective-permute-start | bytes 589832 | tf_op jit(solution)/shard_map/ppermute | solution.py:303
  43.5 4.6 %collective-permute-done.5.refs_3_ = f32[64,768]{1,0:T(8,128)S(1)} collective-permute-done((f32[64,768]{1,0:T(8,128)S(1)}, f32[64,768]{1,0:T(8,128)S(1)}, u32[]{:S(2)}, u32[]{:S(2)}) %collective-permute-start.5) | collective-permute-done | bytes 196640 | tf_op jit(solution)/shard_map/ppermute | solution.py:299
  48.1 1.4 %collective-permute-start.7 = (f32[64,768]{1,0:T(8,128)S(1)}, f32[64,768]{1,0:T(8,128)S(1)}, u32[]{:S(2)}, u32[]{:S(2)}) collective-permute-start(f32[64,768]{1,0:T(8,128)S(1)} %collective-permute-done.5.refs_3_), channel_id=1, source_target_pairs={{0,2},{2,4},{4,6},{6,7},{7,5},{5,3},{3,1},{1,0},{8,10},{10,12},{12... | collective-permute-start | bytes 589832 | tf_op jit(solution)/shard_map/ppermute | solution.py:299
  49.5 0.0 collective-permute-done.6.refs_4_
  49.5 0.6 collective-permute-start.8
  50.1 5.4 %collective-permute-done.7.refs_5_ = f32[64,768]{1,0:T(8,128)S(1)} collective-permute-done((f32[64,768]{1,0:T(8,128)S(1)}, f32[64,768]{1,0:T(8,128)S(1)}, u32[]{:S(2)}, u32[]{:S(2)}) %collective-permute-start.7) | collective-permute-done | bytes 196640 | tf_op jit(solution)/shard_map/ppermute | solution.py:299
  55.5 1.5 %collective-permute-start.9 = (f32[64,768]{1,0:T(8,128)S(1)}, f32[64,768]{1,0:T(8,128)S(1)}, u32[]{:S(2)}, u32[]{:S(2)}) collective-permute-start(f32[64,768]{1,0:T(8,128)S(1)} %collective-permute-done.7.refs_5_), channel_id=1, source_target_pairs={{0,2},{2,4},{4,6},{6,7},{7,5},{5,3},{3,1},{1,0},{8,10},{10,12},{12... | collective-permute-start | bytes 589832 | tf_op jit(solution)/shard_map/ppermute | solution.py:299
  57.0 0.0 copy-start.4
  57.0 0.0 copy-start.5
  57.1 0.0 copy-start.7
  57.1 0.0 collective-permute-done.8.refs_6_
  57.1 4.1 %collective-permute-done.9.refs_7_ = f32[64,768]{1,0:T(8,128)S(1)} collective-permute-done((f32[64,768]{1,0:T(8,128)S(1)}, f32[64,768]{1,0:T(8,128)S(1)}, u32[]{:S(2)}, u32[]{:S(2)}) %collective-permute-start.9) | collective-permute-done | bytes 196640 | tf_op jit(solution)/shard_map/ppermute | solution.py:299
  61.2 0.6 shard_map.85
  61.8 0.7 collective-permute-start.10
  62.6 0.7 slice.24
  63.2 1.5 %collective-permute-start.13 = (f32[64,512]{1,0:T(8,128)}, f32[64,512]{1,0:T(8,128)S(1)}, u32[]{:S(2)}, u32[]{:S(2)}) collective-permute-start(f32[64,512]{1,0:T(8,128)} %slice.24), channel_id=1, source_target_pairs={{0,16},{1,24},{2,0},{3,8},{8,17},{9,25},{10,1},{11,9},{16,18},{17,... | collective-permute-start | bytes 393224 | tf_op jit(solution)/shard_map/ppermute | solution.py:311
  64.8 1.6 %collective-permute-start.12 = (f32[64,512]{1,0:T(8,128)}, f32[64,512]{1,0:T(8,128)S(1)}, u32[]{:S(2)}, u32[]{:S(2)}) collective-permute-start(f32[64,512]{1,0:T(8,128)} %slice.24), channel_id=1, source_target_pairs={{0,0},{1,8},{2,16},{3,24},{8,1},{9,9},{10,17},{11,25},{16,2},{17,1... | collective-permute-start | bytes 393224 | tf_op jit(solution)/shard_map/ppermute | solution.py:311
  66.3 0.1 pad_bitcast_fusion
  66.4 0.0 collective-permute-done.10
  66.4 0.0 copy-start.2
  66.4 1.4 %collective-permute-start.11 = (f32[256,256]{1,0:T(8,128)S(1)}, f32[256,256]{1,0:T(8,128)S(1)}, u32[]{:S(2)}, u32[]{:S(2)}) collective-permute-start(f32[256,256]{1,0:T(8,128)S(1)} %add.45), channel_id=1, source_target_pairs={{8,0},{24,16},{9,1},{25,17},{10,2},{26,18},{11,3},{27,19},{12,4},{... | collective-permute-start | bytes 786440 | tf_op jit(solution)/shard_map/ppermute | solution.py:333
  67.9 1.5 %collective-permute-done.13.refs_9_ = f32[64,512]{1,0:T(8,128)S(1)} collective-permute-done((f32[64,512]{1,0:T(8,128)}, f32[64,512]{1,0:T(8,128)S(1)}, u32[]{:S(2)}, u32[]{:S(2)}) %collective-permute-start.13) | collective-permute-done | bytes 131104 | tf_op jit(solution)/shard_map/ppermute | solution.py:311
  69.4 0.2 collective-permute-start.15
  69.6 0.0 collective-permute-done.12.refs_8_
  69.6 4.1 %collective-permute-start.14 = (f32[64,512]{1,0:T(8,128)S(1)}, f32[64,512]{1,0:T(8,128)S(1)}, u32[]{:S(2)}, u32[]{:S(2)}) collective-permute-start(f32[64,512]{1,0:T(8,128)S(1)} %collective-permute-done.12.refs_8_), channel_id=1, source_target_pairs={{0,8},{8,0},{16,24},{24,16},{1,9},{9,1},{17,25},{25,17},{2,10},{10... | collective-permute-start | bytes 393224 | tf_op jit(solution)/shard_map/ppermute | solution.py:252
  73.7 0.0 collective-permute-done.11
  73.8 0.0 collective-permute-done.15.refs_11_
  73.8 0.9 %collective-permute-done.14.refs_10_ = f32[64,512]{1,0:T(8,128)S(1)} collective-permute-done((f32[64,512]{1,0:T(8,128)S(1)}, f32[64,512]{1,0:T(8,128)S(1)}, u32[]{:S(2)}, u32[]{:S(2)}) %collective-permute-start.14) | collective-permute-done | bytes 131104 | tf_op jit(solution)/shard_map/ppermute | solution.py:252
  74.7 4.2 %shard_map.86 = f32[512,256]{1,0:T(8,128)} custom-call(s32[8]{0:T(128)S(1)} %compare_select_fusion.2.order, s32[4]{0:T(128)S(1)} %broadcast_xor_fusion.own_order, s32[3]{0:T(128)S(1)} %pad_add_fusion.me, s32[1,512]{1,0:T(1,128)S(1)} %get-tuple-element.9.target, f32[512,256]{1,0:T(8,128)S(1)} %shard_map.83.block, f32[256,256]{1,0:T(8,128)S(1)} %add.46.corner, ...), custom_call_target="tpu_custom_call" | custom-call | tf_op jit(solution)/shard_map/pallas_call | solution.py:57
  (24 shorter events, 0.2 us)
Async XLA Ops:
  0.0 0.7 copy-start.3
  0.7 1.0 %copy-start = (f32[512,256]{1,0:T(8,128)S(1)}, f32[512,256]{1,0:T(8,128)}, u32[]{:S(2)}) copy-start(f32[512,256]{1,0:T(8,128)} %block.3) | copy-start | bytes 1572868
  3.6 1.7 %collective-permute-start = (f32[256,256]{1,0:T(8,128)S(1)}, f32[256,256]{1,0:T(8,128)S(1)}, u32[]{:S(2)}, u32[]{:S(2)}) collective-permute-start(f32[256,256]{1,0:T(8,128)S(1)} %get-tuple-element.11), channel_id=1, source_target_pairs={{0,8},{8,0},{16,24},{24,16},{1,9},{9,1},{17,25},{25,17},{2,10},{10... | collective-permute-start | bytes 786440 | tf_op jit(solution)/shard_map/ppermute | solution.py:252
  5.3 8.2 %copy-start.1 = (f32[512,256]{1,0:T(8,128)S(1)}, f32[512,256]{1,0:T(8,128)}, u32[]{:S(2)}) copy-start(f32[512,256]{1,0:T(8,128)} %block.3) | copy-start | bytes 1572868
  5.4 6.8 %collective-permute-start.1 = (f32[128,256]{1,0:T(8,128)S(1)}, f32[128,256]{1,0:T(8,128)S(1)}, u32[]{:S(2)}, u32[]{:S(2)}) collective-permute-start(f32[128,256]{1,0:T(8,128)S(1)} %slice_select_fusion.1), channel_id=1, source_target_pairs={{0,16},{8,24},{16,0},{24,8},{1,17},{9,25},{17,1},{25,9},{2,18},{10... | collective-permute-start | bytes 393224 | tf_op jit(solution)/shard_map/ppermute | solution.py:252
  12.1 1.4 %collective-permute-start.2 = (f32[128,256]{1,0:T(8,128)S(1)}, f32[128,256]{1,0:T(8,128)S(1)}, u32[]{:S(2)}, u32[]{:S(2)}) collective-permute-start(f32[128,256]{1,0:T(8,128)S(1)} %get-tuple-element.15.mine), channel_id=1, source_target_pairs={{0,8},{8,0},{16,24},{24,16},{1,9},{9,1},{17,25},{25,17},{2,10},{10... | collective-permute-start | bytes 393224 | tf_op jit(solution)/shard_map/ppermute | solution.py:252
  35.8 5.7 %collective-permute-start.3 = (f32[64,768]{1,0:T(8,128)S(1)}, f32[64,768]{1,0:T(8,128)S(1)}, u32[]{:S(2)}, u32[]{:S(2)}) collective-permute-start(f32[64,768]{1,0:T(8,128)S(1)} %shard_map.84.refs_0_), channel_id=1, source_target_pairs={{0,2},{2,4},{4,6},{6,7},{7,5},{5,3},{3,1},{1,0},{8,10},{10,12},{12... | collective-permute-start | bytes 589832 | tf_op jit(solution)/shard_map/ppermute | solution.py:299
  36.9 5.7 %collective-permute-start.4 = (f32[64,768]{1,0:T(8,128)S(1)}, f32[64,768]{1,0:T(8,128)S(1)}, u32[]{:S(2)}, u32[]{:S(2)}) collective-permute-start(f32[64,768]{1,0:T(8,128)S(1)} %shard_map.84.refs_0_), channel_id=1, source_target_pairs={{2,0},{4,2},{6,4},{7,6},{5,7},{3,5},{1,3},{0,1},{10,8},{12,10},{14... | collective-permute-start | bytes 589832 | tf_op jit(solution)/shard_map/ppermute | solution.py:303
  41.5 6.6 %collective-permute-start.5 = (f32[64,768]{1,0:T(8,128)S(1)}, f32[64,768]{1,0:T(8,128)S(1)}, u32[]{:S(2)}, u32[]{:S(2)}) collective-permute-start(f32[64,768]{1,0:T(8,128)S(1)} %collective-permute-done.3.refs_1_), channel_id=1, source_target_pairs={{0,2},{2,4},{4,6},{6,7},{7,5},{5,3},{3,1},{1,0},{8,10},{10,12},{12... | collective-permute-start | bytes 589832 | tf_op jit(solution)/shard_map/ppermute | solution.py:299
  42.6 6.9 %collective-permute-start.6 = (f32[64,768]{1,0:T(8,128)S(1)}, f32[64,768]{1,0:T(8,128)S(1)}, u32[]{:S(2)}, u32[]{:S(2)}) collective-permute-start(f32[64,768]{1,0:T(8,128)S(1)} %collective-permute-done.4.refs_2_), channel_id=1, source_target_pairs={{2,0},{4,2},{6,4},{7,6},{5,7},{3,5},{1,3},{0,1},{10,8},{12,10},{14... | collective-permute-start | bytes 589832 | tf_op jit(solution)/shard_map/ppermute | solution.py:303
  48.1 7.5 %collective-permute-start.7 = (f32[64,768]{1,0:T(8,128)S(1)}, f32[64,768]{1,0:T(8,128)S(1)}, u32[]{:S(2)}, u32[]{:S(2)}) collective-permute-start(f32[64,768]{1,0:T(8,128)S(1)} %collective-permute-done.5.refs_3_), channel_id=1, source_target_pairs={{0,2},{2,4},{4,6},{6,7},{7,5},{5,3},{3,1},{1,0},{8,10},{10,12},{12... | collective-permute-start | bytes 589832 | tf_op jit(solution)/shard_map/ppermute | solution.py:299
  49.5 7.5 %copy-start.9 = (s32[8]{0:T(128)S(1)}, s32[8]{0:T(128)}, u32[]{:S(2)}) copy-start(s32[8]{0:T(128)} %constant.67.clone) | copy-start | bytes 100
  49.5 7.6 %collective-permute-start.8 = (f32[64,768]{1,0:T(8,128)S(1)}, f32[64,768]{1,0:T(8,128)S(1)}, u32[]{:S(2)}, u32[]{:S(2)}) collective-permute-start(f32[64,768]{1,0:T(8,128)S(1)} %collective-permute-done.6.refs_4_), channel_id=1, source_target_pairs={{2,0},{4,2},{6,4},{7,6},{5,7},{3,5},{1,3},{0,1},{10,8},{12,10},{14... | collective-permute-start | bytes 589832 | tf_op jit(solution)/shard_map/ppermute | solution.py:303
  55.5 5.7 %collective-permute-start.9 = (f32[64,768]{1,0:T(8,128)S(1)}, f32[64,768]{1,0:T(8,128)S(1)}, u32[]{:S(2)}, u32[]{:S(2)}) collective-permute-start(f32[64,768]{1,0:T(8,128)S(1)} %collective-permute-done.7.refs_5_), channel_id=1, source_target_pairs={{0,2},{2,4},{4,6},{6,7},{7,5},{5,3},{3,1},{1,0},{8,10},{10,12},{12... | collective-permute-start | bytes 589832 | tf_op jit(solution)/shard_map/ppermute | solution.py:299
  57.0 5.5 %copy-start.4 = (f32[2,256]{1,0:T(2,128)S(1)}, f32[2,256]{1,0:T(2,128)}, u32[]{:S(2)}) copy-start(f32[2,256]{1,0:T(2,128)} %param.12) | copy-start | bytes 6148
  57.0 5.5 %copy-start.5 = (s32[2,256]{1,0:T(2,128)S(1)}, s32[2,256]{1,0:T(2,128)}, u32[]{:S(2)}) copy-start(s32[2,256]{1,0:T(2,128)} %param.13) | copy-start | bytes 6148
  57.1 5.5 %copy-start.7 = (pred[256]{0:T(512)(128)(4,1)S(1)}, pred[256]{0:T(512)(128)(4,1)}, u32[]{:S(2)}) copy-start(pred[256]{0:T(512)(128)(4,1)} %constant.65.clone.1) | copy-start | bytes 772
  61.8 4.5 %collective-permute-start.10 = (f32[256,256]{1,0:T(8,128)S(1)}, f32[256,256]{1,0:T(8,128)S(1)}, u32[]{:S(2)}, u32[]{:S(2)}) collective-permute-start(f32[256,256]{1,0:T(8,128)S(1)} %shard_map.85), channel_id=1, source_target_pairs={{8,24},{9,25},{10,26},{11,27},{12,28},{13,29},{14,30},{15,31}} | collective-permute-start | bytes 786440 | tf_op jit(solution)/shard_map/ppermute | solution.py:330
  63.2 6.1 %collective-permute-start.13 = (f32[64,512]{1,0:T(8,128)}, f32[64,512]{1,0:T(8,128)S(1)}, u32[]{:S(2)}, u32[]{:S(2)}) collective-permute-start(f32[64,512]{1,0:T(8,128)} %slice.24), channel_id=1, source_target_pairs={{0,16},{1,24},{2,0},{3,8},{8,17},{9,25},{10,1},{11,9},{16,18},{17,... | collective-permute-start | bytes 393224 | tf_op jit(solution)/shard_map/ppermute | solution.py:311
  64.8 4.8 %collective-permute-start.12 = (f32[64,512]{1,0:T(8,128)}, f32[64,512]{1,0:T(8,128)S(1)}, u32[]{:S(2)}, u32[]{:S(2)}) collective-permute-start(f32[64,512]{1,0:T(8,128)} %slice.24), channel_id=1, source_target_pairs={{0,0},{1,8},{2,16},{3,24},{8,1},{9,9},{10,17},{11,25},{16,2},{17,1... | collective-permute-start | bytes 393224 | tf_op jit(solution)/shard_map/ppermute | solution.py:311
  66.4 1.5 %copy-start.6 = (f32[2,256]{1,0:T(2,128)S(1)}, f32[2,256]{1,0:T(2,128)}, u32[]{:S(2)}) copy-start(f32[2,256]{1,0:T(2,128)} %param.11) | copy-start | bytes 6148
  66.4 7.3 %copy-start.8 = (s32[4]{0:T(128)S(1)}, s32[4]{0:T(128)}, u32[]{:S(2)}) copy-start(s32[4]{0:T(128)} %constant.68.clone) | copy-start | bytes 52
  66.4 8.3 %copy-start.2 = (f32[2,256,256]{2,1,0:T(8,128)S(1)}, f32[2,256,256]{2,1,0:T(8,128)}, u32[]{:S(2)}) copy-start(f32[2,256,256]{2,1,0:T(8,128)} %inverses.1) | copy-start | bytes 1572868
  66.4 7.3 %collective-permute-start.11 = (f32[256,256]{1,0:T(8,128)S(1)}, f32[256,256]{1,0:T(8,128)S(1)}, u32[]{:S(2)}, u32[]{:S(2)}) collective-permute-start(f32[256,256]{1,0:T(8,128)S(1)} %add.45), channel_id=1, source_target_pairs={{8,0},{24,16},{9,1},{25,17},{10,2},{26,18},{11,3},{27,19},{12,4},{... | collective-permute-start | bytes 786440 | tf_op jit(solution)/shard_map/ppermute | solution.py:333
  69.4 4.4 %collective-permute-start.15 = (f32[64,512]{1,0:T(8,128)S(1)}, f32[64,512]{1,0:T(8,128)S(1)}, u32[]{:S(2)}, u32[]{:S(2)}) collective-permute-start(f32[64,512]{1,0:T(8,128)S(1)} %collective-permute-done.13.refs_9_), channel_id=1, source_target_pairs={{0,8},{8,0},{16,24},{24,16},{1,9},{9,1},{17,25},{25,17},{2,10},{10... | collective-permute-start | bytes 393224 | tf_op jit(solution)/shard_map/ppermute | solution.py:252
  69.6 5.1 %collective-permute-start.14 = (f32[64,512]{1,0:T(8,128)S(1)}, f32[64,512]{1,0:T(8,128)S(1)}, u32[]{:S(2)}, u32[]{:S(2)}) collective-permute-start(f32[64,512]{1,0:T(8,128)S(1)} %collective-permute-done.12.refs_8_), channel_id=1, source_target_pairs={{0,8},{8,0},{16,24},{24,16},{1,9},{9,1},{17,25},{25,17},{2,10},{10... | collective-permute-start | bytes 393224 | tf_op jit(solution)/shard_map/ppermute | solution.py:252

commit v3 on v2

--- a/solution.py
+++ b/solution.py
@@ -9,7 +9,7 @@
 
 f32 = jnp.float32
 bf16 = jnp.bfloat16
-VMEM_LIMIT = 20 * 1024 * 1024
+VMEM_LIMIT = 16 * 1024 * 1024
 
 
 def split(value):
@@ -44,15 +44,17 @@
     return jnp.where(mask, 1.0, 0.0).astype(bf16)
 
 
-def scale(lower, factors, panel):
-    pivot, link, link_before = (factors[3 * panel + i : 3 * panel + i + 1, :] for i in range(3))
+def scale(lower, pivots, couplings, pattern, panel):
     width = lower.shape[1]
+    index = lax.broadcasted_iota(jnp.int32, (1, width), 1)
+    link = couplings[panel : panel + 1, :] * pattern[panel : panel + 1, :].astype(f32)
+    link = jnp.where(index < width - 1, link, 0.0)
     after = pltpu.roll(lower, width - 1, 1)
     before = pltpu.roll(lower, 1, 1)
-    return lower * pivot + after * link + before * link_before
-
-
-def call(body, outs, *args, smem=0, scratch=()):
+    return lower * pivots[panel : panel + 1, :] + after * link + before * pltpu.roll(link, 1, 1)
+
+
+def call(body, outs, *args, smem=0, far=0, scratch=()):
     vmem = pl.BlockSpec(memory_space=pltpu.VMEM)
     return pl.pallas_call(
         body,
@@ -60,7 +62,9 @@
             jax.ShapeDtypeStruct(*out) if isinstance(out[1], type) else jax.ShapeDtypeStruct(out, f32)
             for out in outs
         ],
-        in_specs=[pl.BlockSpec(memory_space=pltpu.SMEM)] * smem + [vmem] * (len(args) - smem),
+        in_specs=[pl.BlockSpec(memory_space=pltpu.SMEM)] * smem
+        + [vmem] * (len(args) - smem - far)
+        + [pl.BlockSpec(memory_space=pltpu.HBM)] * far,
         out_specs=[vmem] * len(outs),
         scratch_shapes=list(scratch),
         compiler_params=pltpu.CompilerParams(vmem_limit_bytes=VMEM_LIMIT),
@@ -75,57 +79,48 @@
     return jnp.concatenate(ids, axis=axis)
 
 
-def gather_moved(rows_axis, me, swaps, block, keep, send, target_out, source_out):
+def swap_lists(swaps):
     lines = swaps[...]
+    upright = jnp.concatenate([lines, lines], axis=0).T
+    return [lines[i : i + 1, :] for i in range(4)], [upright[:, i : i + 1] for i in range(4)]
+
+
+def either(hit, values, other, axis):
+    found = jnp.max(jnp.where(hit, 1, 0), axis=axis, keepdims=True) > 0
+    return jnp.where(found, jnp.sum(jnp.where(hit, values, 0), axis=axis, keepdims=True), other)
+
+
+def gather_moved(rows_axis, me, swaps_far, block_far, keep, send, swaps, block, done):
+    fetch_swaps = pltpu.make_async_copy(swaps_far, swaps, done.at[0])
+    fetch = pltpu.make_async_copy(block_far, block, done.at[1])
+    fetch_swaps.start()
+    fetch.start()
+    fetch_swaps.wait()
     height, tile = block.shape
-    amount = lines.shape[1]
-    upright = jnp.concatenate([lines, lines], axis=0).T
-    lead0, partner0, lead1, partner1 = (lines[i : i + 1, :] for i in range(4))
-    lead0_up, partner0_up, lead1_up, partner1_up = (upright[:, i : i + 1] for i in range(4))
-
-    def through(values):
-        hit = partner0_up == values
-        return jnp.where(
-            jnp.max(jnp.where(hit, 1, 0), axis=0, keepdims=True) > 0,
-            jnp.sum(jnp.where(hit, lead0_up, 0), axis=0, keepdims=True),
-            values,
-        )
-
-    def through_up(values):
-        hit = values == partner0
-        return jnp.where(
-            jnp.max(jnp.where(hit, 1, 0), axis=1, keepdims=True) > 0,
-            jnp.sum(jnp.where(hit, lead0, 0), axis=1, keepdims=True),
-            values,
-        )
-
+    (lead0, partner0, _, _), ups = swap_lists(swaps)
+    wanted = [ups[0], ups[1]] + [either(ups[i] == partner0, lead0, ups[i], 1) for i in (2, 3)]
+    ids = row_ids(me[0], rows_axis, height, tile, 1)
+    chosen = ones_where(jnp.concatenate(wanted, axis=0) == ids)
+    fetch.wait()
+    rows = pick_rows(chosen, block[...])
+    half = keep.shape[0]
     odd = me[2] == 1
-    source1, source1_lead = through(lead1), through(partner1)
-    source1_up, source1_lead_up = through_up(lead1_up), through_up(partner1_up)
-    wanted = jnp.concatenate([lead0_up, partner0_up, source1_up, source1_lead_up], axis=0)
-    ids = row_ids(me[0], rows_axis, height, tile, 1)
-    rows = pick_rows(ones_where(wanted == ids), block[...])
-    half = keep.shape[0]
     keep[...] = jnp.where(odd, rows[half:], rows[:half])
     send[...] = jnp.where(odd, rows[:half], rows[half:])
 
+
+def index_vectors(swaps, target, source):
+    (lead0, partner0, lead1, partner1), (lead0_up, partner0_up, lead1_up, partner1_up) = swap_lists(swaps)
     hit = jnp.logical_or(lead1_up == partner0, partner1_up == partner0)
     again = jnp.max(jnp.where(hit, 1, 0), axis=0, keepdims=True) > 0
-    target_out[...] = jnp.concatenate([lead0, jnp.where(again, -1, partner0), lead1, partner1], axis=1)
-
+    target[...] = jnp.concatenate([lead0, jnp.where(again, -1, partner0), lead1, partner1], axis=1)
+    tile = (source.shape[1] - 2 * lead0.shape[1]) // 2
     index = lax.broadcasted_iota(jnp.int32, (1, tile), 1)
-
-    def lead_source(ids, leads_up, sources_up):
-        hit = leads_up == ids
-        return jnp.where(
-            jnp.max(jnp.where(hit, 1, 0), axis=0, keepdims=True) > 0,
-            jnp.sum(jnp.where(hit, sources_up, 0), axis=0, keepdims=True),
-            ids,
-        )
-
-    first = lead_source(index, lead0_up, partner0_up)
-    second = through(lead_source(index + tile, lead1_up, partner1_up))
-    source_out[...] = jnp.concatenate([first, second, lead0, source1], axis=1)
+    first = either(lead0_up == index, partner0_up, index, 0)
+    second = either(lead1_up == index + tile, partner1_up, index + tile, 0)
+    second = either(partner0_up == second, lead0_up, second, 0)
+    source1 = either(partner0_up == lead1, lead0_up, lead1, 0)
+    source[...] = jnp.concatenate([first, second, lead0, source1], axis=1)
 
 
 def place_moved(rows_axis, me, target, block, lead_rows, mine, other, out):
@@ -144,7 +139,7 @@
     out[...] = jnp.where(moved, rows, block[...])
 
 
-def pick_columns(lead_tiles, source, whole, out):
+def pick_columns(lead_tiles, source, whole, out, panel_out):
     piece = out.shape[0]
     tile = whole.shape[1]
     lead = lead_tiles * tile
@@ -161,7 +156,9 @@
             total = total + term
         else:
             total = jnp.concatenate([total[:, :lead] + term, total[:, lead:]], axis=1)
-    out[...] = total[:piece] + total[piece:]
+    total = total[:piece] + total[piece:]
+    out[...] = total
+    panel_out[...] = total[:, :lead]
 
 
 def first_corner(order, me, *refs):
@@ -181,8 +178,17 @@
             out[pl.ds(pl.multiple_of(order[i] * piece, piece), piece), :] = ref[:, :tile]
 
 
-def finish(rows_axis, order, own_order, me, target, block, corner, inverses, factors, *refs):
-    *pieces, out, rows, own = refs
+def finish(
+    rows_axis, order, own_order, me, target, block, inverses, pivots, couplings, pattern, *refs
+):
+    *pieces, out, rows, own, corner = refs
+    pieces, corners = pieces[:-rows_axis], pieces[-rows_axis:]
+    for i, ref in enumerate(corners):
+
+        @pl.when(me[0] == i)
+        def _(ref=ref):
+            corner[...] = ref[...]
+
     height, tile = block.shape
     piece = pieces[0].shape[0]
     count = height // piece
@@ -209,16 +215,16 @@
 
     low0 = jnp.where(ids >= tile, mm(first, inverses[0]), 0.0)
     low0_own = jnp.where(col > 0, mm(own[:, :tile], inverses[0]), 0.0)
-    scaled0 = scale(low0_own, factors, 0)
+    scaled0 = scale(low0_own, pivots, couplings, pattern, 0)
     matrix = matrix - mm_nt(low0, scaled0)
     matrix = jnp.where(jnp.logical_and(ids >= tile, col == 0), low0, matrix)
 
-    scaled_corner = scale(mm(corner[...], inverses[0]), factors, 0)
+    scaled_corner = scale(mm(corner[...], inverses[0]), pivots, couplings, pattern, 0)
     low1 = mm(second - mm_nt(low0, scaled_corner), inverses[1])
     low1 = jnp.where(ids >= 2 * tile, low1, 0.0)
     low1_own = mm(own[:, tile : 2 * tile] - mm_nt(low0_own, scaled_corner), inverses[1])
     low1_own = jnp.where(col > 1, low1_own, 0.0)
-    scaled1 = scale(low1_own, factors, 1)
+    scaled1 = scale(low1_own, pivots, couplings, pattern, 1)
     matrix = matrix - mm_nt(low1, scaled1)
     out[...] = jnp.where(jnp.logical_and(ids >= 2 * tile, col == 1), low1, matrix)
 
@@ -241,24 +247,25 @@
     piece = height // cols_axis
     lead = panels * tile
 
-    links = couplings * pattern.astype(f32)
-    ends = jnp.zeros((panels, 1), f32)
-    links_after = jnp.concatenate([links[:, :-1], ends], axis=1)
-    links_before = jnp.concatenate([ends, links[:, :-1]], axis=1)
-    factors = jnp.stack([pivots, links_after, links_before], axis=1).reshape(3 * panels, tile)
     me = jnp.stack([row, col, row % 2]).astype(jnp.int32)
 
     def flip(value, bit):
         return lax.ppermute(value, "row", [(i, i ^ bit) for i in range(rows_axis)])
 
     half = 2 * amount
-    keep, send, target, source = call(
+    lists = swaps.reshape(2 * panels, amount)
+    keep, send = call(
         functools.partial(gather_moved, rows_axis),
-        [(half, tile), (half, tile), ((1, 2 * half), jnp.int32), ((1, lead + half), jnp.int32)],
+        [(half, tile), (half, tile)],
         me,
-        swaps.reshape(2 * panels, amount),
+        lists,
         kkt,
         smem=1,
+        far=2,
+        scratch=[pltpu.VMEM(lists.shape, jnp.int32), pltpu.VMEM(kkt.shape, f32), pltpu.SemaphoreType.DMA((2,))],
+    )
+    target, source = call(
+        index_vectors, [((1, 2 * half), jnp.int32), ((1, lead + half), jnp.int32)], lists
     )
     mine = keep + flip(send, 1)
     if rows_axis == 4:
@@ -287,7 +294,9 @@
     )
 
     whole = lax.all_to_all(block, "col", 0, 0, tiled=True)
-    (part,) = call(functools.partial(pick_columns, panels), [(piece, lead + half)], source, whole)
+    part, panel_part = call(
+        functools.partial(pick_columns, panels), [(piece, lead + half), (piece, lead)], source, whole
+    )
     ring = list(range(0, cols_axis, 2)) + list(range(cols_axis - 1, 0, -2))
     after = [(ring[i], ring[(i + 1) % cols_axis]) for i in range(cols_axis)]
     before = [(b, a) for a, b in after]
@@ -309,7 +318,7 @@
 
     near_parts = [
         lax.ppermute(
-            part[:, :lead],
+            panel_part,
             ("row", "col"),
             [
                 (t % rows_axis * cols_axis + t // rows_axis * pieces + i, (i ^ bits) * cols_axis + t)
@@ -324,14 +333,7 @@
     own_order = row ^ jnp.array(own_bits, jnp.int32)
 
     (corner,) = call(first_corner, [(tile, tile)], order, me, *parts, smem=2)
-    bit = 2
-    holders = [1]
-    while bit < rows_axis:
-        corner = corner + lax.ppermute(corner, "row", [(i, i ^ bit) for i in holders])
-        holders += [i ^ bit for i in holders]
-        bit *= 2
-    corner = corner + lax.ppermute(corner, "row", [(i, i ^ 1) for i in holders])
-
+    corners = [corner if r == 1 else lax.ppermute(corner, "row", [(1, r)]) for r in range(rows_axis)]
     (out,) = call(
         functools.partial(finish, rows_axis),
         [(height, tile)],
@@ -340,13 +342,19 @@
         me,
         target,
         block,
-        corner,
         inverses,
-        factors,
+        pivots,
+        couplings,
+        pattern,
         *parts,
         *own_parts,
+        *corners,
         smem=3,
-        scratch=[pltpu.VMEM((height, lead + half), f32), pltpu.VMEM((tile, lead), f32)],
+        scratch=[
+            pltpu.VMEM((height, lead + half), f32),
+            pltpu.VMEM((tile, lead), f32),
+            pltpu.VMEM((tile, tile), f32),
+        ],
     )
     return out
 

time: 79.2 us -> 76.1 us (0.961)
  the two profiles are of different devices: /device:TPU:0 before, /device:TPU:12 now
where the time goes in v3:
time: 76.1 us; the launch traced here: 75.8 us
  waiting for transfers between devices  31.3 us (41%)
  blocking collectives  19.9 us (26%)
  starting transfers between devices  14 us (18%)
  Pallas kernels  8.55 us (11%)
  local copies, waits for them, and re-layouts  1.68 us (2%)
    all_to_all x1, blocking collectives, shards(): whole = lax.all_to_all(block, 'col', 0, 0, tiled=True)  19.9 us
    ppermute x4, waiting for transfers between devices, shards(): right = lax.ppermute(right, 'col', after)  15 us
    ppermute x5, waiting for transfers between devices, flip(): return lax.ppermute(value, 'row', [(i, i ^ bit) for i in range(rows_axis)])  8.58 us
    pallas_call x6, Pallas kernels, call(): pl.pallas_call(body, out_shape=[jax.ShapeDtypeStruct(*out) if isinstance(...  8.55 us
    ppermute x3, starting transfers between devices, shards(): left = lax.ppermute(left, 'col', before)  7.5 us
    ppermute x3, waiting for transfers between devices, shards(): lax.ppermute(corner, 'row', [(1, r)])  4.7 us
    ppermute x3, waiting for transfers between devices, shards(): left = lax.ppermute(left, 'col', before)  3.04 us
    ppermute x3, starting transfers between devices, shards(): lax.ppermute(corner, 'row', [(1, r)])  2.65 us
  transfers between devices with their start and end apart: 17, of which 11 were waited for; matrix products, arithmetic and copies ran while one was open for 0% of the time, Pallas kernels for 1%

profile of v3, /device:TPU:12, one launch (start us, length us, event | category | flops | bytes accessed | tf_op | source)
XLA Modules:
  0.0 75.8 jit_solution(4239837170639327302)
XLA Ops:
  0.0 0.1 pad_add_fusion.me
  0.1 0.6 copy-done.3
  0.7 1.0 %copy-done = f32[512,256]{1,0:T(8,128)S(1)} copy-done((f32[512,256]{1,0:T(8,128)S(1)}, f32[512,256]{1,0:T(8,128)}, u32[]{:S(2)}) %copy-start) | copy-done | bytes 524312
  1.7 1.7 %shard_map.83 = (f32[256,256]{1,0:T(8,128)S(1)}, f32[256,256]{1,0:T(8,128)S(1)}) custom-call(s32[3]{0:T(128)S(1)} %pad_add_fusion.me, s32[4,128]{1,0:T(4,128)S(1)} %bitcast.8, f32[512,256]{1,0:T(8,128)S(1)} %copy-done), custom_call_target="tpu_custom_call" | custom-call | tf_op jit(solution)/shard_map/pallas_call | solution.py:59
  3.5 0.1 collective-permute-start
  3.5 1.5 %collective-permute-done = f32[256,256]{1,0:T(8,128)S(1)} collective-permute-done((f32[256,256]{1,0:T(8,128)S(1)}, f32[256,256]{1,0:T(8,128)S(1)}, u32[]{:S(2)}, u32[]{:S(2)}) %collective-permute-start) | collective-permute-done | bytes 262176 | tf_op jit(solution)/shard_map/ppermute | solution.py:253
  5.1 0.0 copy-start.1
  5.1 0.6 collective-permute-start.1
  5.7 5.0 %collective-permute-done.1 = f32[128,256]{1,0:T(8,128)S(1)} collective-permute-done((f32[128,256]{1,0:T(8,128)S(1)}, f32[128,256]{1,0:T(8,128)S(1)}, u32[]{:S(2)}, u32[]{:S(2)}) %collective-permute-start.1) | collective-permute-done | bytes 131104 | tf_op jit(solution)/shard_map/ppermute | solution.py:253
  10.8 0.1 collective-permute-start.2
  10.9 0.3 shard_map.82
  11.2 1.0 %collective-permute-done.2.other = f32[128,256]{1,0:T(8,128)S(1)} collective-permute-done((f32[128,256]{1,0:T(8,128)S(1)}, f32[128,256]{1,0:T(8,128)S(1)}, u32[]{:S(2)}, u32[]{:S(2)}) %collective-permute-start.2) | collective-permute-done | bytes 131104 | tf_op jit(solution)/shard_map/ppermute | solution.py:253
  12.2 1.1 %shard_map.84.block = f32[512,256]{1,0:T(8,128)S(1)} custom-call(s32[3]{0:T(128)S(1)} %pad_add_fusion.me, s32[1,512]{1,0:T(1,128)S(1)} %get-tuple-element.11.target, f32[512,256]{1,0:T(8,128)S(1)} %copy-done.1, f32[128,256]{1,0:T(8,128)S(1)} %get-tuple-element.18.lead_rows, f32[128,256]{1,0:T(8,128)S(1)} %get-tuple-element.17.mine, ...), custom_call_target="tpu_custom_call" | custom-call | tf_op jit(solution)/shard_map/pallas_call | solution.py:59
  13.3 19.9 %all_to_all.11 = f32[8,64,256]{2,1,0:T(8,128)S(1)} all-to-all(f32[8,64,256]{2,1,0:T(8,128)S(1)} %bitcast.6), channel_id=1, replica_groups=mesh['row'=4,'col'=8] {'col'}, dimensions={0} | all-to-all | bytes 1048576 | tf_op jit(solution)/shard_map/all_to_all | solution.py:296
  33.2 0.5 shard_map.85
  33.7 0.6 collective-permute-start.3
  34.3 1.5 %collective-permute-start.4 = (f32[64,768]{1,0:T(8,128)S(1)}, f32[64,768]{1,0:T(8,128)S(1)}, u32[]{:S(2)}, u32[]{:S(2)}) collective-permute-start(f32[64,768]{1,0:T(8,128)S(1)} %get-tuple-element.15.refs_0_), channel_id=1, source_target_pairs={{2,0},{4,2},{6,4},{7,6},{5,7},{3,5},{1,3},{0,1},{10,8},{12,10},{14... | collective-permute-start | bytes 589832 | tf_op jit(solution)/shard_map/ppermute | solution.py:312
  35.8 3.7 %collective-permute-done.3.refs_1_ = f32[64,768]{1,0:T(8,128)S(1)} collective-permute-done((f32[64,768]{1,0:T(8,128)S(1)}, f32[64,768]{1,0:T(8,128)S(1)}, u32[]{:S(2)}, u32[]{:S(2)}) %collective-permute-start.3) | collective-permute-done | bytes 196640 | tf_op jit(solution)/shard_map/ppermute | solution.py:308
  39.5 0.8 %collective-permute-start.5 = (f32[64,768]{1,0:T(8,128)S(1)}, f32[64,768]{1,0:T(8,128)S(1)}, u32[]{:S(2)}, u32[]{:S(2)}) collective-permute-start(f32[64,768]{1,0:T(8,128)S(1)} %collective-permute-done.3.refs_1_), channel_id=1, source_target_pairs={{0,2},{2,4},{4,6},{6,7},{7,5},{5,3},{3,1},{1,0},{8,10},{10,12},{12... | collective-permute-start | bytes 589832 | tf_op jit(solution)/shard_map/ppermute | solution.py:308
  40.2 0.0 collective-permute-done.4.refs_2_
  40.2 1.3 %collective-permute-start.6 = (f32[64,768]{1,0:T(8,128)S(1)}, f32[64,768]{1,0:T(8,128)S(1)}, u32[]{:S(2)}, u32[]{:S(2)}) collective-permute-start(f32[64,768]{1,0:T(8,128)S(1)} %collective-permute-done.4.refs_2_), channel_id=1, source_target_pairs={{2,0},{4,2},{6,4},{7,6},{5,7},{3,5},{1,3},{0,1},{10,8},{12,10},{14... | collective-permute-start | bytes 589832 | tf_op jit(solution)/shard_map/ppermute | solution.py:312
  41.5 4.8 %collective-permute-done.5.refs_3_ = f32[64,768]{1,0:T(8,128)S(1)} collective-permute-done((f32[64,768]{1,0:T(8,128)S(1)}, f32[64,768]{1,0:T(8,128)S(1)}, u32[]{:S(2)}, u32[]{:S(2)}) %collective-permute-start.5) | collective-permute-done | bytes 196640 | tf_op jit(solution)/shard_map/ppermute | solution.py:308
  46.3 0.0 collective-permute-start.7
  46.3 0.5 collective-permute-start.11
  46.8 0.7 collective-permute-start.10
  47.5 0.0 collective-permute-done.6.refs_4_
  47.5 4.8 %collective-permute-start.8 = (f32[64,768]{1,0:T(8,128)S(1)}, f32[64,768]{1,0:T(8,128)S(1)}, u32[]{:S(2)}, u32[]{:S(2)}) collective-permute-start(f32[64,768]{1,0:T(8,128)S(1)} %collective-permute-done.6.refs_4_), channel_id=1, source_target_pairs={{2,0},{4,2},{6,4},{7,6},{5,7},{3,5},{1,3},{0,1},{10,8},{12,10},{14... | collective-permute-start | bytes 589832 | tf_op jit(solution)/shard_map/ppermute | solution.py:312
  52.3 0.9 %collective-permute-done.7.refs_5_ = f32[64,768]{1,0:T(8,128)S(1)} collective-permute-done((f32[64,768]{1,0:T(8,128)S(1)}, f32[64,768]{1,0:T(8,128)S(1)}, u32[]{:S(2)}, u32[]{:S(2)}) %collective-permute-start.7) | collective-permute-done | bytes 196640 | tf_op jit(solution)/shard_map/ppermute | solution.py:308
  53.2 0.0 collective-permute-start.9
  53.2 0.0 copy-start.7
  53.3 0.0 copy-start.2
  53.3 3.0 %collective-permute-done.8.refs_6_ = f32[64,768]{1,0:T(8,128)S(1)} collective-permute-done((f32[64,768]{1,0:T(8,128)S(1)}, f32[64,768]{1,0:T(8,128)S(1)}, u32[]{:S(2)}, u32[]{:S(2)}) %collective-permute-start.8) | collective-permute-done | bytes 196640 | tf_op jit(solution)/shard_map/ppermute | solution.py:312
  56.3 5.5 %collective-permute-done.9.refs_7_ = f32[64,768]{1,0:T(8,128)S(1)} collective-permute-done((f32[64,768]{1,0:T(8,128)S(1)}, f32[64,768]{1,0:T(8,128)S(1)}, u32[]{:S(2)}, u32[]{:S(2)}) %collective-permute-start.9) | collective-permute-done | bytes 196640 | tf_op jit(solution)/shard_map/ppermute | solution.py:308
  61.8 0.6 shard_map.86.refs_13_
  62.5 0.7 collective-permute-start.16
  63.2 1.3 %collective-permute-start.15 = (f32[256,256]{1,0:T(8,128)S(1)}, f32[256,256]{1,0:T(8,128)S(1)}, u32[]{:S(2)}, u32[]{:S(2)}) collective-permute-start(f32[256,256]{1,0:T(8,128)S(1)} %shard_map.86.refs_13_), channel_id=1, source_target_pairs={{8,16},{9,17},{10,18},{11,19},{12,20},{13,21},{14,22},{15,23}} | collective-permute-start | bytes 786440 | tf_op jit(solution)/shard_map/ppermute | solution.py:336
  64.5 0.7 collective-permute-start.14
  65.1 0.0 collective-permute-done.11.refs_9_
  65.2 0.1 collective-permute-start.13
  65.2 0.0 collective-permute-done.10.refs_8_
  65.2 0.5 collective-permute-start.12
  65.7 0.8 %collective-permute-done.13.refs_11_ = f32[64,512]{1,0:T(8,128)S(1)} collective-permute-done((f32[64,512]{1,0:T(8,128)S(1)}, f32[64,512]{1,0:T(8,128)S(1)}, u32[]{:S(2)}, u32[]{:S(2)}) %collective-permute-start.13) | collective-permute-done | bytes 131104 | tf_op jit(solution)/shard_map/ppermute | solution.py:253
  66.6 0.2 collective-permute-done.12.refs_10_
  66.8 0.0 collective-permute-done.16.refs_15_
  66.8 4.7 %collective-permute-done.15.refs_14_ = f32[256,256]{1,0:T(8,128)S(1)} collective-permute-done((f32[256,256]{1,0:T(8,128)S(1)}, f32[256,256]{1,0:T(8,128)S(1)}, u32[]{:S(2)}, u32[]{:S(2)}) %collective-permute-start.15) | collective-permute-done | bytes 262176 | tf_op jit(solution)/shard_map/ppermute | solution.py:336
  71.5 0.0 collective-permute-done.14.refs_12_
  71.5 0.0 copy-done.4
  71.5 4.3 %shard_map.87 = f32[512,256]{1,0:T(8,128)} custom-call(s32[8]{0:T(128)S(1)} %compare_select_fusion.2.order, s32[4]{0:T(128)S(1)} %broadcast_xor_fusion.own_order, s32[3]{0:T(128)S(1)} %pad_add_fusion.me, s32[1,512]{1,0:T(1,128)S(1)} %get-tuple-element.11.target, f32[512,256]{1,0:T(8,128)S(1)} %shard_map.84.block, f32[2,256,256]{2,1,0:T(8,128)S(1)} %copy-done.2, ...), custom_call_target="tpu_custom_call" | custom-call | tf_op jit(solution)/shard_map/pallas_call | solution.py:59
  (17 shorter events, 0.1 us)
Async XLA Ops:
  0.0 0.7 copy-start.3
  0.7 1.0 %copy-start = (f32[512,256]{1,0:T(8,128)S(1)}, f32[512,256]{1,0:T(8,128)}, u32[]{:S(2)}) copy-start(f32[512,256]{1,0:T(8,128)} %block.1) | copy-start | bytes 1572868
  3.5 1.6 %collective-permute-start = (f32[256,256]{1,0:T(8,128)S(1)}, f32[256,256]{1,0:T(8,128)S(1)}, u32[]{:S(2)}, u32[]{:S(2)}) collective-permute-start(f32[256,256]{1,0:T(8,128)S(1)} %get-tuple-element.13), channel_id=1, source_target_pairs={{0,8},{8,0},{16,24},{24,16},{1,9},{9,1},{17,25},{25,17},{2,10},{10... | collective-permute-start | bytes 786440 | tf_op jit(solution)/shard_map/ppermute | solution.py:253
  5.1 7.1 %copy-start.1 = (f32[512,256]{1,0:T(8,128)S(1)}, f32[512,256]{1,0:T(8,128)}, u32[]{:S(2)}) copy-start(f32[512,256]{1,0:T(8,128)} %block.1) | copy-start | bytes 1572868
  5.1 5.6 %collective-permute-start.1 = (f32[128,256]{1,0:T(8,128)S(1)}, f32[128,256]{1,0:T(8,128)S(1)}, u32[]{:S(2)}, u32[]{:S(2)}) collective-permute-start(f32[128,256]{1,0:T(8,128)S(1)} %slice_select_fusion.1), channel_id=1, source_target_pairs={{0,16},{8,24},{16,0},{24,8},{1,17},{9,25},{17,1},{25,9},{2,18},{10... | collective-permute-start | bytes 393224 | tf_op jit(solution)/shard_map/ppermute | solution.py:253
  10.8 1.4 %collective-permute-start.2 = (f32[128,256]{1,0:T(8,128)S(1)}, f32[128,256]{1,0:T(8,128)S(1)}, u32[]{:S(2)}, u32[]{:S(2)}) collective-permute-start(f32[128,256]{1,0:T(8,128)S(1)} %get-tuple-element.17.mine), channel_id=1, source_target_pairs={{0,8},{8,0},{16,24},{24,16},{1,9},{9,1},{17,25},{25,17},{2,10},{10... | collective-permute-start | bytes 393224 | tf_op jit(solution)/shard_map/ppermute | solution.py:253
  33.7 5.8 %collective-permute-start.3 = (f32[64,768]{1,0:T(8,128)S(1)}, f32[64,768]{1,0:T(8,128)S(1)}, u32[]{:S(2)}, u32[]{:S(2)}) collective-permute-start(f32[64,768]{1,0:T(8,128)S(1)} %get-tuple-element.15.refs_0_), channel_id=1, source_target_pairs={{0,2},{2,4},{4,6},{6,7},{7,5},{5,3},{3,1},{1,0},{8,10},{10,12},{12... | collective-permute-start | bytes 589832 | tf_op jit(solution)/shard_map/ppermute | solution.py:308
  34.3 5.9 %collective-permute-start.4 = (f32[64,768]{1,0:T(8,128)S(1)}, f32[64,768]{1,0:T(8,128)S(1)}, u32[]{:S(2)}, u32[]{:S(2)}) collective-permute-start(f32[64,768]{1,0:T(8,128)S(1)} %get-tuple-element.15.refs_0_), channel_id=1, source_target_pairs={{2,0},{4,2},{6,4},{7,6},{5,7},{3,5},{1,3},{0,1},{10,8},{12,10},{14... | collective-permute-start | bytes 589832 | tf_op jit(solution)/shard_map/ppermute | solution.py:312
  39.5 6.9 %collective-permute-start.5 = (f32[64,768]{1,0:T(8,128)S(1)}, f32[64,768]{1,0:T(8,128)S(1)}, u32[]{:S(2)}, u32[]{:S(2)}) collective-permute-start(f32[64,768]{1,0:T(8,128)S(1)} %collective-permute-done.3.refs_1_), channel_id=1, source_target_pairs={{0,2},{2,4},{4,6},{6,7},{7,5},{5,3},{3,1},{1,0},{8,10},{10,12},{12... | collective-permute-start | bytes 589832 | tf_op jit(solution)/shard_map/ppermute | solution.py:308
  40.2 7.3 %collective-permute-start.6 = (f32[64,768]{1,0:T(8,128)S(1)}, f32[64,768]{1,0:T(8,128)S(1)}, u32[]{:S(2)}, u32[]{:S(2)}) collective-permute-start(f32[64,768]{1,0:T(8,128)S(1)} %collective-permute-done.4.refs_2_), channel_id=1, source_target_pairs={{2,0},{4,2},{6,4},{7,6},{5,7},{3,5},{1,3},{0,1},{10,8},{12,10},{14... | collective-permute-start | bytes 589832 | tf_op jit(solution)/shard_map/ppermute | solution.py:312
  46.3 6.9 %collective-permute-start.7 = (f32[64,768]{1,0:T(8,128)S(1)}, f32[64,768]{1,0:T(8,128)S(1)}, u32[]{:S(2)}, u32[]{:S(2)}) collective-permute-start(f32[64,768]{1,0:T(8,128)S(1)} %collective-permute-done.5.refs_3_), channel_id=1, source_target_pairs={{0,2},{2,4},{4,6},{6,7},{7,5},{5,3},{3,1},{1,0},{8,10},{10,12},{12... | collective-permute-start | bytes 589832 | tf_op jit(solution)/shard_map/ppermute | solution.py:308
  46.3 6.9 %copy-start.8 = (s32[8]{0:T(128)S(1)}, s32[8]{0:T(128)}, u32[]{:S(2)}) copy-start(s32[8]{0:T(128)} %constant.63.clone) | copy-start | bytes 100
  46.3 18.8 %collective-permute-start.11 = (f32[64,512]{1,0:T(8,128)S(1)}, f32[64,512]{1,0:T(8,128)S(1)}, u32[]{:S(2)}, u32[]{:S(2)}) collective-permute-start(f32[64,512]{1,0:T(8,128)S(1)} %get-tuple-element.16), channel_id=1, source_target_pairs={{0,16},{1,24},{2,0},{3,8},{8,17},{9,25},{10,1},{11,9},{16,18},{17,... | collective-permute-start | bytes 393224 | tf_op jit(solution)/shard_map/ppermute | solution.py:320
  46.8 18.4 %collective-permute-start.10 = (f32[64,512]{1,0:T(8,128)S(1)}, f32[64,512]{1,0:T(8,128)S(1)}, u32[]{:S(2)}, u32[]{:S(2)}) collective-permute-start(f32[64,512]{1,0:T(8,128)S(1)} %get-tuple-element.16), channel_id=1, source_target_pairs={{0,0},{1,8},{2,16},{3,24},{8,1},{9,9},{10,17},{11,25},{16,2},{17,1... | collective-permute-start | bytes 393224 | tf_op jit(solution)/shard_map/ppermute | solution.py:320
  47.5 8.8 %collective-permute-start.8 = (f32[64,768]{1,0:T(8,128)S(1)}, f32[64,768]{1,0:T(8,128)S(1)}, u32[]{:S(2)}, u32[]{:S(2)}) collective-permute-start(f32[64,768]{1,0:T(8,128)S(1)} %collective-permute-done.6.refs_4_), channel_id=1, source_target_pairs={{2,0},{4,2},{6,4},{7,6},{5,7},{3,5},{1,3},{0,1},{10,8},{12,10},{14... | collective-permute-start | bytes 589832 | tf_op jit(solution)/shard_map/ppermute | solution.py:312
  53.2 8.6 %collective-permute-start.9 = (f32[64,768]{1,0:T(8,128)S(1)}, f32[64,768]{1,0:T(8,128)S(1)}, u32[]{:S(2)}, u32[]{:S(2)}) collective-permute-start(f32[64,768]{1,0:T(8,128)S(1)} %collective-permute-done.7.refs_5_), channel_id=1, source_target_pairs={{0,2},{2,4},{4,6},{6,7},{7,5},{5,3},{3,1},{1,0},{8,10},{10,12},{12... | collective-permute-start | bytes 589832 | tf_op jit(solution)/shard_map/ppermute | solution.py:308
  53.2 12.5 %copy-start.7 = (s32[4]{0:T(128)S(1)}, s32[4]{0:T(128)}, u32[]{:S(2)}) copy-start(s32[4]{0:T(128)} %constant.64.clone) | copy-start | bytes 52
  53.3 18.2 %copy-start.2 = (f32[2,256,256]{2,1,0:T(8,128)S(1)}, f32[2,256,256]{2,1,0:T(8,128)}, u32[]{:S(2)}) copy-start(f32[2,256,256]{2,1,0:T(8,128)} %inverses.1) | copy-start | bytes 1572868
  61.8 9.6 %copy-start.4 = (f32[2,256]{1,0:T(2,128)S(1)}, f32[2,256]{1,0:T(2,128)}, u32[]{:S(2)}) copy-start(f32[2,256]{1,0:T(2,128)} %pivots.1) | copy-start | bytes 6148
  61.8 9.6 %copy-start.5 = (f32[2,256]{1,0:T(2,128)S(1)}, f32[2,256]{1,0:T(2,128)}, u32[]{:S(2)}) copy-start(f32[2,256]{1,0:T(2,128)} %couplings.1) | copy-start | bytes 6148
  61.8 9.6 %copy-start.6 = (s32[2,256]{1,0:T(2,128)S(1)}, s32[2,256]{1,0:T(2,128)}, u32[]{:S(2)}) copy-start(s32[2,256]{1,0:T(2,128)} %pattern.1) | copy-start | bytes 6148
  62.5 4.3 %collective-permute-start.16 = (f32[256,256]{1,0:T(8,128)S(1)}, f32[256,256]{1,0:T(8,128)S(1)}, u32[]{:S(2)}, u32[]{:S(2)}) collective-permute-start(f32[256,256]{1,0:T(8,128)S(1)} %shard_map.86.refs_13_), channel_id=1, source_target_pairs={{8,24},{9,25},{10,26},{11,27},{12,28},{13,29},{14,30},{15,31}} | collective-permute-start | bytes 786440 | tf_op jit(solution)/shard_map/ppermute | solution.py:336
  63.2 8.3 %collective-permute-start.15 = (f32[256,256]{1,0:T(8,128)S(1)}, f32[256,256]{1,0:T(8,128)S(1)}, u32[]{:S(2)}, u32[]{:S(2)}) collective-permute-start(f32[256,256]{1,0:T(8,128)S(1)} %shard_map.86.refs_13_), channel_id=1, source_target_pairs={{8,16},{9,17},{10,18},{11,19},{12,20},{13,21},{14,22},{15,23}} | collective-permute-start | bytes 786440 | tf_op jit(solution)/shard_map/ppermute | solution.py:336
  64.5 7.0 %collective-permute-start.14 = (f32[256,256]{1,0:T(8,128)S(1)}, f32[256,256]{1,0:T(8,128)S(1)}, u32[]{:S(2)}, u32[]{:S(2)}) collective-permute-start(f32[256,256]{1,0:T(8,128)S(1)} %shard_map.86.refs_13_), channel_id=1, source_target_pairs={{8,0},{9,1},{10,2},{11,3},{12,4},{13,5},{14,6},{15,7}} | collective-permute-start | bytes 786440 | tf_op jit(solution)/shard_map/ppermute | solution.py:336
  65.2 1.4 %collective-permute-start.13 = (f32[64,512]{1,0:T(8,128)S(1)}, f32[64,512]{1,0:T(8,128)S(1)}, u32[]{:S(2)}, u32[]{:S(2)}) collective-permute-start(f32[64,512]{1,0:T(8,128)S(1)} %collective-permute-done.11.refs_9_), channel_id=1, source_target_pairs={{0,8},{8,0},{16,24},{24,16},{1,9},{9,1},{17,25},{25,17},{2,10},{10... | collective-permute-start | bytes 393224 | tf_op jit(solution)/shard_map/ppermute | solution.py:253
  65.2 1.5 %collective-permute-start.12 = (f32[64,512]{1,0:T(8,128)S(1)}, f32[64,512]{1,0:T(8,128)S(1)}, u32[]{:S(2)}, u32[]{:S(2)}) collective-permute-start(f32[64,512]{1,0:T(8,128)S(1)} %collective-permute-done.10.refs_8_), channel_id=1, source_target_pairs={{0,8},{8,0},{16,24},{24,16},{1,9},{9,1},{17,25},{25,17},{2,10},{10... | collective-permute-start | bytes 393224 | tf_op jit(solution)/shard_map/ppermute | solution.py:253

commit v4 on v3

--- a/solution.py
+++ b/solution.py
@@ -54,7 +54,7 @@
     return lower * pivots[panel : panel + 1, :] + after * link + before * pltpu.roll(link, 1, 1)
 
 
-def call(body, outs, *args, smem=0, far=0, scratch=()):
+def call(body, outs, *args, smem=0, scratch=()):
     vmem = pl.BlockSpec(memory_space=pltpu.VMEM)
     return pl.pallas_call(
         body,
@@ -62,9 +62,7 @@
             jax.ShapeDtypeStruct(*out) if isinstance(out[1], type) else jax.ShapeDtypeStruct(out, f32)
             for out in outs
         ],
-        in_specs=[pl.BlockSpec(memory_space=pltpu.SMEM)] * smem
-        + [vmem] * (len(args) - smem - far)
-        + [pl.BlockSpec(memory_space=pltpu.HBM)] * far,
+        in_specs=[pl.BlockSpec(memory_space=pltpu.SMEM)] * smem + [vmem] * (len(args) - smem),
         out_specs=[vmem] * len(outs),
         scratch_shapes=list(scratch),
         compiler_params=pltpu.CompilerParams(vmem_limit_bytes=VMEM_LIMIT),
@@ -90,18 +88,12 @@
     return jnp.where(found, jnp.sum(jnp.where(hit, values, 0), axis=axis, keepdims=True), other)
 
 
-def gather_moved(rows_axis, me, swaps_far, block_far, keep, send, swaps, block, done):
-    fetch_swaps = pltpu.make_async_copy(swaps_far, swaps, done.at[0])
-    fetch = pltpu.make_async_copy(block_far, block, done.at[1])
-    fetch_swaps.start()
-    fetch.start()
-    fetch_swaps.wait()
+def gather_moved(rows_axis, me, swaps, block, keep, send):
     height, tile = block.shape
     (lead0, partner0, _, _), ups = swap_lists(swaps)
     wanted = [ups[0], ups[1]] + [either(ups[i] == partner0, lead0, ups[i], 1) for i in (2, 3)]
     ids = row_ids(me[0], rows_axis, height, tile, 1)
     chosen = ones_where(jnp.concatenate(wanted, axis=0) == ids)
-    fetch.wait()
     rows = pick_rows(chosen, block[...])
     half = keep.shape[0]
     odd = me[2] == 1
@@ -123,7 +115,7 @@
     source[...] = jnp.concatenate([first, second, lead0, source1], axis=1)
 
 
-def place_moved(rows_axis, me, target, block, lead_rows, mine, other, out):
+def place_moved(rows_axis, me, aims_col, target, block, lead_rows, mine, other, out, *pieces):
     height, tile = block.shape
     amount = target.shape[1] // 4
     odd = me[2] == 1
@@ -137,45 +129,42 @@
     moved = jnp.max(jnp.where(hit, 1, 0), axis=1, keepdims=True) > 0
     rows = pick_rows(ones_where(hit), jnp.concatenate([lead_rows[...], first, second], axis=0))
     out[...] = jnp.where(moved, rows, block[...])
-
-
-def pick_columns(lead_tiles, source, whole, out, panel_out):
-    piece = out.shape[0]
-    tile = whole.shape[1]
+    for i, ref in enumerate(pieces):
+        piece = ref.shape[0]
+        ref[...] = out[pl.ds(pl.multiple_of(aims_col[i] * piece, piece), piece), :]
+
+
+def pick_columns(lead_tiles, me, tiles, source, inverses, *refs):
+    *pieces, out, panel_out = refs
+    piece, tile = pieces[0].shape
     lead = lead_tiles * tile
     wanted = source[...]
     index = lax.broadcasted_iota(jnp.int32, (tile, 1), 0)
-    total = None
-    for t in range(whole.shape[0] // piece):
-        block = jnp.concatenate(split(whole[t * piece : (t + 1) * piece, :]), axis=0)
-        part = wanted if t < lead_tiles else wanted[:, :lead]
-        term = jnp.dot(block, ones_where(index + t * tile == part), preferred_element_type=f32)
-        if total is None:
-            total = term
-        elif t < lead_tiles:
-            total = total + term
-        else:
-            total = jnp.concatenate([total[:, :lead] + term, total[:, lead:]], axis=1)
+    total = 0.0
+    for i, ref in enumerate(pieces):
+        block = jnp.concatenate(split(ref[...]), axis=0)
+        total = total + jnp.dot(block, ones_where(index + tiles[i] * tile == wanted), preferred_element_type=f32)
     total = total[:piece] + total[piece:]
-    out[...] = total
-    panel_out[...] = total[:, :lead]
-
-
-def first_corner(order, me, *refs):
+    in_first_tile = me[1] < tile // piece
+    for panel in range(lead_tiles):
+        place = slice(panel * tile, (panel + 1) * tile)
+        plain = jnp.logical_and(me[0] == panel, in_first_tile)
+        part = total[:, place]
+        part = jnp.where(plain, part, mm(part, inverses[panel]))
+        out[:, place] = part
+        panel_out[:, place] = part
+    out[:, lead:] = total[:, lead:]
+
+
+def collect(rank, *refs):
     *pieces, out = refs
     piece = pieces[0].shape[0]
-    tile = out.shape[0]
-    holder = me[0] == 1
-
-    @pl.when(jnp.logical_not(holder))
-    def _():
-        out[...] = jnp.zeros_like(out)
-
+    count = out.shape[0] // piece
     for i, ref in enumerate(pieces):
 
-        @pl.when(jnp.logical_and(holder, order[i] < tile // piece))
+        @pl.when(rank[i] < count)
         def _(i=i, ref=ref):
-            out[pl.ds(pl.multiple_of(order[i] * piece, piece), piece), :] = ref[:, :tile]
+            out[pl.ds(pl.multiple_of(rank[i] * piece, piece), piece), :] = ref[:, : out.shape[1]]
 
 
 def finish(
@@ -213,17 +202,14 @@
     matrix = jnp.where(moved, swapped, block[...])
     matrix = jnp.where(col == 0, first, jnp.where(col == 1, second, matrix))
 
-    low0 = jnp.where(ids >= tile, mm(first, inverses[0]), 0.0)
-    low0_own = jnp.where(col > 0, mm(own[:, :tile], inverses[0]), 0.0)
+    low0 = jnp.where(ids >= tile, first, 0.0)
+    low0_own = jnp.where(col > 0, own[:, :tile], 0.0)
     scaled0 = scale(low0_own, pivots, couplings, pattern, 0)
     matrix = matrix - mm_nt(low0, scaled0)
-    matrix = jnp.where(jnp.logical_and(ids >= tile, col == 0), low0, matrix)
-
-    scaled_corner = scale(mm(corner[...], inverses[0]), pivots, couplings, pattern, 0)
-    low1 = mm(second - mm_nt(low0, scaled_corner), inverses[1])
-    low1 = jnp.where(ids >= 2 * tile, low1, 0.0)
-    low1_own = mm(own[:, tile : 2 * tile] - mm_nt(low0_own, scaled_corner), inverses[1])
-    low1_own = jnp.where(col > 1, low1_own, 0.0)
+
+    update = mm(scale(corner[...], pivots, couplings, pattern, 0).T, inverses[1])
+    low1 = jnp.where(ids >= 2 * tile, second - mm(low0, update), 0.0)
+    low1_own = jnp.where(col > 1, own[:, tile : 2 * tile] - mm(low0_own, update), 0.0)
     scaled1 = scale(low1_own, pivots, couplings, pattern, 1)
     matrix = matrix - mm_nt(low1, scaled1)
     out[...] = jnp.where(jnp.logical_and(ids >= 2 * tile, col == 1), low1, matrix)
@@ -261,8 +247,6 @@
         lists,
         kkt,
         smem=1,
-        far=2,
-        scratch=[pltpu.VMEM(lists.shape, jnp.int32), pltpu.VMEM(kkt.shape, f32), pltpu.SemaphoreType.DMA((2,))],
     )
     target, source = call(
         index_vectors, [((1, 2 * half), jnp.int32), ((1, lead + half), jnp.int32)], lists
@@ -281,41 +265,41 @@
         lead_rows = mine[amount:]
         mine = mine[:amount]
     other = flip(mine, 1)
-    (block,) = call(
+    direct = cols_axis <= 8
+    tiles = jnp.arange(cols_axis, dtype=jnp.int32)
+    tiles = col ^ tiles if direct else tiles
+    block, *pieces = call(
         functools.partial(place_moved, rows_axis),
-        [(height, tile)],
+        [(height, tile)] + [(piece, tile)] * (cols_axis if direct else 0),
         me,
+        tiles,
         target,
         kkt,
         lead_rows,
         mine,
         other,
-        smem=1,
-    )
-
-    whole = lax.all_to_all(block, "col", 0, 0, tiled=True)
+        smem=2,
+    )
+    if direct:
+        for i in reversed(range(1, cols_axis)):
+            pieces[i] = lax.ppermute(pieces[i], "col", [(c, c ^ i) for c in range(cols_axis)])
+    else:
+        whole = lax.all_to_all(block, "col", 0, 0, tiled=True)
+        pieces = [whole[i * piece : (i + 1) * piece] for i in range(cols_axis)]
     part, panel_part = call(
-        functools.partial(pick_columns, panels), [(piece, lead + half), (piece, lead)], source, whole
+        functools.partial(pick_columns, panels),
+        [(piece, lead + half), (piece, lead)],
+        me,
+        tiles,
+        source,
+        inverses,
+        *pieces,
+        smem=2,
     )
     ring = list(range(0, cols_axis, 2)) + list(range(cols_axis - 1, 0, -2))
     after = [(ring[i], ring[(i + 1) % cols_axis]) for i in range(cols_axis)]
     before = [(b, a) for a, b in after]
     pieces = tile // piece
-    right, left = part, part
-    parts, steps = [part], [0]
-    last = cols_axis // 2
-    for step in range(1, last + 1):
-        right = lax.ppermute(right, "col", after)
-        parts.append(right)
-        steps.append(-step)
-        if step < last:
-            left = lax.ppermute(left, "col", before)
-            parts.append(left)
-            steps.append(step)
-    place = jnp.where(col % 2 == 0, col // 2, cols_axis - 1 - col // 2)
-    order = (place + jnp.array(steps, jnp.int32)) % cols_axis
-    order = jnp.where(order < last, 2 * order, 2 * (cols_axis - 1 - order) + 1)
-
     near_parts = [
         lax.ppermute(
             panel_part,
@@ -328,12 +312,33 @@
         )
         for bits in range(0, rows_axis, 2)
     ]
-    own_parts = near_parts + [flip(near_part, 1) for near_part in near_parts]
+    right, left = part, part
+    parts, steps = [part], [0]
+    last = cols_axis // 2
+    for step in range(1, last + 1):
+        if step == last:
+            right, near_parts = lax.optimization_barrier((right, near_parts))
+            parts[-2] = right
+        right = lax.ppermute(right, "col", after)
+        parts.append(right)
+        steps.append(-step)
+        if step < last:
+            left = lax.ppermute(left, "col", before)
+            parts.append(left)
+            steps.append(step)
+    place = jnp.where(col % 2 == 0, col // 2, cols_axis - 1 - col // 2)
+    order = (place + jnp.array(steps, jnp.int32)) % cols_axis
+    order = jnp.where(order < last, 2 * order, 2 * (cols_axis - 1 - order) + 1)
+
     own_bits = [bits + core for core in range(2) for bits in range(0, rows_axis, 2)]
     own_order = row ^ jnp.array(own_bits, jnp.int32)
 
-    (corner,) = call(first_corner, [(tile, tile)], order, me, *parts, smem=2)
+    pairs = [(cols_axis + c, cols_axis + ring[(ring.index(c) + last) % cols_axis]) for c in range(pieces)]
+    extra = lax.ppermute(panel_part[:, :tile], ("row", "col"), pairs)
+    (corner,) = call(collect, [(tile, tile)], order, *parts[:-1], extra, smem=1)
     corners = [corner if r == 1 else lax.ppermute(corner, "row", [(1, r)]) for r in range(rows_axis)]
+    parts[-1], corners[3], near_parts = lax.optimization_barrier((parts[-1], corners[3], near_parts))
+    own_parts = near_parts + [flip(near_part, 1) for near_part in near_parts]
     (out,) = call(
         functools.partial(finish, rows_axis),
         [(height, tile)],

time: 76.1 us -> 71.4 us (0.938)
  the two profiles are of different devices: /device:TPU:12 before, /device:TPU:0 now
where the time goes in v4:
time: 71.4 us; the launch traced here: 71.1 us
  waiting for transfers between devices  32.4 us (45%)
  starting transfers between devices  28 us (39%)
  Pallas kernels  8.71 us (12%)
  local copies, waits for them, and re-layouts  1.69 us (2%)
    ppermute x4, waiting for transfers between devices, shards(): right = lax.ppermute(right, 'col', after)  11.8 us
    ppermute x7, starting transfers between devices, shards(): lax.ppermute(pieces[i], 'col', [(c, c ^ i) for c in range(cols_axis)])  11.3 us
    pallas_call x6, Pallas kernels, call(): pl.pallas_call(body, out_shape=[jax.ShapeDtypeStruct(*out) if isinstance(...  8.71 us
    ppermute x5, waiting for transfers between devices, flip(): return lax.ppermute(value, 'row', [(i, i ^ bit) for i in range(rows_axis)])  7.15 us
    ppermute x7, waiting for transfers between devices, shards(): lax.ppermute(pieces[i], 'col', [(c, c ^ i) for c in range(cols_axis)])  7.02 us
    ppermute x3, waiting for transfers between devices, shards(): left = lax.ppermute(left, 'col', before)  6.4 us
    ppermute x4, starting transfers between devices, shards(): right = lax.ppermute(right, 'col', after)  4.59 us
    ppermute x5, starting transfers between devices, flip(): return lax.ppermute(value, 'row', [(i, i ^ bit) for i in range(rows_axis)])  4.05 us
  transfers between devices with their start and end apart: 25, of which 13 were waited for; matrix products, arithmetic and copies ran while one was open for 0% of the time, Pallas kernels for 0%

profile of v4, /device:TPU:0, one launch (start us, length us, event | category | flops | bytes accessed | tf_op | source)
XLA Modules:
  0.0 71.1 jit_solution(8893605684936657330)
XLA Ops:
  0.0 0.1 pad_add_fusion.me
  0.1 0.6 copy-done.3
  0.7 1.0 %copy-done = f32[512,256]{1,0:T(8,128)S(1)} copy-done((f32[512,256]{1,0:T(8,128)S(1)}, f32[512,256]{1,0:T(8,128)}, u32[]{:S(2)}) %copy-start) | copy-done | bytes 524312
  1.7 1.8 %shard_map.83 = (f32[256,256]{1,0:T(8,128)S(1)}, f32[256,256]{1,0:T(8,128)S(1)}) custom-call(s32[3]{0:T(128)S(1)} %pad_add_fusion.me, s32[4,128]{1,0:T(4,128)S(1)} %bitcast.4, f32[512,256]{1,0:T(8,128)S(1)} %copy-done), custom_call_target="tpu_custom_call" | custom-call | tf_op jit(solution)/shard_map/pallas_call | solution.py:59
  3.5 0.5 collective-permute-start
  4.1 1.2 %collective-permute-done = f32[256,256]{1,0:T(8,128)S(1)} collective-permute-done((f32[256,256]{1,0:T(8,128)S(1)}, f32[256,256]{1,0:T(8,128)S(1)}, u32[]{:S(2)}, u32[]{:S(2)}) %collective-permute-start) | collective-permute-done | bytes 262176 | tf_op jit(solution)/shard_map/ppermute | solution.py:239
  5.3 0.0 copy-start.1
  5.3 2.9 %collective-permute-start.1 = (f32[128,256]{1,0:T(8,128)S(1)}, f32[128,256]{1,0:T(8,128)S(1)}, u32[]{:S(2)}, u32[]{:S(2)}) collective-permute-start(f32[128,256]{1,0:T(8,128)S(1)} %slice_select_fusion.1), channel_id=1, source_target_pairs={{0,16},{8,24},{16,0},{24,8},{1,17},{9,25},{17,1},{25,9},{2,18},{10... | collective-permute-start | bytes 393224 | tf_op jit(solution)/shard_map/ppermute | solution.py:239
  8.2 3.8 %collective-permute-done.1 = f32[128,256]{1,0:T(8,128)S(1)} collective-permute-done((f32[128,256]{1,0:T(8,128)S(1)}, f32[128,256]{1,0:T(8,128)S(1)}, u32[]{:S(2)}, u32[]{:S(2)}) %collective-permute-start.1) | collective-permute-done | bytes 131104 | tf_op jit(solution)/shard_map/ppermute | solution.py:239
  12.1 0.1 collective-permute-start.2
  12.2 0.3 shard_map.82
  12.5 1.0 %collective-permute-done.2.other = f32[128,256]{1,0:T(8,128)S(1)} collective-permute-done((f32[128,256]{1,0:T(8,128)S(1)}, f32[128,256]{1,0:T(8,128)S(1)}, u32[]{:S(2)}, u32[]{:S(2)}) %collective-permute-start.2) | collective-permute-done | bytes 131104 | tf_op jit(solution)/shard_map/ppermute | solution.py:239
  13.5 1.1 %shard_map.84 = (f32[512,256]{1,0:T(8,128)S(1)}, f32[64,256]{1,0:T(8,128)S(1)}, f32[64,256]{1,0:T(8,128)S(1)}, f32[64,256]{1,0:T(8,128)S(1)}, f32[64,256]{1,0:T(...) custom-call(s32[3]{0:T(128)S(1)} %pad_add_fusion.me, ...), custom_call_target="tpu_custom_call" | custom-call | tf_op jit(solution)/shard_map/pallas_call | solution.py:59
  14.6 1.8 %collective-permute-start.3 = (f32[64,256]{1,0:T(8,128)S(1)}, f32[64,256]{1,0:T(8,128)S(1)}, u32[]{:S(2)}, u32[]{:S(2)}) collective-permute-start(f32[64,256]{1,0:T(8,128)S(1)} %get-tuple-element.33), channel_id=1, source_target_pairs={{0,1},{1,0},{2,3},{3,2},{4,5},{5,4},{6,7},{7,6},{8,9},{9,8},{10,11... | collective-permute-start | bytes 196616 | tf_op jit(solution)/shard_map/ppermute | solution.py:285
  16.4 1.6 %collective-permute-start.4 = (f32[64,256]{1,0:T(8,128)S(1)}, f32[64,256]{1,0:T(8,128)S(1)}, u32[]{:S(2)}, u32[]{:S(2)}) collective-permute-start(f32[64,256]{1,0:T(8,128)S(1)} %get-tuple-element.34), channel_id=1, source_target_pairs={{0,2},{1,3},{2,0},{3,1},{4,6},{5,7},{6,4},{7,5},{8,10},{9,11},{10,... | collective-permute-start | bytes 196616 | tf_op jit(solution)/shard_map/ppermute | solution.py:285
  18.0 0.2 collective-permute-start.5
  18.2 2.8 %collective-permute-start.6 = (f32[64,256]{1,0:T(8,128)S(1)}, f32[64,256]{1,0:T(8,128)S(1)}, u32[]{:S(2)}, u32[]{:S(2)}) collective-permute-start(f32[64,256]{1,0:T(8,128)S(1)} %get-tuple-element.36), channel_id=1, source_target_pairs={{0,4},{1,5},{2,6},{3,7},{4,0},{5,1},{6,2},{7,3},{8,12},{9,13},{10,... | collective-permute-start | bytes 196616 | tf_op jit(solution)/shard_map/ppermute | solution.py:285
  21.0 1.3 %collective-permute-start.7 = (f32[64,256]{1,0:T(8,128)S(1)}, f32[64,256]{1,0:T(8,128)S(1)}, u32[]{:S(2)}, u32[]{:S(2)}) collective-permute-start(f32[64,256]{1,0:T(8,128)S(1)} %get-tuple-element.37), channel_id=1, source_target_pairs={{0,5},{1,4},{2,7},{3,6},{4,1},{5,0},{6,3},{7,2},{8,13},{9,12},{10,... | collective-permute-start | bytes 196616 | tf_op jit(solution)/shard_map/ppermute | solution.py:285
  22.3 3.6 %collective-permute-start.8 = (f32[64,256]{1,0:T(8,128)S(1)}, f32[64,256]{1,0:T(8,128)S(1)}, u32[]{:S(2)}, u32[]{:S(2)}) collective-permute-start(f32[64,256]{1,0:T(8,128)S(1)} %get-tuple-element.38), channel_id=1, source_target_pairs={{0,6},{1,7},{2,4},{3,5},{4,2},{5,3},{6,0},{7,1},{8,14},{9,15},{10,... | collective-permute-start | bytes 196616 | tf_op jit(solution)/shard_map/ppermute | solution.py:285
  25.9 0.0 collective-permute-start.9
  25.9 5.5 %collective-permute-done.7.refs_5_ = f32[64,256]{1,0:T(8,128)S(1)} collective-permute-done((f32[64,256]{1,0:T(8,128)S(1)}, f32[64,256]{1,0:T(8,128)S(1)}, u32[]{:S(2)}, u32[]{:S(2)}) %collective-permute-start.7) | collective-permute-done | bytes 65568 | tf_op jit(solution)/shard_map/ppermute | solution.py:285
  31.4 1.5 %collective-permute-done.9.refs_7_ = f32[64,256]{1,0:T(8,128)S(1)} collective-permute-done((f32[64,256]{1,0:T(8,128)S(1)}, f32[64,256]{1,0:T(8,128)S(1)}, u32[]{:S(2)}, u32[]{:S(2)}) %collective-permute-start.9) | collective-permute-done | bytes 65568 | tf_op jit(solution)/shard_map/ppermute | solution.py:285
  32.9 1.5 %shard_map.85 = (f32[64,768]{1,0:T(8,128)S(1)}, f32[64,512]{1,0:T(8,128)S(1)}) custom-call(s32[3]{0:T(128)S(1)} %pad_add_fusion.me, s32[8]{0:T(128)S(1)} %iota_xor_fusion.aims_col.tiles, s32[1,768]{1,0:T(1,128)S(1)} %get-tuple-element.31.source, f32[2,256,256]{2,1,0:T(8,128)S(1)} %copy-done.2, f32[64,256]{1,0:T(8,128)S(1)} %get-tuple-element.32.refs_0_, ...), custom_call_target="tpu_custom_call" | custom-call | tf_op jit(solution)/shard_map/pallas_call | solution.py:59
  34.4 0.6 collective-permute-start.11
  35.0 1.5 %collective-permute-start.10 = (f32[64,768]{1,0:T(8,128)S(1)}, f32[64,768]{1,0:T(8,128)S(1)}, u32[]{:S(2)}, u32[]{:S(2)}) collective-permute-start(f32[64,768]{1,0:T(8,128)S(1)} %get-tuple-element.40.refs_0_), channel_id=1, source_target_pairs={{0,2},{2,4},{4,6},{6,7},{7,5},{5,3},{3,1},{1,0},{8,10},{10,12},{12... | collective-permute-start | bytes 589832 | tf_op jit(solution)/shard_map/ppermute | solution.py:322
  36.5 4.5 %collective-permute-done.11.refs_2_ = f32[64,768]{1,0:T(8,128)S(1)} collective-permute-done((f32[64,768]{1,0:T(8,128)S(1)}, f32[64,768]{1,0:T(8,128)S(1)}, u32[]{:S(2)}, u32[]{:S(2)}) %collective-permute-start.11) | collective-permute-done | bytes 196640 | tf_op jit(solution)/shard_map/ppermute | solution.py:326
  41.0 0.2 collective-permute-start.13
  41.2 0.5 collective-permute-done.10.refs_1_
  41.7 1.3 %collective-permute-start.12 = (f32[64,768]{1,0:T(8,128)S(1)}, f32[64,768]{1,0:T(8,128)S(1)}, u32[]{:S(2)}, u32[]{:S(2)}) collective-permute-start(f32[64,768]{1,0:T(8,128)S(1)} %collective-permute-done.10.refs_1_), channel_id=1, source_target_pairs={{0,2},{2,4},{4,6},{6,7},{7,5},{5,3},{3,1},{1,0},{8,10},{10,12},{12... | collective-permute-start | bytes 589832 | tf_op jit(solution)/shard_map/ppermute | solution.py:322
  43.0 1.6 %collective-permute-start.16 = (f32[64,512]{1,0:T(8,128)S(1)}, f32[64,512]{1,0:T(8,128)S(1)}, u32[]{:S(2)}, u32[]{:S(2)}) collective-permute-start(f32[64,512]{1,0:T(8,128)S(1)} %get-tuple-element.41), channel_id=1, source_target_pairs={{0,16},{1,24},{2,0},{3,8},{8,17},{9,25},{10,1},{11,9},{16,18},{17,... | collective-permute-start | bytes 393224 | tf_op jit(solution)/shard_map/ppermute | solution.py:304
  44.6 0.7 collective-permute-start.15
  45.3 0.7 collective-permute-start.19
  45.9 1.7 %collective-permute-done.13.refs_4_ = f32[64,768]{1,0:T(8,128)S(1)} collective-permute-done((f32[64,768]{1,0:T(8,128)S(1)}, f32[64,768]{1,0:T(8,128)S(1)}, u32[]{:S(2)}, u32[]{:S(2)}) %collective-permute-start.13) | collective-permute-done | bytes 196640 | tf_op jit(solution)/shard_map/ppermute | solution.py:326
  47.6 1.7 %collective-permute-start.17 = (f32[64,768]{1,0:T(8,128)S(1)}, f32[64,768]{1,0:T(8,128)S(1)}, u32[]{:S(2)}, u32[]{:S(2)}) collective-permute-start(f32[64,768]{1,0:T(8,128)S(1)} %collective-permute-done.13.refs_4_), channel_id=1, source_target_pairs={{2,0},{4,2},{6,4},{7,6},{5,7},{3,5},{1,3},{0,1},{10,8},{12,10},{14... | collective-permute-start | bytes 589832 | tf_op jit(solution)/shard_map/ppermute | solution.py:326
  49.3 1.5 %collective-permute-start.14 = (f32[64,768]{1,0:T(8,128)S(1)}, f32[64,768]{1,0:T(8,128)S(1)}, u32[]{:S(2)}, u32[]{:S(2)}) collective-permute-start(f32[64,768]{1,0:T(8,128)S(1)} %collective-permute-done.12.refs_3_), channel_id=1, source_target_pairs={{0,2},{2,4},{4,6},{6,7},{7,5},{5,3},{3,1},{1,0},{8,10},{10,12},{12... | collective-permute-start | bytes 589832 | tf_op jit(solution)/shard_map/ppermute | solution.py:322
  50.8 5.8 %collective-permute-done.14.refs_5_ = f32[64,768]{1,0:T(8,128)S(1)} collective-permute-done((f32[64,768]{1,0:T(8,128)S(1)}, f32[64,768]{1,0:T(8,128)S(1)}, u32[]{:S(2)}, u32[]{:S(2)}) %collective-permute-start.14) | collective-permute-done | bytes 196640 | tf_op jit(solution)/shard_map/ppermute | solution.py:322
  56.7 0.3 collective-permute-done.17.refs_6_
  57.0 0.6 shard_map.86.refs_13_
  57.6 0.7 collective-permute-start.20
  58.3 0.3 collective-permute-start.18
  58.6 0.7 collective-permute-start.24
  59.3 1.3 %collective-permute-start.23 = (f32[256,256]{1,0:T(8,128)S(1)}, f32[256,256]{1,0:T(8,128)S(1)}, u32[]{:S(2)}, u32[]{:S(2)}) collective-permute-start(f32[256,256]{1,0:T(8,128)S(1)} %shard_map.86.refs_13_), channel_id=1, source_target_pairs={{8,0},{9,1},{10,2},{11,3},{12,4},{13,5},{14,6},{15,7}} | collective-permute-start | bytes 786440 | tf_op jit(solution)/shard_map/ppermute | solution.py:339
  60.6 5.5 %collective-permute-done.18.refs_7_ = f32[64,768]{1,0:T(8,128)S(1)} collective-permute-done((f32[64,768]{1,0:T(8,128)S(1)}, f32[64,768]{1,0:T(8,128)S(1)}, u32[]{:S(2)}, u32[]{:S(2)}) %collective-permute-start.18) | collective-permute-done | bytes 196640 | tf_op jit(solution)/shard_map/ppermute | solution.py:322
  66.0 0.4 collective-permute-start.21
  66.4 0.1 collective-permute-start.22
  66.6 0.8 %collective-permute-done.21.refs_10_ = f32[64,512]{1,0:T(8,128)S(1)} collective-permute-done((f32[64,512]{1,0:T(8,128)S(1)}, f32[64,512]{1,0:T(8,128)S(1)}, u32[]{:S(2)}, u32[]{:S(2)}) %collective-permute-start.21) | collective-permute-done | bytes 131104 | tf_op jit(solution)/shard_map/ppermute | solution.py:239
  67.4 0.4 collective-permute-done.22.refs_11_
  67.8 3.4 %shard_map.87 = f32[512,256]{1,0:T(8,128)} custom-call(s32[8]{0:T(128)S(1)} %compare_select_fusion.2.rank.order, s32[4]{0:T(128)S(1)} %broadcast_xor_fusion.own_order, s32[3]{0:T(128)S(1)} %pad_add_fusion.me, s32[1,512]{1,0:T(1,128)S(1)} %get-tuple-element.27.target, f32[512,256]{1,0:T(8,128)S(1)} %get-tuple-element.30.block, f32[2,256,256]{2,1,0:T(8,128)S(1)} %copy-done.2, ...), custom_call_target="tpu_custom_call" | custom-call | tf_op jit(solution)/shard_map/pallas_call | solution.py:59
  (34 shorter events, 0.2 us)
Async XLA Ops:
  0.0 0.7 copy-start.3
  0.7 1.0 %copy-start = (f32[512,256]{1,0:T(8,128)S(1)}, f32[512,256]{1,0:T(8,128)}, u32[]{:S(2)}) copy-start(f32[512,256]{1,0:T(8,128)} %block.3) | copy-start | bytes 1572868
  3.5 1.7 %collective-permute-start = (f32[256,256]{1,0:T(8,128)S(1)}, f32[256,256]{1,0:T(8,128)S(1)}, u32[]{:S(2)}, u32[]{:S(2)}) collective-permute-start(f32[256,256]{1,0:T(8,128)S(1)} %get-tuple-element.29), channel_id=1, source_target_pairs={{0,8},{8,0},{16,24},{24,16},{1,9},{9,1},{17,25},{25,17},{2,10},{10... | collective-permute-start | bytes 786440 | tf_op jit(solution)/shard_map/ppermute | solution.py:239
  5.3 8.2 %copy-start.1 = (f32[512,256]{1,0:T(8,128)S(1)}, f32[512,256]{1,0:T(8,128)}, u32[]{:S(2)}) copy-start(f32[512,256]{1,0:T(8,128)} %block.3) | copy-start | bytes 1572868
  5.3 6.7 %collective-permute-start.1 = (f32[128,256]{1,0:T(8,128)S(1)}, f32[128,256]{1,0:T(8,128)S(1)}, u32[]{:S(2)}, u32[]{:S(2)}) collective-permute-start(f32[128,256]{1,0:T(8,128)S(1)} %slice_select_fusion.1), channel_id=1, source_target_pairs={{0,16},{8,24},{16,0},{24,8},{1,17},{9,25},{17,1},{25,9},{2,18},{10... | collective-permute-start | bytes 393224 | tf_op jit(solution)/shard_map/ppermute | solution.py:239
  12.1 20.9 %copy-start.2 = (f32[2,256,256]{2,1,0:T(8,128)S(1)}, f32[2,256,256]{2,1,0:T(8,128)}, u32[]{:S(2)}) copy-start(f32[2,256,256]{2,1,0:T(8,128)} %inverses.3) | copy-start | bytes 1572868
  12.1 1.4 %collective-permute-start.2 = (f32[128,256]{1,0:T(8,128)S(1)}, f32[128,256]{1,0:T(8,128)S(1)}, u32[]{:S(2)}, u32[]{:S(2)}) collective-permute-start(f32[128,256]{1,0:T(8,128)S(1)} %get-tuple-element.49.mine), channel_id=1, source_target_pairs={{0,8},{8,0},{16,24},{24,16},{1,9},{9,1},{17,25},{25,17},{2,10},{10... | collective-permute-start | bytes 393224 | tf_op jit(solution)/shard_map/ppermute | solution.py:239
  14.6 7.6 %collective-permute-start.3 = (f32[64,256]{1,0:T(8,128)S(1)}, f32[64,256]{1,0:T(8,128)S(1)}, u32[]{:S(2)}, u32[]{:S(2)}) collective-permute-start(f32[64,256]{1,0:T(8,128)S(1)} %get-tuple-element.33), channel_id=1, source_target_pairs={{0,1},{1,0},{2,3},{3,2},{4,5},{5,4},{6,7},{7,6},{8,9},{9,8},{10,11... | collective-permute-start | bytes 196616 | tf_op jit(solution)/shard_map/ppermute | solution.py:285
  16.4 9.5 %collective-permute-start.4 = (f32[64,256]{1,0:T(8,128)S(1)}, f32[64,256]{1,0:T(8,128)S(1)}, u32[]{:S(2)}, u32[]{:S(2)}) collective-permute-start(f32[64,256]{1,0:T(8,128)S(1)} %get-tuple-element.34), channel_id=1, source_target_pairs={{0,2},{1,3},{2,0},{3,1},{4,6},{5,7},{6,4},{7,5},{8,10},{9,11},{10,... | collective-permute-start | bytes 196616 | tf_op jit(solution)/shard_map/ppermute | solution.py:285
  18.0 7.9 %collective-permute-start.5 = (f32[64,256]{1,0:T(8,128)S(1)}, f32[64,256]{1,0:T(8,128)S(1)}, u32[]{:S(2)}, u32[]{:S(2)}) collective-permute-start(f32[64,256]{1,0:T(8,128)S(1)} %get-tuple-element.35), channel_id=1, source_target_pairs={{0,3},{1,2},{2,1},{3,0},{4,7},{5,6},{6,5},{7,4},{8,11},{9,10},{10,... | collective-permute-start | bytes 196616 | tf_op jit(solution)/shard_map/ppermute | solution.py:285
  18.2 7.7 %collective-permute-start.6 = (f32[64,256]{1,0:T(8,128)S(1)}, f32[64,256]{1,0:T(8,128)S(1)}, u32[]{:S(2)}, u32[]{:S(2)}) collective-permute-start(f32[64,256]{1,0:T(8,128)S(1)} %get-tuple-element.36), channel_id=1, source_target_pairs={{0,4},{1,5},{2,6},{3,7},{4,0},{5,1},{6,2},{7,3},{8,12},{9,13},{10,... | collective-permute-start | bytes 196616 | tf_op jit(solution)/shard_map/ppermute | solution.py:285
  21.0 10.5 %collective-permute-start.7 = (f32[64,256]{1,0:T(8,128)S(1)}, f32[64,256]{1,0:T(8,128)S(1)}, u32[]{:S(2)}, u32[]{:S(2)}) collective-permute-start(f32[64,256]{1,0:T(8,128)S(1)} %get-tuple-element.37), channel_id=1, source_target_pairs={{0,5},{1,4},{2,7},{3,6},{4,1},{5,0},{6,3},{7,2},{8,13},{9,12},{10,... | collective-permute-start | bytes 196616 | tf_op jit(solution)/shard_map/ppermute | solution.py:285
  22.3 9.2 %collective-permute-start.8 = (f32[64,256]{1,0:T(8,128)S(1)}, f32[64,256]{1,0:T(8,128)S(1)}, u32[]{:S(2)}, u32[]{:S(2)}) collective-permute-start(f32[64,256]{1,0:T(8,128)S(1)} %get-tuple-element.38), channel_id=1, source_target_pairs={{0,6},{1,7},{2,4},{3,5},{4,2},{5,3},{6,0},{7,1},{8,14},{9,15},{10,... | collective-permute-start | bytes 196616 | tf_op jit(solution)/shard_map/ppermute | solution.py:285
  25.9 7.1 %collective-permute-start.9 = (f32[64,256]{1,0:T(8,128)S(1)}, f32[64,256]{1,0:T(8,128)S(1)}, u32[]{:S(2)}, u32[]{:S(2)}) collective-permute-start(f32[64,256]{1,0:T(8,128)S(1)} %get-tuple-element.39), channel_id=1, source_target_pairs={{0,7},{1,6},{2,5},{3,4},{4,3},{5,2},{6,1},{7,0},{8,15},{9,14},{10,... | collective-permute-start | bytes 196616 | tf_op jit(solution)/shard_map/ppermute | solution.py:285
  34.4 6.5 %collective-permute-start.11 = (f32[64,768]{1,0:T(8,128)S(1)}, f32[64,768]{1,0:T(8,128)S(1)}, u32[]{:S(2)}, u32[]{:S(2)}) collective-permute-start(f32[64,768]{1,0:T(8,128)S(1)} %get-tuple-element.40.refs_0_), channel_id=1, source_target_pairs={{2,0},{4,2},{6,4},{7,6},{5,7},{3,5},{1,3},{0,1},{10,8},{12,10},{14... | collective-permute-start | bytes 589832 | tf_op jit(solution)/shard_map/ppermute | solution.py:326
  35.0 6.7 %collective-permute-start.10 = (f32[64,768]{1,0:T(8,128)S(1)}, f32[64,768]{1,0:T(8,128)S(1)}, u32[]{:S(2)}, u32[]{:S(2)}) collective-permute-start(f32[64,768]{1,0:T(8,128)S(1)} %get-tuple-element.40.refs_0_), channel_id=1, source_target_pairs={{0,2},{2,4},{4,6},{6,7},{7,5},{5,3},{3,1},{1,0},{8,10},{10,12},{12... | collective-permute-start | bytes 589832 | tf_op jit(solution)/shard_map/ppermute | solution.py:322
  41.0 6.6 %collective-permute-start.13 = (f32[64,768]{1,0:T(8,128)S(1)}, f32[64,768]{1,0:T(8,128)S(1)}, u32[]{:S(2)}, u32[]{:S(2)}) collective-permute-start(f32[64,768]{1,0:T(8,128)S(1)} %collective-permute-done.11.refs_2_), channel_id=1, source_target_pairs={{2,0},{4,2},{6,4},{7,6},{5,7},{3,5},{1,3},{0,1},{10,8},{12,10},{14... | collective-permute-start | bytes 589832 | tf_op jit(solution)/shard_map/ppermute | solution.py:326
  41.7 7.6 %collective-permute-start.12 = (f32[64,768]{1,0:T(8,128)S(1)}, f32[64,768]{1,0:T(8,128)S(1)}, u32[]{:S(2)}, u32[]{:S(2)}) collective-permute-start(f32[64,768]{1,0:T(8,128)S(1)} %collective-permute-done.10.refs_1_), channel_id=1, source_target_pairs={{0,2},{2,4},{4,6},{6,7},{7,5},{5,3},{3,1},{1,0},{8,10},{10,12},{12... | collective-permute-start | bytes 589832 | tf_op jit(solution)/shard_map/ppermute | solution.py:322
  43.0 7.8 %copy-start.8 = (s32[8]{0:T(128)S(1)}, s32[8]{0:T(128)}, u32[]{:S(2)}) copy-start(s32[8]{0:T(128)} %constant.63.clone) | copy-start | bytes 100
  43.0 7.8 %collective-permute-start.16 = (f32[64,512]{1,0:T(8,128)S(1)}, f32[64,512]{1,0:T(8,128)S(1)}, u32[]{:S(2)}, u32[]{:S(2)}) collective-permute-start(f32[64,512]{1,0:T(8,128)S(1)} %get-tuple-element.41), channel_id=1, source_target_pairs={{0,16},{1,24},{2,0},{3,8},{8,17},{9,25},{10,1},{11,9},{16,18},{17,... | collective-permute-start | bytes 393224 | tf_op jit(solution)/shard_map/ppermute | solution.py:304
  44.6 6.2 %collective-permute-start.15 = (f32[64,512]{1,0:T(8,128)S(1)}, f32[64,512]{1,0:T(8,128)S(1)}, u32[]{:S(2)}, u32[]{:S(2)}) collective-permute-start(f32[64,512]{1,0:T(8,128)S(1)} %get-tuple-element.41), channel_id=1, source_target_pairs={{0,0},{1,8},{2,16},{3,24},{8,1},{9,9},{10,17},{11,25},{16,2},{17,1... | collective-permute-start | bytes 393224 | tf_op jit(solution)/shard_map/ppermute | solution.py:304
  45.3 11.4 %collective-permute-start.19 = (f32[64,256]{1,0:T(8,128)S(1)}, f32[64,256]{1,0:T(8,128)S(1)}, u32[]{:S(2)}, u32[]{:S(2)}) collective-permute-start(f32[64,256]{1,0:T(8,128)S(1)} %slice.13), channel_id=1, source_target_pairs={{8,15},{9,14},{10,13},{11,12}} | collective-permute-start | bytes 196616 | tf_op jit(solution)/shard_map/ppermute | solution.py:337
  47.6 9.4 %collective-permute-start.17 = (f32[64,768]{1,0:T(8,128)S(1)}, f32[64,768]{1,0:T(8,128)S(1)}, u32[]{:S(2)}, u32[]{:S(2)}) collective-permute-start(f32[64,768]{1,0:T(8,128)S(1)} %collective-permute-done.13.refs_4_), channel_id=1, source_target_pairs={{2,0},{4,2},{6,4},{7,6},{5,7},{3,5},{1,3},{0,1},{10,8},{12,10},{14... | collective-permute-start | bytes 589832 | tf_op jit(solution)/shard_map/ppermute | solution.py:326
  49.3 7.4 %collective-permute-start.14 = (f32[64,768]{1,0:T(8,128)S(1)}, f32[64,768]{1,0:T(8,128)S(1)}, u32[]{:S(2)}, u32[]{:S(2)}) collective-permute-start(f32[64,768]{1,0:T(8,128)S(1)} %collective-permute-done.12.refs_3_), channel_id=1, source_target_pairs={{0,2},{2,4},{4,6},{6,7},{7,5},{5,3},{3,1},{1,0},{8,10},{10,12},{12... | collective-permute-start | bytes 589832 | tf_op jit(solution)/shard_map/ppermute | solution.py:322
  50.8 15.7 %copy-start.7 = (s32[4]{0:T(128)S(1)}, s32[4]{0:T(128)}, u32[]{:S(2)}) copy-start(s32[4]{0:T(128)} %constant.64.clone) | copy-start | bytes 52
  57.0 10.8 %copy-start.5 = (f32[2,256]{1,0:T(2,128)S(1)}, f32[2,256]{1,0:T(2,128)}, u32[]{:S(2)}) copy-start(f32[2,256]{1,0:T(2,128)} %couplings.1) | copy-start | bytes 6148
  57.0 10.8 %copy-start.6 = (s32[2,256]{1,0:T(2,128)S(1)}, s32[2,256]{1,0:T(2,128)}, u32[]{:S(2)}) copy-start(s32[2,256]{1,0:T(2,128)} %pattern.1) | copy-start | bytes 6148
  57.6 10.2 %copy-start.4 = (f32[2,256]{1,0:T(2,128)S(1)}, f32[2,256]{1,0:T(2,128)}, u32[]{:S(2)}) copy-start(f32[2,256]{1,0:T(2,128)} %pivots.1) | copy-start | bytes 6148
  57.6 8.4 %collective-permute-start.20 = (f32[256,256]{1,0:T(8,128)S(1)}, f32[256,256]{1,0:T(8,128)S(1)}, u32[]{:S(2)}, u32[]{:S(2)}) collective-permute-start(f32[256,256]{1,0:T(8,128)S(1)} %shard_map.86.refs_13_), channel_id=1, source_target_pairs={{8,24},{9,25},{10,26},{11,27},{12,28},{13,29},{14,30},{15,31}} | collective-permute-start | bytes 786440 | tf_op jit(solution)/shard_map/ppermute | solution.py:339
  58.3 7.7 %collective-permute-start.18 = (f32[64,768]{1,0:T(8,128)S(1)}, f32[64,768]{1,0:T(8,128)S(1)}, u32[]{:S(2)}, u32[]{:S(2)}) collective-permute-start(f32[64,768]{1,0:T(8,128)S(1)} %collective-permute-done.14.refs_5_), channel_id=1, source_target_pairs={{0,2},{2,4},{4,6},{6,7},{7,5},{5,3},{3,1},{1,0},{8,10},{10,12},{12... | collective-permute-start | bytes 589832 | tf_op jit(solution)/shard_map/ppermute | solution.py:322
  58.6 8.0 %collective-permute-start.24 = (f32[256,256]{1,0:T(8,128)S(1)}, f32[256,256]{1,0:T(8,128)S(1)}, u32[]{:S(2)}, u32[]{:S(2)}) collective-permute-start(f32[256,256]{1,0:T(8,128)S(1)} %shard_map.86.refs_13_), channel_id=1, source_target_pairs={{8,16},{9,17},{10,18},{11,19},{12,20},{13,21},{14,22},{15,23}} | collective-permute-start | bytes 786440 | tf_op jit(solution)/shard_map/ppermute | solution.py:339
  59.3 7.3 %collective-permute-start.23 = (f32[256,256]{1,0:T(8,128)S(1)}, f32[256,256]{1,0:T(8,128)S(1)}, u32[]{:S(2)}, u32[]{:S(2)}) collective-permute-start(f32[256,256]{1,0:T(8,128)S(1)} %shard_map.86.refs_13_), channel_id=1, source_target_pairs={{8,0},{9,1},{10,2},{11,3},{12,4},{13,5},{14,6},{15,7}} | collective-permute-start | bytes 786440 | tf_op jit(solution)/shard_map/ppermute | solution.py:339
  66.0 1.4 %collective-permute-start.21 = (f32[64,512]{1,0:T(8,128)S(1)}, f32[64,512]{1,0:T(8,128)S(1)}, u32[]{:S(2)}, u32[]{:S(2)}) collective-permute-start(f32[64,512]{1,0:T(8,128)S(1)} %collective-permute-done.15.refs_8_), channel_id=1, source_target_pairs={{0,8},{8,0},{16,24},{24,16},{1,9},{9,1},{17,25},{25,17},{2,10},{10... | collective-permute-start | bytes 393224 | tf_op jit(solution)/shard_map/ppermute | solution.py:239
  66.4 1.3 %collective-permute-start.22 = (f32[64,512]{1,0:T(8,128)S(1)}, f32[64,512]{1,0:T(8,128)S(1)}, u32[]{:S(2)}, u32[]{:S(2)}) collective-permute-start(f32[64,512]{1,0:T(8,128)S(1)} %collective-permute-done.16.refs_9_), channel_id=1, source_target_pairs={{0,8},{8,0},{16,24},{24,16},{1,9},{9,1},{17,25},{25,17},{2,10},{10... | collective-permute-start | bytes 393224 | tf_op jit(solution)/shard_map/ppermute | solution.py:239

commit v5 on v4

--- a/solution.py
+++ b/solution.py
@@ -101,7 +101,8 @@
     send[...] = jnp.where(odd, rows[:half], rows[half:])
 
 
-def index_vectors(swaps, target, source):
+def index_vectors(swaps, inverses, target, source, high, low):
+    high[...], low[...] = split(inverses[...])
     (lead0, partner0, lead1, partner1), (lead0_up, partner0_up, lead1_up, partner1_up) = swap_lists(swaps)
     hit = jnp.logical_or(lead1_up == partner0, partner1_up == partner0)
     again = jnp.max(jnp.where(hit, 1, 0), axis=0, keepdims=True) > 0
@@ -134,23 +135,37 @@
         ref[...] = out[pl.ds(pl.multiple_of(aims_col[i] * piece, piece), piece), :]
 
 
-def pick_columns(lead_tiles, me, tiles, source, inverses, *refs):
-    *pieces, out, panel_out = refs
-    piece, tile = pieces[0].shape
-    lead = lead_tiles * tile
+def picked(tiles, source, pieces):
+    tile = pieces[0].shape[1]
     wanted = source[...]
     index = lax.broadcasted_iota(jnp.int32, (tile, 1), 0)
     total = 0.0
     for i, ref in enumerate(pieces):
         block = jnp.concatenate(split(ref[...]), axis=0)
         total = total + jnp.dot(block, ones_where(index + tiles[i] * tile == wanted), preferred_element_type=f32)
+    return total
+
+
+def pick_first(tiles, source, *refs):
+    *pieces, out = refs
+    out[...] = picked(tiles, source, pieces)
+
+
+def pick_columns(lead_tiles, me, tiles, source, high, low, so_far, *refs):
+    *pieces, out, panel_out = refs
+    piece, tile = pieces[0].shape
+    lead = lead_tiles * tile
+    total = so_far[...] + picked(tiles, source, pieces)
     total = total[:piece] + total[piece:]
     in_first_tile = me[1] < tile // piece
     for panel in range(lead_tiles):
         place = slice(panel * tile, (panel + 1) * tile)
         plain = jnp.logical_and(me[0] == panel, in_first_tile)
         part = total[:, place]
-        part = jnp.where(plain, part, mm(part, inverses[panel]))
+        parts = split(part)
+        both = jnp.dot(jnp.concatenate(parts, axis=0), high[panel], preferred_element_type=f32)
+        product = both[:piece] + (both[piece:] + jnp.dot(parts[0], low[panel], preferred_element_type=f32))
+        part = jnp.where(plain, part, product)
         out[:, place] = part
         panel_out[:, place] = part
     out[:, lead:] = total[:, lead:]
@@ -248,8 +263,11 @@
         kkt,
         smem=1,
     )
-    target, source = call(
-        index_vectors, [((1, 2 * half), jnp.int32), ((1, lead + half), jnp.int32)], lists
+    target, source, high, low = call(
+        index_vectors,
+        [((1, 2 * half), jnp.int32), ((1, lead + half), jnp.int32)] + [(inverses.shape, bf16)] * 2,
+        lists,
+        inverses,
     )
     mine = keep + flip(send, 1)
     if rows_axis == 4:
@@ -286,14 +304,20 @@
     else:
         whole = lax.all_to_all(block, "col", 0, 0, tiled=True)
         pieces = [whole[i * piece : (i + 1) * piece] for i in range(cols_axis)]
+    near = cols_axis // 2 + 1
+    (so_far,) = call(
+        pick_first, [(2 * piece, lead + half)], tiles[:near], source, *pieces[:near], smem=1
+    )
     part, panel_part = call(
         functools.partial(pick_columns, panels),
         [(piece, lead + half), (piece, lead)],
         me,
-        tiles,
+        tiles[near:],
         source,
-        inverses,
-        *pieces,
+        high,
+        low,
+        so_far,
+        *pieces[near:],
         smem=2,
     )
     ring = list(range(0, cols_axis, 2)) + list(range(cols_axis - 1, 0, -2))
@@ -337,8 +361,9 @@
     extra = lax.ppermute(panel_part[:, :tile], ("row", "col"), pairs)
     (corner,) = call(collect, [(tile, tile)], order, *parts[:-1], extra, smem=1)
     corners = [corner if r == 1 else lax.ppermute(corner, "row", [(1, r)]) for r in range(rows_axis)]
-    parts[-1], corners[3], near_parts = lax.optimization_barrier((parts[-1], corners[3], near_parts))
-    own_parts = near_parts + [flip(near_part, 1) for near_part in near_parts]
+    free = [flip(near_part, 1) for near_part in near_parts[:-1]]
+    parts[-1], corners[3], tied = lax.optimization_barrier((parts[-1], corners[3], near_parts[-1]))
+    own_parts = near_parts + free + [flip(tied, 1)]
     (out,) = call(
         functools.partial(finish, rows_axis),
         [(height, tile)],

time: 71.4 us -> 70.6 us (0.989)
  waiting for transfers between devices: 32.4 us -> 26.6 us
  starting transfers between devices: 28 us -> 32.2 us
    ppermute x4, waiting for transfers between devices: 11.8 us -> 7.43 us  [shards(): right = lax.ppermute(right, 'col', after)]
    ppermute x5, starting transfers between devices: 4.05 us -> 8.23 us  [flip(): return lax.ppermute(value, 'row', [(i, i ^ bit) for i in range(rows_axis)])]
    ppermute x7, waiting for transfers between devices: 7.02 us -> 5.96 us  [shards(): lax.ppermute(pieces[i], 'col', [(c, c ^ i) for c in range(cols_axis)])]
    pallas_call x6 -> x7, Pallas kernels: 8.71 us -> 9.39 us  [call(): pl.pallas_call(body, out_shape=[jax.ShapeDtypeStruct(*out) if isinstance(...]
  transfers between devices with their start and end apart: 25 -> 25, of which waited for: 13 -> 12; matrix products, arithmetic and copies ran while one was open for 0% -> 0% of each run, Pallas kernels for 0% -> 2%
where the time goes in v5:
time: 70.6 us; the launch traced here: 70.3 us
  starting transfers between devices  32.2 us (46%)
  waiting for transfers between devices  26.6 us (38%)
  Pallas kernels  9.39 us (13%)
  local copies, waits for them, and re-layouts  1.76 us (2%)
    ppermute x7, starting transfers between devices, shards(): lax.ppermute(pieces[i], 'col', [(c, c ^ i) for c in range(cols_axis)])  11.3 us
    pallas_call x7, Pallas kernels, call(): pl.pallas_call(body, out_shape=[jax.ShapeDtypeStruct(*out) if isinstance(...  9.39 us
    ppermute x5, starting transfers between devices, flip(): return lax.ppermute(value, 'row', [(i, i ^ bit) for i in range(rows_axis)])  8.23 us
    ppermute x4, waiting for transfers between devices, shards(): right = lax.ppermute(right, 'col', after)  7.43 us
    ppermute x5, waiting for transfers between devices, flip(): return lax.ppermute(value, 'row', [(i, i ^ bit) for i in range(rows_axis)])  6.8 us
    ppermute x3, waiting for transfers between devices, shards(): left = lax.ppermute(left, 'col', before)  6.41 us
    ppermute x7, waiting for transfers between devices, shards(): lax.ppermute(pieces[i], 'col', [(c, c ^ i) for c in range(cols_axis)])  5.96 us
    ppermute x4, starting transfers between devices, shards(): right = lax.ppermute(right, 'col', after)  4.57 us
  transfers between devices with their start and end apart: 25, of which 12 were waited for; matrix products, arithmetic and copies ran while one was open for 0% of the time, Pallas kernels for 2%

profile of v5, /device:TPU:0, one launch (start us, length us, event | category | flops | bytes accessed | tf_op | source)
XLA Modules:
  0.0 70.3 jit_solution(10737618333533988539)
XLA Ops:
  0.0 0.1 pad_add_fusion.me
  0.1 0.6 copy-done.3
  0.7 1.0 %copy-done = f32[512,256]{1,0:T(8,128)S(1)} copy-done((f32[512,256]{1,0:T(8,128)S(1)}, f32[512,256]{1,0:T(8,128)}, u32[]{:S(2)}) %copy-start) | copy-done | bytes 524312
  1.7 1.8 %shard_map.83 = (f32[256,256]{1,0:T(8,128)S(1)}, f32[256,256]{1,0:T(8,128)S(1)}) custom-call(s32[3]{0:T(128)S(1)} %pad_add_fusion.me, s32[4,128]{1,0:T(4,128)S(1)} %bitcast.5, f32[512,256]{1,0:T(8,128)S(1)} %copy-done), custom_call_target="tpu_custom_call" | custom-call | tf_op jit(solution)/shard_map/pallas_call | solution.py:59
  3.5 0.5 collective-permute-start
  4.1 1.2 %collective-permute-done = f32[256,256]{1,0:T(8,128)S(1)} collective-permute-done((f32[256,256]{1,0:T(8,128)S(1)}, f32[256,256]{1,0:T(8,128)S(1)}, u32[]{:S(2)}, u32[]{:S(2)}) %collective-permute-start) | collective-permute-done | bytes 262176 | tf_op jit(solution)/shard_map/ppermute | solution.py:254
  5.3 2.9 %collective-permute-start.1 = (f32[128,256]{1,0:T(8,128)S(1)}, f32[128,256]{1,0:T(8,128)S(1)}, u32[]{:S(2)}, u32[]{:S(2)}) collective-permute-start(f32[128,256]{1,0:T(8,128)S(1)} %slice_select_fusion.1), channel_id=1, source_target_pairs={{0,16},{8,24},{16,0},{24,8},{1,17},{9,25},{17,1},{25,9},{2,18},{10... | collective-permute-start | bytes 393224 | tf_op jit(solution)/shard_map/ppermute | solution.py:254
  8.3 3.8 %collective-permute-done.1 = f32[128,256]{1,0:T(8,128)S(1)} collective-permute-done((f32[128,256]{1,0:T(8,128)S(1)}, f32[128,256]{1,0:T(8,128)S(1)}, u32[]{:S(2)}, u32[]{:S(2)}) %collective-permute-start.1) | collective-permute-done | bytes 131104 | tf_op jit(solution)/shard_map/ppermute | solution.py:254
  12.1 0.1 collective-permute-start.2
  12.2 0.4 shard_map.82
  12.6 0.9 %collective-permute-done.2.other = f32[128,256]{1,0:T(8,128)S(1)} collective-permute-done((f32[128,256]{1,0:T(8,128)S(1)}, f32[128,256]{1,0:T(8,128)S(1)}, u32[]{:S(2)}, u32[]{:S(2)}) %collective-permute-start.2) | collective-permute-done | bytes 131104 | tf_op jit(solution)/shard_map/ppermute | solution.py:254
  13.5 1.1 %shard_map.84 = (f32[512,256]{1,0:T(8,128)S(1)}, f32[64,256]{1,0:T(8,128)S(1)}, f32[64,256]{1,0:T(8,128)S(1)}, f32[64,256]{1,0:T(8,128)S(1)}, f32[64,256]{1,0:T(...) custom-call(s32[3]{0:T(128)S(1)} %pad_add_fusion.me, ...), custom_call_target="tpu_custom_call" | custom-call | tf_op jit(solution)/shard_map/pallas_call | solution.py:59
  14.6 1.8 %collective-permute-start.3 = (f32[64,256]{1,0:T(8,128)S(1)}, f32[64,256]{1,0:T(8,128)S(1)}, u32[]{:S(2)}, u32[]{:S(2)}) collective-permute-start(f32[64,256]{1,0:T(8,128)S(1)} %get-tuple-element.36), channel_id=1, source_target_pairs={{0,1},{1,0},{2,3},{3,2},{4,5},{5,4},{6,7},{7,6},{8,9},{9,8},{10,11... | collective-permute-start | bytes 196616 | tf_op jit(solution)/shard_map/ppermute | solution.py:303
  16.4 1.6 %collective-permute-start.4 = (f32[64,256]{1,0:T(8,128)S(1)}, f32[64,256]{1,0:T(8,128)S(1)}, u32[]{:S(2)}, u32[]{:S(2)}) collective-permute-start(f32[64,256]{1,0:T(8,128)S(1)} %get-tuple-element.37), channel_id=1, source_target_pairs={{0,2},{1,3},{2,0},{3,1},{4,6},{5,7},{6,4},{7,5},{8,10},{9,11},{10,... | collective-permute-start | bytes 196616 | tf_op jit(solution)/shard_map/ppermute | solution.py:303
  18.0 0.2 collective-permute-start.5
  18.2 2.8 %collective-permute-start.6 = (f32[64,256]{1,0:T(8,128)S(1)}, f32[64,256]{1,0:T(8,128)S(1)}, u32[]{:S(2)}, u32[]{:S(2)}) collective-permute-start(f32[64,256]{1,0:T(8,128)S(1)} %get-tuple-element.39), channel_id=1, source_target_pairs={{0,4},{1,5},{2,6},{3,7},{4,0},{5,1},{6,2},{7,3},{8,12},{9,13},{10,... | collective-permute-start | bytes 196616 | tf_op jit(solution)/shard_map/ppermute | solution.py:303
  21.0 1.3 %collective-permute-start.7 = (f32[64,256]{1,0:T(8,128)S(1)}, f32[64,256]{1,0:T(8,128)S(1)}, u32[]{:S(2)}, u32[]{:S(2)}) collective-permute-start(f32[64,256]{1,0:T(8,128)S(1)} %get-tuple-element.40), channel_id=1, source_target_pairs={{0,5},{1,4},{2,7},{3,6},{4,1},{5,0},{6,3},{7,2},{8,13},{9,12},{10,... | collective-permute-start | bytes 196616 | tf_op jit(solution)/shard_map/ppermute | solution.py:303
  22.3 3.6 %collective-permute-start.8 = (f32[64,256]{1,0:T(8,128)S(1)}, f32[64,256]{1,0:T(8,128)S(1)}, u32[]{:S(2)}, u32[]{:S(2)}) collective-permute-start(f32[64,256]{1,0:T(8,128)S(1)} %get-tuple-element.41), channel_id=1, source_target_pairs={{0,6},{1,7},{2,4},{3,5},{4,2},{5,3},{6,0},{7,1},{8,14},{9,15},{10,... | collective-permute-start | bytes 196616 | tf_op jit(solution)/shard_map/ppermute | solution.py:303
  25.9 0.0 collective-permute-start.9
  25.9 0.1 slice.19.tiles
  26.0 1.0 %shard_map.85.so_far = f32[128,768]{1,0:T(8,128)S(1)} custom-call(s32[5]{0:T(128)S(1)} %bitcast.7, s32[1,768]{1,0:T(1,128)S(1)} %get-tuple-element.32.source, f32[64,256]{1,0:T(8,128)S(1)} %get-tuple-element.35.refs_0_, f32[64,256]{1,0:T(8,128)S(1)} %collective-permute-done.3.refs_1_, f32[64,256]{1,0:T(8,128)S(1)} %collective-permute-done.4.refs_2_, ...), custom_call_target="tpu_custom_call" | custom-call | tf_op jit(solution)/shard_map/pallas_call | solution.py:59
  27.0 4.5 %collective-permute-done.7.refs_0_ = f32[64,256]{1,0:T(8,128)S(1)} collective-permute-done((f32[64,256]{1,0:T(8,128)S(1)}, f32[64,256]{1,0:T(8,128)S(1)}, u32[]{:S(2)}, u32[]{:S(2)}) %collective-permute-start.7) | collective-permute-done | bytes 65568 | tf_op jit(solution)/shard_map/ppermute | solution.py:303
  31.4 1.5 %collective-permute-done.9.refs_2_ = f32[64,256]{1,0:T(8,128)S(1)} collective-permute-done((f32[64,256]{1,0:T(8,128)S(1)}, f32[64,256]{1,0:T(8,128)S(1)}, u32[]{:S(2)}, u32[]{:S(2)}) %collective-permute-start.9) | collective-permute-done | bytes 65568 | tf_op jit(solution)/shard_map/ppermute | solution.py:303
  32.9 1.1 %shard_map.86 = (f32[64,768]{1,0:T(8,128)S(1)}, f32[64,512]{1,0:T(8,128)S(1)}) custom-call(s32[3]{0:T(128)S(1)} %pad_add_fusion.me, s32[3]{0:T(128)S(1)} %slice.19.tiles, s32[1,768]{1,0:T(1,128)S(1)} %get-tuple-element.32.source, bf16[2,256,256]{2,1,0:T(8,128)(2,1)S(1)} %get-tuple-element.33.high, bf16[2,256,256]{2,1,0:T(8,128)(2,1)S(1)} %get-tuple-element.34.low, ...), custom_call_target="tpu_custom_call" | custom-call | tf_op jit(solution)/shard_map/pallas_call | solution.py:59
  34.0 0.6 collective-permute-start.11
  34.6 1.5 %collective-permute-start.10 = (f32[64,768]{1,0:T(8,128)S(1)}, f32[64,768]{1,0:T(8,128)S(1)}, u32[]{:S(2)}, u32[]{:S(2)}) collective-permute-start(f32[64,768]{1,0:T(8,128)S(1)} %get-tuple-element.43.refs_0_), channel_id=1, source_target_pairs={{0,2},{2,4},{4,6},{6,7},{7,5},{5,3},{3,1},{1,0},{8,10},{10,12},{12... | collective-permute-start | bytes 589832 | tf_op jit(solution)/shard_map/ppermute | solution.py:346
  36.1 4.5 %collective-permute-done.11.refs_2_ = f32[64,768]{1,0:T(8,128)S(1)} collective-permute-done((f32[64,768]{1,0:T(8,128)S(1)}, f32[64,768]{1,0:T(8,128)S(1)}, u32[]{:S(2)}, u32[]{:S(2)}) %collective-permute-start.11) | collective-permute-done | bytes 196640 | tf_op jit(solution)/shard_map/ppermute | solution.py:350
  40.6 0.3 collective-permute-start.13
  40.8 0.5 collective-permute-done.10.refs_1_
  41.3 1.3 %collective-permute-start.12 = (f32[64,768]{1,0:T(8,128)S(1)}, f32[64,768]{1,0:T(8,128)S(1)}, u32[]{:S(2)}, u32[]{:S(2)}) collective-permute-start(f32[64,768]{1,0:T(8,128)S(1)} %collective-permute-done.10.refs_1_), channel_id=1, source_target_pairs={{0,2},{2,4},{4,6},{6,7},{7,5},{5,3},{3,1},{1,0},{8,10},{10,12},{12... | collective-permute-start | bytes 589832 | tf_op jit(solution)/shard_map/ppermute | solution.py:346
  42.6 1.6 %collective-permute-start.16 = (f32[64,512]{1,0:T(8,128)S(1)}, f32[64,512]{1,0:T(8,128)S(1)}, u32[]{:S(2)}, u32[]{:S(2)}) collective-permute-start(f32[64,512]{1,0:T(8,128)S(1)} %get-tuple-element.44), channel_id=1, source_target_pairs={{0,16},{1,24},{2,0},{3,8},{8,17},{9,25},{10,1},{11,9},{16,18},{17,... | collective-permute-start | bytes 393224 | tf_op jit(solution)/shard_map/ppermute | solution.py:328
  44.2 0.7 collective-permute-start.15
  44.8 0.7 collective-permute-start.19
  45.5 1.7 %collective-permute-done.13.refs_4_ = f32[64,768]{1,0:T(8,128)S(1)} collective-permute-done((f32[64,768]{1,0:T(8,128)S(1)}, f32[64,768]{1,0:T(8,128)S(1)}, u32[]{:S(2)}, u32[]{:S(2)}) %collective-permute-start.13) | collective-permute-done | bytes 196640 | tf_op jit(solution)/shard_map/ppermute | solution.py:350
  47.2 1.7 %collective-permute-start.17 = (f32[64,768]{1,0:T(8,128)S(1)}, f32[64,768]{1,0:T(8,128)S(1)}, u32[]{:S(2)}, u32[]{:S(2)}) collective-permute-start(f32[64,768]{1,0:T(8,128)S(1)} %collective-permute-done.13.refs_4_), channel_id=1, source_target_pairs={{2,0},{4,2},{6,4},{7,6},{5,7},{3,5},{1,3},{0,1},{10,8},{12,10},{14... | collective-permute-start | bytes 589832 | tf_op jit(solution)/shard_map/ppermute | solution.py:350
  48.9 1.5 %collective-permute-start.14 = (f32[64,768]{1,0:T(8,128)S(1)}, f32[64,768]{1,0:T(8,128)S(1)}, u32[]{:S(2)}, u32[]{:S(2)}) collective-permute-start(f32[64,768]{1,0:T(8,128)S(1)} %collective-permute-done.12.refs_3_), channel_id=1, source_target_pairs={{0,2},{2,4},{4,6},{6,7},{7,5},{5,3},{3,1},{1,0},{8,10},{10,12},{12... | collective-permute-start | bytes 589832 | tf_op jit(solution)/shard_map/ppermute | solution.py:346
  50.4 5.8 %collective-permute-done.14.refs_5_ = f32[64,768]{1,0:T(8,128)S(1)} collective-permute-done((f32[64,768]{1,0:T(8,128)S(1)}, f32[64,768]{1,0:T(8,128)S(1)}, u32[]{:S(2)}, u32[]{:S(2)}) %collective-permute-start.14) | collective-permute-done | bytes 196640 | tf_op jit(solution)/shard_map/ppermute | solution.py:346
  56.3 0.3 collective-permute-done.17.refs_6_
  56.5 0.6 shard_map.87.refs_13_
  57.2 0.7 collective-permute-start.20
  57.9 0.3 collective-permute-start.18
  58.2 0.7 collective-permute-start.24
  58.8 1.3 %collective-permute-start.23 = (f32[256,256]{1,0:T(8,128)S(1)}, f32[256,256]{1,0:T(8,128)S(1)}, u32[]{:S(2)}, u32[]{:S(2)}) collective-permute-start(f32[256,256]{1,0:T(8,128)S(1)} %shard_map.87.refs_13_), channel_id=1, source_target_pairs={{8,0},{9,1},{10,2},{11,3},{12,4},{13,5},{14,6},{15,7}} | collective-permute-start | bytes 786440 | tf_op jit(solution)/shard_map/ppermute | solution.py:363
  60.1 4.3 %collective-permute-start.21 = (f32[64,512]{1,0:T(8,128)S(1)}, f32[64,512]{1,0:T(8,128)S(1)}, u32[]{:S(2)}, u32[]{:S(2)}) collective-permute-start(f32[64,512]{1,0:T(8,128)S(1)} %collective-permute-done.15.refs_8_), channel_id=1, source_target_pairs={{0,8},{8,0},{16,24},{24,16},{1,9},{9,1},{17,25},{25,17},{2,10},{10... | collective-permute-start | bytes 393224 | tf_op jit(solution)/shard_map/ppermute | solution.py:254
  64.5 1.1 %collective-permute-done.18.refs_7_ = f32[64,768]{1,0:T(8,128)S(1)} collective-permute-done((f32[64,768]{1,0:T(8,128)S(1)}, f32[64,768]{1,0:T(8,128)S(1)}, u32[]{:S(2)}, u32[]{:S(2)}) %collective-permute-start.18) | collective-permute-done | bytes 196640 | tf_op jit(solution)/shard_map/ppermute | solution.py:346
  65.6 0.4 collective-permute-start.22
  66.0 1.0 %collective-permute-done.22.refs_11_ = f32[64,512]{1,0:T(8,128)S(1)} collective-permute-done((f32[64,512]{1,0:T(8,128)S(1)}, f32[64,512]{1,0:T(8,128)S(1)}, u32[]{:S(2)}, u32[]{:S(2)}) %collective-permute-start.22) | collective-permute-done | bytes 131104 | tf_op jit(solution)/shard_map/ppermute | solution.py:254
  67.0 3.3 %shard_map.88 = f32[512,256]{1,0:T(8,128)} custom-call(s32[8]{0:T(128)S(1)} %compare_select_fusion.2.rank.order, s32[4]{0:T(128)S(1)} %broadcast_xor_fusion.own_order, s32[3]{0:T(128)S(1)} %pad_add_fusion.me, s32[1,512]{1,0:T(1,128)S(1)} %get-tuple-element.28.target, f32[512,256]{1,0:T(8,128)S(1)} %get-tuple-element.31.block, f32[2,256,256]{2,1,0:T(8,128)S(1)} %copy-done.2, ...), custom_call_target="tpu_custom_call" | custom-call | tf_op jit(solution)/shard_map/pallas_call | solution.py:59
  (36 shorter events, 0.2 us)
Async XLA Ops:
  0.0 0.7 copy-start.3
  0.7 1.0 %copy-start = (f32[512,256]{1,0:T(8,128)S(1)}, f32[512,256]{1,0:T(8,128)}, u32[]{:S(2)}) copy-start(f32[512,256]{1,0:T(8,128)} %block.3) | copy-start | bytes 1572868
  3.5 1.7 %collective-permute-start = (f32[256,256]{1,0:T(8,128)S(1)}, f32[256,256]{1,0:T(8,128)S(1)}, u32[]{:S(2)}, u32[]{:S(2)}) collective-permute-start(f32[256,256]{1,0:T(8,128)S(1)} %get-tuple-element.30), channel_id=1, source_target_pairs={{0,8},{8,0},{16,24},{24,16},{1,9},{9,1},{17,25},{25,17},{2,10},{10... | collective-permute-start | bytes 786440 | tf_op jit(solution)/shard_map/ppermute | solution.py:254
  5.3 6.9 %copy-start.2 = (f32[2,256,256]{2,1,0:T(8,128)S(1)}, f32[2,256,256]{2,1,0:T(8,128)}, u32[]{:S(2)}) copy-start(f32[2,256,256]{2,1,0:T(8,128)} %inverses.3) | copy-start | bytes 1572868
  5.3 8.2 %copy-start.1 = (f32[512,256]{1,0:T(8,128)S(1)}, f32[512,256]{1,0:T(8,128)}, u32[]{:S(2)}) copy-start(f32[512,256]{1,0:T(8,128)} %block.3) | copy-start | bytes 1572868
  5.3 6.7 %collective-permute-start.1 = (f32[128,256]{1,0:T(8,128)S(1)}, f32[128,256]{1,0:T(8,128)S(1)}, u32[]{:S(2)}, u32[]{:S(2)}) collective-permute-start(f32[128,256]{1,0:T(8,128)S(1)} %slice_select_fusion.1), channel_id=1, source_target_pairs={{0,16},{8,24},{16,0},{24,8},{1,17},{9,25},{17,1},{25,9},{2,18},{10... | collective-permute-start | bytes 393224 | tf_op jit(solution)/shard_map/ppermute | solution.py:254
  12.1 1.4 %collective-permute-start.2 = (f32[128,256]{1,0:T(8,128)S(1)}, f32[128,256]{1,0:T(8,128)S(1)}, u32[]{:S(2)}, u32[]{:S(2)}) collective-permute-start(f32[128,256]{1,0:T(8,128)S(1)} %get-tuple-element.51.mine), channel_id=1, source_target_pairs={{0,8},{8,0},{16,24},{24,16},{1,9},{9,1},{17,25},{25,17},{2,10},{10... | collective-permute-start | bytes 393224 | tf_op jit(solution)/shard_map/ppermute | solution.py:254
  14.6 7.6 %collective-permute-start.3 = (f32[64,256]{1,0:T(8,128)S(1)}, f32[64,256]{1,0:T(8,128)S(1)}, u32[]{:S(2)}, u32[]{:S(2)}) collective-permute-start(f32[64,256]{1,0:T(8,128)S(1)} %get-tuple-element.36), channel_id=1, source_target_pairs={{0,1},{1,0},{2,3},{3,2},{4,5},{5,4},{6,7},{7,6},{8,9},{9,8},{10,11... | collective-permute-start | bytes 196616 | tf_op jit(solution)/shard_map/ppermute | solution.py:303
  16.4 9.5 %collective-permute-start.4 = (f32[64,256]{1,0:T(8,128)S(1)}, f32[64,256]{1,0:T(8,128)S(1)}, u32[]{:S(2)}, u32[]{:S(2)}) collective-permute-start(f32[64,256]{1,0:T(8,128)S(1)} %get-tuple-element.37), channel_id=1, source_target_pairs={{0,2},{1,3},{2,0},{3,1},{4,6},{5,7},{6,4},{7,5},{8,10},{9,11},{10,... | collective-permute-start | bytes 196616 | tf_op jit(solution)/shard_map/ppermute | solution.py:303
  18.0 8.0 %collective-permute-start.5 = (f32[64,256]{1,0:T(8,128)S(1)}, f32[64,256]{1,0:T(8,128)S(1)}, u32[]{:S(2)}, u32[]{:S(2)}) collective-permute-start(f32[64,256]{1,0:T(8,128)S(1)} %get-tuple-element.38), channel_id=1, source_target_pairs={{0,3},{1,2},{2,1},{3,0},{4,7},{5,6},{6,5},{7,4},{8,11},{9,10},{10,... | collective-permute-start | bytes 196616 | tf_op jit(solution)/shard_map/ppermute | solution.py:303
  18.2 7.8 %collective-permute-start.6 = (f32[64,256]{1,0:T(8,128)S(1)}, f32[64,256]{1,0:T(8,128)S(1)}, u32[]{:S(2)}, u32[]{:S(2)}) collective-permute-start(f32[64,256]{1,0:T(8,128)S(1)} %get-tuple-element.39), channel_id=1, source_target_pairs={{0,4},{1,5},{2,6},{3,7},{4,0},{5,1},{6,2},{7,3},{8,12},{9,13},{10,... | collective-permute-start | bytes 196616 | tf_op jit(solution)/shard_map/ppermute | solution.py:303
  21.0 10.5 %collective-permute-start.7 = (f32[64,256]{1,0:T(8,128)S(1)}, f32[64,256]{1,0:T(8,128)S(1)}, u32[]{:S(2)}, u32[]{:S(2)}) collective-permute-start(f32[64,256]{1,0:T(8,128)S(1)} %get-tuple-element.40), channel_id=1, source_target_pairs={{0,5},{1,4},{2,7},{3,6},{4,1},{5,0},{6,3},{7,2},{8,13},{9,12},{10,... | collective-permute-start | bytes 196616 | tf_op jit(solution)/shard_map/ppermute | solution.py:303
  22.3 9.2 %collective-permute-start.8 = (f32[64,256]{1,0:T(8,128)S(1)}, f32[64,256]{1,0:T(8,128)S(1)}, u32[]{:S(2)}, u32[]{:S(2)}) collective-permute-start(f32[64,256]{1,0:T(8,128)S(1)} %get-tuple-element.41), channel_id=1, source_target_pairs={{0,6},{1,7},{2,4},{3,5},{4,2},{5,3},{6,0},{7,1},{8,14},{9,15},{10,... | collective-permute-start | bytes 196616 | tf_op jit(solution)/shard_map/ppermute | solution.py:303
  25.9 7.1 %collective-permute-start.9 = (f32[64,256]{1,0:T(8,128)S(1)}, f32[64,256]{1,0:T(8,128)S(1)}, u32[]{:S(2)}, u32[]{:S(2)}) collective-permute-start(f32[64,256]{1,0:T(8,128)S(1)} %get-tuple-element.42), channel_id=1, source_target_pairs={{0,7},{1,6},{2,5},{3,4},{4,3},{5,2},{6,1},{7,0},{8,15},{9,14},{10,... | collective-permute-start | bytes 196616 | tf_op jit(solution)/shard_map/ppermute | solution.py:303
  34.0 6.5 %collective-permute-start.11 = (f32[64,768]{1,0:T(8,128)S(1)}, f32[64,768]{1,0:T(8,128)S(1)}, u32[]{:S(2)}, u32[]{:S(2)}) collective-permute-start(f32[64,768]{1,0:T(8,128)S(1)} %get-tuple-element.43.refs_0_), channel_id=1, source_target_pairs={{2,0},{4,2},{6,4},{7,6},{5,7},{3,5},{1,3},{0,1},{10,8},{12,10},{14... | collective-permute-start | bytes 589832 | tf_op jit(solution)/shard_map/ppermute | solution.py:350
  34.6 6.7 %collective-permute-start.10 = (f32[64,768]{1,0:T(8,128)S(1)}, f32[64,768]{1,0:T(8,128)S(1)}, u32[]{:S(2)}, u32[]{:S(2)}) collective-permute-start(f32[64,768]{1,0:T(8,128)S(1)} %get-tuple-element.43.refs_0_), channel_id=1, source_target_pairs={{0,2},{2,4},{4,6},{6,7},{7,5},{5,3},{3,1},{1,0},{8,10},{10,12},{12... | collective-permute-start | bytes 589832 | tf_op jit(solution)/shard_map/ppermute | solution.py:346
  40.6 6.6 %collective-permute-start.13 = (f32[64,768]{1,0:T(8,128)S(1)}, f32[64,768]{1,0:T(8,128)S(1)}, u32[]{:S(2)}, u32[]{:S(2)}) collective-permute-start(f32[64,768]{1,0:T(8,128)S(1)} %collective-permute-done.11.refs_2_), channel_id=1, source_target_pairs={{2,0},{4,2},{6,4},{7,6},{5,7},{3,5},{1,3},{0,1},{10,8},{12,10},{14... | collective-permute-start | bytes 589832 | tf_op jit(solution)/shard_map/ppermute | solution.py:350
  41.3 7.6 %collective-permute-start.12 = (f32[64,768]{1,0:T(8,128)S(1)}, f32[64,768]{1,0:T(8,128)S(1)}, u32[]{:S(2)}, u32[]{:S(2)}) collective-permute-start(f32[64,768]{1,0:T(8,128)S(1)} %collective-permute-done.10.refs_1_), channel_id=1, source_target_pairs={{0,2},{2,4},{4,6},{6,7},{7,5},{5,3},{3,1},{1,0},{8,10},{10,12},{12... | collective-permute-start | bytes 589832 | tf_op jit(solution)/shard_map/ppermute | solution.py:346
  42.6 7.8 %copy-start.8 = (s32[8]{0:T(128)S(1)}, s32[8]{0:T(128)}, u32[]{:S(2)}) copy-start(s32[8]{0:T(128)} %constant.63.clone) | copy-start | bytes 100
  42.6 7.8 %collective-permute-start.16 = (f32[64,512]{1,0:T(8,128)S(1)}, f32[64,512]{1,0:T(8,128)S(1)}, u32[]{:S(2)}, u32[]{:S(2)}) collective-permute-start(f32[64,512]{1,0:T(8,128)S(1)} %get-tuple-element.44), channel_id=1, source_target_pairs={{0,16},{1,24},{2,0},{3,8},{8,17},{9,25},{10,1},{11,9},{16,18},{17,... | collective-permute-start | bytes 393224 | tf_op jit(solution)/shard_map/ppermute | solution.py:328
  44.2 6.2 %collective-permute-start.15 = (f32[64,512]{1,0:T(8,128)S(1)}, f32[64,512]{1,0:T(8,128)S(1)}, u32[]{:S(2)}, u32[]{:S(2)}) collective-permute-start(f32[64,512]{1,0:T(8,128)S(1)} %get-tuple-element.44), channel_id=1, source_target_pairs={{0,0},{1,8},{2,16},{3,24},{8,1},{9,9},{10,17},{11,25},{16,2},{17,1... | collective-permute-start | bytes 393224 | tf_op jit(solution)/shard_map/ppermute | solution.py:328
  44.8 11.4 %collective-permute-start.19 = (f32[64,256]{1,0:T(8,128)S(1)}, f32[64,256]{1,0:T(8,128)S(1)}, u32[]{:S(2)}, u32[]{:S(2)}) collective-permute-start(f32[64,256]{1,0:T(8,128)S(1)} %slice.21), channel_id=1, source_target_pairs={{8,15},{9,14},{10,13},{11,12}} | collective-permute-start | bytes 196616 | tf_op jit(solution)/shard_map/ppermute | solution.py:361
  47.2 9.4 %collective-permute-start.17 = (f32[64,768]{1,0:T(8,128)S(1)}, f32[64,768]{1,0:T(8,128)S(1)}, u32[]{:S(2)}, u32[]{:S(2)}) collective-permute-start(f32[64,768]{1,0:T(8,128)S(1)} %collective-permute-done.13.refs_4_), channel_id=1, source_target_pairs={{2,0},{4,2},{6,4},{7,6},{5,7},{3,5},{1,3},{0,1},{10,8},{12,10},{14... | collective-permute-start | bytes 589832 | tf_op jit(solution)/shard_map/ppermute | solution.py:350
  48.9 7.4 %collective-permute-start.14 = (f32[64,768]{1,0:T(8,128)S(1)}, f32[64,768]{1,0:T(8,128)S(1)}, u32[]{:S(2)}, u32[]{:S(2)}) collective-permute-start(f32[64,768]{1,0:T(8,128)S(1)} %collective-permute-done.12.refs_3_), channel_id=1, source_target_pairs={{0,2},{2,4},{4,6},{6,7},{7,5},{5,3},{3,1},{1,0},{8,10},{10,12},{12... | collective-permute-start | bytes 589832 | tf_op jit(solution)/shard_map/ppermute | solution.py:346
  50.4 15.6 %copy-start.7 = (s32[4]{0:T(128)S(1)}, s32[4]{0:T(128)}, u32[]{:S(2)}) copy-start(s32[4]{0:T(128)} %constant.64.clone) | copy-start | bytes 52
  56.5 10.4 %copy-start.5 = (f32[2,256]{1,0:T(2,128)S(1)}, f32[2,256]{1,0:T(2,128)}, u32[]{:S(2)}) copy-start(f32[2,256]{1,0:T(2,128)} %couplings.1) | copy-start | bytes 6148
  56.5 10.4 %copy-start.6 = (s32[2,256]{1,0:T(2,128)S(1)}, s32[2,256]{1,0:T(2,128)}, u32[]{:S(2)}) copy-start(s32[2,256]{1,0:T(2,128)} %pattern.1) | copy-start | bytes 6148
  57.2 9.8 %copy-start.4 = (f32[2,256]{1,0:T(2,128)S(1)}, f32[2,256]{1,0:T(2,128)}, u32[]{:S(2)}) copy-start(f32[2,256]{1,0:T(2,128)} %pivots.1) | copy-start | bytes 6148
  57.2 8.4 %collective-permute-start.20 = (f32[256,256]{1,0:T(8,128)S(1)}, f32[256,256]{1,0:T(8,128)S(1)}, u32[]{:S(2)}, u32[]{:S(2)}) collective-permute-start(f32[256,256]{1,0:T(8,128)S(1)} %shard_map.87.refs_13_), channel_id=1, source_target_pairs={{8,24},{9,25},{10,26},{11,27},{12,28},{13,29},{14,30},{15,31}} | collective-permute-start | bytes 786440 | tf_op jit(solution)/shard_map/ppermute | solution.py:363
  57.9 7.7 %collective-permute-start.18 = (f32[64,768]{1,0:T(8,128)S(1)}, f32[64,768]{1,0:T(8,128)S(1)}, u32[]{:S(2)}, u32[]{:S(2)}) collective-permute-start(f32[64,768]{1,0:T(8,128)S(1)} %collective-permute-done.14.refs_5_), channel_id=1, source_target_pairs={{0,2},{2,4},{4,6},{6,7},{7,5},{5,3},{3,1},{1,0},{8,10},{10,12},{12... | collective-permute-start | bytes 589832 | tf_op jit(solution)/shard_map/ppermute | solution.py:346
  58.2 7.8 %collective-permute-start.24 = (f32[256,256]{1,0:T(8,128)S(1)}, f32[256,256]{1,0:T(8,128)S(1)}, u32[]{:S(2)}, u32[]{:S(2)}) collective-permute-start(f32[256,256]{1,0:T(8,128)S(1)} %shard_map.87.refs_13_), channel_id=1, source_target_pairs={{8,16},{9,17},{10,18},{11,19},{12,20},{13,21},{14,22},{15,23}} | collective-permute-start | bytes 786440 | tf_op jit(solution)/shard_map/ppermute | solution.py:363
  58.8 7.2 %collective-permute-start.23 = (f32[256,256]{1,0:T(8,128)S(1)}, f32[256,256]{1,0:T(8,128)S(1)}, u32[]{:S(2)}, u32[]{:S(2)}) collective-permute-start(f32[256,256]{1,0:T(8,128)S(1)} %shard_map.87.refs_13_), channel_id=1, source_target_pairs={{8,0},{9,1},{10,2},{11,3},{12,4},{13,5},{14,6},{15,7}} | collective-permute-start | bytes 786440 | tf_op jit(solution)/shard_map/ppermute | solution.py:363
  60.1 5.9 %collective-permute-start.21 = (f32[64,512]{1,0:T(8,128)S(1)}, f32[64,512]{1,0:T(8,128)S(1)}, u32[]{:S(2)}, u32[]{:S(2)}) collective-permute-start(f32[64,512]{1,0:T(8,128)S(1)} %collective-permute-done.15.refs_8_), channel_id=1, source_target_pairs={{0,8},{8,0},{16,24},{24,16},{1,9},{9,1},{17,25},{25,17},{2,10},{10... | collective-permute-start | bytes 393224 | tf_op jit(solution)/shard_map/ppermute | solution.py:254
  65.6 1.4 %collective-permute-start.22 = (f32[64,512]{1,0:T(8,128)S(1)}, f32[64,512]{1,0:T(8,128)S(1)}, u32[]{:S(2)}, u32[]{:S(2)}) collective-permute-start(f32[64,512]{1,0:T(8,128)S(1)} %collective-permute-done.16.refs_9_), channel_id=1, source_target_pairs={{0,8},{8,0},{16,24},{24,16},{1,9},{9,1},{17,25},{25,17},{2,10},{10... | collective-permute-start | bytes 393224 | tf_op jit(solution)/shard_map/ppermute | solution.py:254

commit v6 on v5

--- a/solution.py
+++ b/solution.py
@@ -304,7 +304,7 @@
     else:
         whole = lax.all_to_all(block, "col", 0, 0, tiled=True)
         pieces = [whole[i * piece : (i + 1) * piece] for i in range(cols_axis)]
-    near = cols_axis // 2 + 1
+    near = cols_axis // 2 + 2
     (so_far,) = call(
         pick_first, [(2 * piece, lead + half)], tiles[:near], source, *pieces[:near], smem=1
     )
@@ -341,8 +341,8 @@
     last = cols_axis // 2
     for step in range(1, last + 1):
         if step == last:
-            right, near_parts = lax.optimization_barrier((right, near_parts))
-            parts[-2] = right
+            right, left, near_parts = lax.optimization_barrier((right, left, near_parts))
+            parts[-2:] = right, left
         right = lax.ppermute(right, "col", after)
         parts.append(right)
         steps.append(-step)

time: 70.6 us -> 70.4 us (level)
    ppermute x3, waiting for transfers between devices: 6.41 us -> 12.4 us  [shards(): left = lax.ppermute(left, 'col', before)]
    ppermute x4, waiting for transfers between devices: 7.43 us -> 1.63 us  [shards(): right = lax.ppermute(right, 'col', after)]
  transfers between devices with their start and end apart: 25 -> 25, of which waited for: 12 -> 11; matrix products, arithmetic and copies ran while one was open for 0% -> 0% of each run, Pallas kernels for 2% -> 2%
where the time goes in v6:
time: 70.4 us; the launch traced here: 70.2 us
  starting transfers between devices  31.9 us (45%)
  waiting for transfers between devices  26.7 us (38%)
  Pallas kernels  9.36 us (13%)
  local copies, waits for them, and re-layouts  1.76 us (2%)
    ppermute x3, waiting for transfers between devices, shards(): left = lax.ppermute(left, 'col', before)  12.4 us
    ppermute x7, starting transfers between devices, shards(): lax.ppermute(pieces[i], 'col', [(c, c ^ i) for c in range(cols_axis)])  11.3 us
    pallas_call x7, Pallas kernels, call(): pl.pallas_call(body, out_shape=[jax.ShapeDtypeStruct(*out) if isinstance(...  9.36 us
    ppermute x5, starting transfers between devices, flip(): return lax.ppermute(value, 'row', [(i, i ^ bit) for i in range(rows_axis)])  8.17 us
    ppermute x5, waiting for transfers between devices, flip(): return lax.ppermute(value, 'row', [(i, i ^ bit) for i in range(rows_axis)])  6.8 us
    ppermute x7, waiting for transfers between devices, shards(): lax.ppermute(pieces[i], 'col', [(c, c ^ i) for c in range(cols_axis)])  5.86 us
    ppermute x4, starting transfers between devices, shards(): right = lax.ppermute(right, 'col', after)  4.43 us
    ppermute x3, starting transfers between devices, shards(): lax.ppermute(corner, 'row', [(1, r)])  2.63 us
  transfers between devices with their start and end apart: 25, of which 11 were waited for; matrix products, arithmetic and copies ran while one was open for 0% of the time, Pallas kernels for 2%

profile of v6, /device:TPU:0, one launch (start us, length us, event | category | flops | bytes accessed | tf_op | source)
XLA Modules:
  0.0 70.2 jit_solution(31666652791804338)
XLA Ops:
  0.0 0.1 pad_add_fusion.me
  0.1 0.6 copy-done.3
  0.7 1.0 %copy-done = f32[512,256]{1,0:T(8,128)S(1)} copy-done((f32[512,256]{1,0:T(8,128)S(1)}, f32[512,256]{1,0:T(8,128)}, u32[]{:S(2)}) %copy-start) | copy-done | bytes 524312
  1.7 1.8 %shard_map.83 = (f32[256,256]{1,0:T(8,128)S(1)}, f32[256,256]{1,0:T(8,128)S(1)}) custom-call(s32[3]{0:T(128)S(1)} %pad_add_fusion.me, s32[4,128]{1,0:T(4,128)S(1)} %bitcast.5, f32[512,256]{1,0:T(8,128)S(1)} %copy-done), custom_call_target="tpu_custom_call" | custom-call | tf_op jit(solution)/shard_map/pallas_call | solution.py:59
  3.5 0.5 collective-permute-start
  4.1 1.2 %collective-permute-done = f32[256,256]{1,0:T(8,128)S(1)} collective-permute-done((f32[256,256]{1,0:T(8,128)S(1)}, f32[256,256]{1,0:T(8,128)S(1)}, u32[]{:S(2)}, u32[]{:S(2)}) %collective-permute-start) | collective-permute-done | bytes 262176 | tf_op jit(solution)/shard_map/ppermute | solution.py:254
  5.3 0.0 copy-start.2
  5.3 2.9 %collective-permute-start.1 = (f32[128,256]{1,0:T(8,128)S(1)}, f32[128,256]{1,0:T(8,128)S(1)}, u32[]{:S(2)}, u32[]{:S(2)}) collective-permute-start(f32[128,256]{1,0:T(8,128)S(1)} %slice_select_fusion.1), channel_id=1, source_target_pairs={{0,16},{8,24},{16,0},{24,8},{1,17},{9,25},{17,1},{25,9},{2,18},{10... | collective-permute-start | bytes 393224 | tf_op jit(solution)/shard_map/ppermute | solution.py:254
  8.3 3.8 %collective-permute-done.1 = f32[128,256]{1,0:T(8,128)S(1)} collective-permute-done((f32[128,256]{1,0:T(8,128)S(1)}, f32[128,256]{1,0:T(8,128)S(1)}, u32[]{:S(2)}, u32[]{:S(2)}) %collective-permute-start.1) | collective-permute-done | bytes 131104 | tf_op jit(solution)/shard_map/ppermute | solution.py:254
  12.1 0.1 collective-permute-start.2
  12.2 0.4 shard_map.82
  12.6 0.9 %collective-permute-done.2.other = f32[128,256]{1,0:T(8,128)S(1)} collective-permute-done((f32[128,256]{1,0:T(8,128)S(1)}, f32[128,256]{1,0:T(8,128)S(1)}, u32[]{:S(2)}, u32[]{:S(2)}) %collective-permute-start.2) | collective-permute-done | bytes 131104 | tf_op jit(solution)/shard_map/ppermute | solution.py:254
  13.5 1.1 %shard_map.84 = (f32[512,256]{1,0:T(8,128)S(1)}, f32[64,256]{1,0:T(8,128)S(1)}, f32[64,256]{1,0:T(8,128)S(1)}, f32[64,256]{1,0:T(8,128)S(1)}, f32[64,256]{1,0:T(...) custom-call(s32[3]{0:T(128)S(1)} %pad_add_fusion.me, ...), custom_call_target="tpu_custom_call" | custom-call | tf_op jit(solution)/shard_map/pallas_call | solution.py:59
  14.6 1.8 %collective-permute-start.3 = (f32[64,256]{1,0:T(8,128)S(1)}, f32[64,256]{1,0:T(8,128)S(1)}, u32[]{:S(2)}, u32[]{:S(2)}) collective-permute-start(f32[64,256]{1,0:T(8,128)S(1)} %get-tuple-element.37), channel_id=1, source_target_pairs={{0,1},{1,0},{2,3},{3,2},{4,5},{5,4},{6,7},{7,6},{8,9},{9,8},{10,11... | collective-permute-start | bytes 196616 | tf_op jit(solution)/shard_map/ppermute | solution.py:303
  16.4 1.6 %collective-permute-start.4 = (f32[64,256]{1,0:T(8,128)S(1)}, f32[64,256]{1,0:T(8,128)S(1)}, u32[]{:S(2)}, u32[]{:S(2)}) collective-permute-start(f32[64,256]{1,0:T(8,128)S(1)} %get-tuple-element.38), channel_id=1, source_target_pairs={{0,2},{1,3},{2,0},{3,1},{4,6},{5,7},{6,4},{7,5},{8,10},{9,11},{10,... | collective-permute-start | bytes 196616 | tf_op jit(solution)/shard_map/ppermute | solution.py:303
  18.0 0.2 collective-permute-start.5
  18.2 2.8 %collective-permute-start.6 = (f32[64,256]{1,0:T(8,128)S(1)}, f32[64,256]{1,0:T(8,128)S(1)}, u32[]{:S(2)}, u32[]{:S(2)}) collective-permute-start(f32[64,256]{1,0:T(8,128)S(1)} %get-tuple-element.40), channel_id=1, source_target_pairs={{0,4},{1,5},{2,6},{3,7},{4,0},{5,1},{6,2},{7,3},{8,12},{9,13},{10,... | collective-permute-start | bytes 196616 | tf_op jit(solution)/shard_map/ppermute | solution.py:303
  21.0 1.3 %collective-permute-start.7 = (f32[64,256]{1,0:T(8,128)S(1)}, f32[64,256]{1,0:T(8,128)S(1)}, u32[]{:S(2)}, u32[]{:S(2)}) collective-permute-start(f32[64,256]{1,0:T(8,128)S(1)} %get-tuple-element.41), channel_id=1, source_target_pairs={{0,5},{1,4},{2,7},{3,6},{4,1},{5,0},{6,3},{7,2},{8,13},{9,12},{10,... | collective-permute-start | bytes 196616 | tf_op jit(solution)/shard_map/ppermute | solution.py:303
  22.3 3.6 %collective-permute-start.8 = (f32[64,256]{1,0:T(8,128)S(1)}, f32[64,256]{1,0:T(8,128)S(1)}, u32[]{:S(2)}, u32[]{:S(2)}) collective-permute-start(f32[64,256]{1,0:T(8,128)S(1)} %get-tuple-element.42), channel_id=1, source_target_pairs={{0,6},{1,7},{2,4},{3,5},{4,2},{5,3},{6,0},{7,1},{8,14},{9,15},{10,... | collective-permute-start | bytes 196616 | tf_op jit(solution)/shard_map/ppermute | solution.py:303
  25.9 0.0 collective-permute-start.9
  25.9 0.1 slice.19.tiles
  26.0 5.5 %collective-permute-done.7.refs_5_ = f32[64,256]{1,0:T(8,128)S(1)} collective-permute-done((f32[64,256]{1,0:T(8,128)S(1)}, f32[64,256]{1,0:T(8,128)S(1)}, u32[]{:S(2)}, u32[]{:S(2)}) %collective-permute-start.7) | collective-permute-done | bytes 65568 | tf_op jit(solution)/shard_map/ppermute | solution.py:303
  31.4 1.1 %shard_map.85.so_far = f32[128,768]{1,0:T(8,128)S(1)} custom-call(s32[6]{0:T(128)S(1)} %bitcast.7, s32[1,768]{1,0:T(1,128)S(1)} %get-tuple-element.33.source, f32[64,256]{1,0:T(8,128)S(1)} %get-tuple-element.36.refs_0_, f32[64,256]{1,0:T(8,128)S(1)} %collective-permute-done.3.refs_1_, f32[64,256]{1,0:T(8,128)S(1)} %collective-permute-done.4.refs_2_, ...), custom_call_target="tpu_custom_call" | custom-call | tf_op jit(solution)/shard_map/pallas_call | solution.py:59
  32.5 0.4 collective-permute-done.9.refs_1_
  32.9 1.0 %shard_map.86 = (f32[64,768]{1,0:T(8,128)S(1)}, f32[64,512]{1,0:T(8,128)S(1)}) custom-call(s32[3]{0:T(128)S(1)} %pad_add_fusion.me, s32[2]{0:T(128)S(1)} %slice.19.tiles, s32[1,768]{1,0:T(1,128)S(1)} %get-tuple-element.33.source, bf16[2,256,256]{2,1,0:T(8,128)(2,1)S(1)} %get-tuple-element.34.high, bf16[2,256,256]{2,1,0:T(8,128)(2,1)S(1)} %get-tuple-element.35.low, ...), custom_call_target="tpu_custom_call" | custom-call | tf_op jit(solution)/shard_map/pallas_call | solution.py:59
  33.9 0.6 collective-permute-start.11
  34.5 1.5 %collective-permute-start.10 = (f32[64,768]{1,0:T(8,128)S(1)}, f32[64,768]{1,0:T(8,128)S(1)}, u32[]{:S(2)}, u32[]{:S(2)}) collective-permute-start(f32[64,768]{1,0:T(8,128)S(1)} %get-tuple-element.44.refs_0_), channel_id=1, source_target_pairs={{0,2},{2,4},{4,6},{6,7},{7,5},{5,3},{3,1},{1,0},{8,10},{10,12},{12... | collective-permute-start | bytes 589832 | tf_op jit(solution)/shard_map/ppermute | solution.py:346
  36.0 4.5 %collective-permute-done.11.refs_2_ = f32[64,768]{1,0:T(8,128)S(1)} collective-permute-done((f32[64,768]{1,0:T(8,128)S(1)}, f32[64,768]{1,0:T(8,128)S(1)}, u32[]{:S(2)}, u32[]{:S(2)}) %collective-permute-start.11) | collective-permute-done | bytes 196640 | tf_op jit(solution)/shard_map/ppermute | solution.py:350
  40.4 0.3 collective-permute-start.13
  40.7 0.5 collective-permute-done.10.refs_1_
  41.2 1.3 %collective-permute-start.12 = (f32[64,768]{1,0:T(8,128)S(1)}, f32[64,768]{1,0:T(8,128)S(1)}, u32[]{:S(2)}, u32[]{:S(2)}) collective-permute-start(f32[64,768]{1,0:T(8,128)S(1)} %collective-permute-done.10.refs_1_), channel_id=1, source_target_pairs={{0,2},{2,4},{4,6},{6,7},{7,5},{5,3},{3,1},{1,0},{8,10},{10,12},{12... | collective-permute-start | bytes 589832 | tf_op jit(solution)/shard_map/ppermute | solution.py:346
  42.5 1.6 %collective-permute-start.17 = (f32[64,512]{1,0:T(8,128)S(1)}, f32[64,512]{1,0:T(8,128)S(1)}, u32[]{:S(2)}, u32[]{:S(2)}) collective-permute-start(f32[64,512]{1,0:T(8,128)S(1)} %get-tuple-element.45), channel_id=1, source_target_pairs={{0,16},{1,24},{2,0},{3,8},{8,17},{9,25},{10,1},{11,9},{16,18},{17,... | collective-permute-start | bytes 393224 | tf_op jit(solution)/shard_map/ppermute | solution.py:328
  44.1 0.7 collective-permute-start.16
  44.7 0.7 collective-permute-start.19
  45.4 1.7 %collective-permute-done.13.refs_4_ = f32[64,768]{1,0:T(8,128)S(1)} collective-permute-done((f32[64,768]{1,0:T(8,128)S(1)}, f32[64,768]{1,0:T(8,128)S(1)}, u32[]{:S(2)}, u32[]{:S(2)}) %collective-permute-start.13) | collective-permute-done | bytes 196640 | tf_op jit(solution)/shard_map/ppermute | solution.py:350
  47.1 1.7 %collective-permute-start.15 = (f32[64,768]{1,0:T(8,128)S(1)}, f32[64,768]{1,0:T(8,128)S(1)}, u32[]{:S(2)}, u32[]{:S(2)}) collective-permute-start(f32[64,768]{1,0:T(8,128)S(1)} %collective-permute-done.13.refs_4_), channel_id=1, source_target_pairs={{2,0},{4,2},{6,4},{7,6},{5,7},{3,5},{1,3},{0,1},{10,8},{12,10},{14... | collective-permute-start | bytes 589832 | tf_op jit(solution)/shard_map/ppermute | solution.py:350
  48.8 1.5 %collective-permute-start.14 = (f32[64,768]{1,0:T(8,128)S(1)}, f32[64,768]{1,0:T(8,128)S(1)}, u32[]{:S(2)}, u32[]{:S(2)}) collective-permute-start(f32[64,768]{1,0:T(8,128)S(1)} %collective-permute-done.12.refs_3_), channel_id=1, source_target_pairs={{0,2},{2,4},{4,6},{6,7},{7,5},{5,3},{3,1},{1,0},{8,10},{10,12},{12... | collective-permute-start | bytes 589832 | tf_op jit(solution)/shard_map/ppermute | solution.py:346
  50.3 6.3 %collective-permute-done.15.refs_6_ = f32[64,768]{1,0:T(8,128)S(1)} collective-permute-done((f32[64,768]{1,0:T(8,128)S(1)}, f32[64,768]{1,0:T(8,128)S(1)}, u32[]{:S(2)}, u32[]{:S(2)}) %collective-permute-start.15) | collective-permute-done | bytes 196640 | tf_op jit(solution)/shard_map/ppermute | solution.py:350
  56.6 0.6 shard_map.87.refs_13_
  57.3 0.7 collective-permute-start.20
  57.9 0.1 collective-permute-start.18
  58.1 0.7 collective-permute-start.24
  58.8 1.3 %collective-permute-start.23 = (f32[256,256]{1,0:T(8,128)S(1)}, f32[256,256]{1,0:T(8,128)S(1)}, u32[]{:S(2)}, u32[]{:S(2)}) collective-permute-start(f32[256,256]{1,0:T(8,128)S(1)} %shard_map.87.refs_13_), channel_id=1, source_target_pairs={{8,0},{9,1},{10,2},{11,3},{12,4},{13,5},{14,6},{15,7}} | collective-permute-start | bytes 786440 | tf_op jit(solution)/shard_map/ppermute | solution.py:363
  60.1 4.3 %collective-permute-start.21 = (f32[64,512]{1,0:T(8,128)S(1)}, f32[64,512]{1,0:T(8,128)S(1)}, u32[]{:S(2)}, u32[]{:S(2)}) collective-permute-start(f32[64,512]{1,0:T(8,128)S(1)} %collective-permute-done.16.refs_8_), channel_id=1, source_target_pairs={{0,8},{8,0},{16,24},{24,16},{1,9},{9,1},{17,25},{25,17},{2,10},{10... | collective-permute-start | bytes 393224 | tf_op jit(solution)/shard_map/ppermute | solution.py:254
  64.3 1.2 %collective-permute-done.18.refs_7_ = f32[64,768]{1,0:T(8,128)S(1)} collective-permute-done((f32[64,768]{1,0:T(8,128)S(1)}, f32[64,768]{1,0:T(8,128)S(1)}, u32[]{:S(2)}, u32[]{:S(2)}) %collective-permute-start.18) | collective-permute-done | bytes 196640 | tf_op jit(solution)/shard_map/ppermute | solution.py:346
  65.5 0.4 collective-permute-start.22
  65.9 1.0 %collective-permute-done.22.refs_11_ = f32[64,512]{1,0:T(8,128)S(1)} collective-permute-done((f32[64,512]{1,0:T(8,128)S(1)}, f32[64,512]{1,0:T(8,128)S(1)}, u32[]{:S(2)}, u32[]{:S(2)}) %collective-permute-start.22) | collective-permute-done | bytes 131104 | tf_op jit(solution)/shard_map/ppermute | solution.py:254
  66.8 3.4 %shard_map.88 = f32[512,256]{1,0:T(8,128)} custom-call(s32[8]{0:T(128)S(1)} %compare_select_fusion.2.rank.order, s32[4]{0:T(128)S(1)} %broadcast_xor_fusion.own_order, s32[3]{0:T(128)S(1)} %pad_add_fusion.me, s32[1,512]{1,0:T(1,128)S(1)} %get-tuple-element.29.target, f32[512,256]{1,0:T(8,128)S(1)} %get-tuple-element.32.block, f32[2,256,256]{2,1,0:T(8,128)S(1)} %copy-done.2, ...), custom_call_target="tpu_custom_call" | custom-call | tf_op jit(solution)/shard_map/pallas_call | solution.py:59
  (36 shorter events, 0.2 us)
Async XLA Ops:
  0.0 0.7 copy-start.3
  0.7 1.0 %copy-start = (f32[512,256]{1,0:T(8,128)S(1)}, f32[512,256]{1,0:T(8,128)}, u32[]{:S(2)}) copy-start(f32[512,256]{1,0:T(8,128)} %block.3) | copy-start | bytes 1572868
  3.5 1.7 %collective-permute-start = (f32[256,256]{1,0:T(8,128)S(1)}, f32[256,256]{1,0:T(8,128)S(1)}, u32[]{:S(2)}, u32[]{:S(2)}) collective-permute-start(f32[256,256]{1,0:T(8,128)S(1)} %get-tuple-element.31), channel_id=1, source_target_pairs={{0,8},{8,0},{16,24},{24,16},{1,9},{9,1},{17,25},{25,17},{2,10},{10... | collective-permute-start | bytes 786440 | tf_op jit(solution)/shard_map/ppermute | solution.py:254
  5.3 6.9 %copy-start.2 = (f32[2,256,256]{2,1,0:T(8,128)S(1)}, f32[2,256,256]{2,1,0:T(8,128)}, u32[]{:S(2)}) copy-start(f32[2,256,256]{2,1,0:T(8,128)} %inverses.3) | copy-start | bytes 1572868
  5.3 8.2 %copy-start.1 = (f32[512,256]{1,0:T(8,128)S(1)}, f32[512,256]{1,0:T(8,128)}, u32[]{:S(2)}) copy-start(f32[512,256]{1,0:T(8,128)} %block.3) | copy-start | bytes 1572868
  5.3 6.7 %collective-permute-start.1 = (f32[128,256]{1,0:T(8,128)S(1)}, f32[128,256]{1,0:T(8,128)S(1)}, u32[]{:S(2)}, u32[]{:S(2)}) collective-permute-start(f32[128,256]{1,0:T(8,128)S(1)} %slice_select_fusion.1), channel_id=1, source_target_pairs={{0,16},{8,24},{16,0},{24,8},{1,17},{9,25},{17,1},{25,9},{2,18},{10... | collective-permute-start | bytes 393224 | tf_op jit(solution)/shard_map/ppermute | solution.py:254
  12.1 1.4 %collective-permute-start.2 = (f32[128,256]{1,0:T(8,128)S(1)}, f32[128,256]{1,0:T(8,128)S(1)}, u32[]{:S(2)}, u32[]{:S(2)}) collective-permute-start(f32[128,256]{1,0:T(8,128)S(1)} %get-tuple-element.53.mine), channel_id=1, source_target_pairs={{0,8},{8,0},{16,24},{24,16},{1,9},{9,1},{17,25},{25,17},{2,10},{10... | collective-permute-start | bytes 393224 | tf_op jit(solution)/shard_map/ppermute | solution.py:254
  14.6 7.6 %collective-permute-start.3 = (f32[64,256]{1,0:T(8,128)S(1)}, f32[64,256]{1,0:T(8,128)S(1)}, u32[]{:S(2)}, u32[]{:S(2)}) collective-permute-start(f32[64,256]{1,0:T(8,128)S(1)} %get-tuple-element.37), channel_id=1, source_target_pairs={{0,1},{1,0},{2,3},{3,2},{4,5},{5,4},{6,7},{7,6},{8,9},{9,8},{10,11... | collective-permute-start | bytes 196616 | tf_op jit(solution)/shard_map/ppermute | solution.py:303
  16.4 9.5 %collective-permute-start.4 = (f32[64,256]{1,0:T(8,128)S(1)}, f32[64,256]{1,0:T(8,128)S(1)}, u32[]{:S(2)}, u32[]{:S(2)}) collective-permute-start(f32[64,256]{1,0:T(8,128)S(1)} %get-tuple-element.38), channel_id=1, source_target_pairs={{0,2},{1,3},{2,0},{3,1},{4,6},{5,7},{6,4},{7,5},{8,10},{9,11},{10,... | collective-permute-start | bytes 196616 | tf_op jit(solution)/shard_map/ppermute | solution.py:303
  18.0 8.0 %collective-permute-start.5 = (f32[64,256]{1,0:T(8,128)S(1)}, f32[64,256]{1,0:T(8,128)S(1)}, u32[]{:S(2)}, u32[]{:S(2)}) collective-permute-start(f32[64,256]{1,0:T(8,128)S(1)} %get-tuple-element.39), channel_id=1, source_target_pairs={{0,3},{1,2},{2,1},{3,0},{4,7},{5,6},{6,5},{7,4},{8,11},{9,10},{10,... | collective-permute-start | bytes 196616 | tf_op jit(solution)/shard_map/ppermute | solution.py:303
  18.2 7.8 %collective-permute-start.6 = (f32[64,256]{1,0:T(8,128)S(1)}, f32[64,256]{1,0:T(8,128)S(1)}, u32[]{:S(2)}, u32[]{:S(2)}) collective-permute-start(f32[64,256]{1,0:T(8,128)S(1)} %get-tuple-element.40), channel_id=1, source_target_pairs={{0,4},{1,5},{2,6},{3,7},{4,0},{5,1},{6,2},{7,3},{8,12},{9,13},{10,... | collective-permute-start | bytes 196616 | tf_op jit(solution)/shard_map/ppermute | solution.py:303
  21.0 10.5 %collective-permute-start.7 = (f32[64,256]{1,0:T(8,128)S(1)}, f32[64,256]{1,0:T(8,128)S(1)}, u32[]{:S(2)}, u32[]{:S(2)}) collective-permute-start(f32[64,256]{1,0:T(8,128)S(1)} %get-tuple-element.41), channel_id=1, source_target_pairs={{0,5},{1,4},{2,7},{3,6},{4,1},{5,0},{6,3},{7,2},{8,13},{9,12},{10,... | collective-permute-start | bytes 196616 | tf_op jit(solution)/shard_map/ppermute | solution.py:303
  22.3 10.3 %collective-permute-start.8 = (f32[64,256]{1,0:T(8,128)S(1)}, f32[64,256]{1,0:T(8,128)S(1)}, u32[]{:S(2)}, u32[]{:S(2)}) collective-permute-start(f32[64,256]{1,0:T(8,128)S(1)} %get-tuple-element.42), channel_id=1, source_target_pairs={{0,6},{1,7},{2,4},{3,5},{4,2},{5,3},{6,0},{7,1},{8,14},{9,15},{10,... | collective-permute-start | bytes 196616 | tf_op jit(solution)/shard_map/ppermute | solution.py:303
  25.9 7.1 %collective-permute-start.9 = (f32[64,256]{1,0:T(8,128)S(1)}, f32[64,256]{1,0:T(8,128)S(1)}, u32[]{:S(2)}, u32[]{:S(2)}) collective-permute-start(f32[64,256]{1,0:T(8,128)S(1)} %get-tuple-element.43), channel_id=1, source_target_pairs={{0,7},{1,6},{2,5},{3,4},{4,3},{5,2},{6,1},{7,0},{8,15},{9,14},{10,... | collective-permute-start | bytes 196616 | tf_op jit(solution)/shard_map/ppermute | solution.py:303
  33.9 6.5 %collective-permute-start.11 = (f32[64,768]{1,0:T(8,128)S(1)}, f32[64,768]{1,0:T(8,128)S(1)}, u32[]{:S(2)}, u32[]{:S(2)}) collective-permute-start(f32[64,768]{1,0:T(8,128)S(1)} %get-tuple-element.44.refs_0_), channel_id=1, source_target_pairs={{2,0},{4,2},{6,4},{7,6},{5,7},{3,5},{1,3},{0,1},{10,8},{12,10},{14... | collective-permute-start | bytes 589832 | tf_op jit(solution)/shard_map/ppermute | solution.py:350
  34.5 6.7 %collective-permute-start.10 = (f32[64,768]{1,0:T(8,128)S(1)}, f32[64,768]{1,0:T(8,128)S(1)}, u32[]{:S(2)}, u32[]{:S(2)}) collective-permute-start(f32[64,768]{1,0:T(8,128)S(1)} %get-tuple-element.44.refs_0_), channel_id=1, source_target_pairs={{0,2},{2,4},{4,6},{6,7},{7,5},{5,3},{3,1},{1,0},{8,10},{10,12},{12... | collective-permute-start | bytes 589832 | tf_op jit(solution)/shard_map/ppermute | solution.py:346
  40.4 6.6 %collective-permute-start.13 = (f32[64,768]{1,0:T(8,128)S(1)}, f32[64,768]{1,0:T(8,128)S(1)}, u32[]{:S(2)}, u32[]{:S(2)}) collective-permute-start(f32[64,768]{1,0:T(8,128)S(1)} %collective-permute-done.11.refs_2_), channel_id=1, source_target_pairs={{2,0},{4,2},{6,4},{7,6},{5,7},{3,5},{1,3},{0,1},{10,8},{12,10},{14... | collective-permute-start | bytes 589832 | tf_op jit(solution)/shard_map/ppermute | solution.py:350
  41.2 7.6 %collective-permute-start.12 = (f32[64,768]{1,0:T(8,128)S(1)}, f32[64,768]{1,0:T(8,128)S(1)}, u32[]{:S(2)}, u32[]{:S(2)}) collective-permute-start(f32[64,768]{1,0:T(8,128)S(1)} %collective-permute-done.10.refs_1_), channel_id=1, source_target_pairs={{0,2},{2,4},{4,6},{6,7},{7,5},{5,3},{3,1},{1,0},{8,10},{10,12},{12... | collective-permute-start | bytes 589832 | tf_op jit(solution)/shard_map/ppermute | solution.py:346
  42.5 7.8 %copy-start.8 = (s32[8]{0:T(128)S(1)}, s32[8]{0:T(128)}, u32[]{:S(2)}) copy-start(s32[8]{0:T(128)} %constant.63.clone) | copy-start | bytes 100
  42.5 7.8 %collective-permute-start.17 = (f32[64,512]{1,0:T(8,128)S(1)}, f32[64,512]{1,0:T(8,128)S(1)}, u32[]{:S(2)}, u32[]{:S(2)}) collective-permute-start(f32[64,512]{1,0:T(8,128)S(1)} %get-tuple-element.45), channel_id=1, source_target_pairs={{0,16},{1,24},{2,0},{3,8},{8,17},{9,25},{10,1},{11,9},{16,18},{17,... | collective-permute-start | bytes 393224 | tf_op jit(solution)/shard_map/ppermute | solution.py:328
  44.1 6.2 %collective-permute-start.16 = (f32[64,512]{1,0:T(8,128)S(1)}, f32[64,512]{1,0:T(8,128)S(1)}, u32[]{:S(2)}, u32[]{:S(2)}) collective-permute-start(f32[64,512]{1,0:T(8,128)S(1)} %get-tuple-element.45), channel_id=1, source_target_pairs={{0,0},{1,8},{2,16},{3,24},{8,1},{9,9},{10,17},{11,25},{16,2},{17,1... | collective-permute-start | bytes 393224 | tf_op jit(solution)/shard_map/ppermute | solution.py:328
  44.7 11.9 %collective-permute-start.19 = (f32[64,256]{1,0:T(8,128)S(1)}, f32[64,256]{1,0:T(8,128)S(1)}, u32[]{:S(2)}, u32[]{:S(2)}) collective-permute-start(f32[64,256]{1,0:T(8,128)S(1)} %slice.21), channel_id=1, source_target_pairs={{8,15},{9,14},{10,13},{11,12}} | collective-permute-start | bytes 196616 | tf_op jit(solution)/shard_map/ppermute | solution.py:361
  47.1 9.5 %collective-permute-start.15 = (f32[64,768]{1,0:T(8,128)S(1)}, f32[64,768]{1,0:T(8,128)S(1)}, u32[]{:S(2)}, u32[]{:S(2)}) collective-permute-start(f32[64,768]{1,0:T(8,128)S(1)} %collective-permute-done.13.refs_4_), channel_id=1, source_target_pairs={{2,0},{4,2},{6,4},{7,6},{5,7},{3,5},{1,3},{0,1},{10,8},{12,10},{14... | collective-permute-start | bytes 589832 | tf_op jit(solution)/shard_map/ppermute | solution.py:350
  48.8 7.8 %collective-permute-start.14 = (f32[64,768]{1,0:T(8,128)S(1)}, f32[64,768]{1,0:T(8,128)S(1)}, u32[]{:S(2)}, u32[]{:S(2)}) collective-permute-start(f32[64,768]{1,0:T(8,128)S(1)} %collective-permute-done.12.refs_3_), channel_id=1, source_target_pairs={{0,2},{2,4},{4,6},{6,7},{7,5},{5,3},{3,1},{1,0},{8,10},{10,12},{12... | collective-permute-start | bytes 589832 | tf_op jit(solution)/shard_map/ppermute | solution.py:346
  50.3 15.6 %copy-start.7 = (s32[4]{0:T(128)S(1)}, s32[4]{0:T(128)}, u32[]{:S(2)}) copy-start(s32[4]{0:T(128)} %constant.64.clone) | copy-start | bytes 52
  56.6 10.3 %copy-start.5 = (f32[2,256]{1,0:T(2,128)S(1)}, f32[2,256]{1,0:T(2,128)}, u32[]{:S(2)}) copy-start(f32[2,256]{1,0:T(2,128)} %couplings.1) | copy-start | bytes 6148
  56.6 10.2 %copy-start.6 = (s32[2,256]{1,0:T(2,128)S(1)}, s32[2,256]{1,0:T(2,128)}, u32[]{:S(2)}) copy-start(s32[2,256]{1,0:T(2,128)} %pattern.1) | copy-start | bytes 6148
  57.2 9.6 %copy-start.4 = (f32[2,256]{1,0:T(2,128)S(1)}, f32[2,256]{1,0:T(2,128)}, u32[]{:S(2)}) copy-start(f32[2,256]{1,0:T(2,128)} %pivots.1) | copy-start | bytes 6148
  57.3 8.2 %collective-permute-start.20 = (f32[256,256]{1,0:T(8,128)S(1)}, f32[256,256]{1,0:T(8,128)S(1)}, u32[]{:S(2)}, u32[]{:S(2)}) collective-permute-start(f32[256,256]{1,0:T(8,128)S(1)} %shard_map.87.refs_13_), channel_id=1, source_target_pairs={{8,24},{9,25},{10,26},{11,27},{12,28},{13,29},{14,30},{15,31}} | collective-permute-start | bytes 786440 | tf_op jit(solution)/shard_map/ppermute | solution.py:363
  57.9 7.5 %collective-permute-start.18 = (f32[64,768]{1,0:T(8,128)S(1)}, f32[64,768]{1,0:T(8,128)S(1)}, u32[]{:S(2)}, u32[]{:S(2)}) collective-permute-start(f32[64,768]{1,0:T(8,128)S(1)} %collective-permute-done.14.refs_5_), channel_id=1, source_target_pairs={{0,2},{2,4},{4,6},{6,7},{7,5},{5,3},{3,1},{1,0},{8,10},{10,12},{12... | collective-permute-start | bytes 589832 | tf_op jit(solution)/shard_map/ppermute | solution.py:346
  58.1 7.8 %collective-permute-start.24 = (f32[256,256]{1,0:T(8,128)S(1)}, f32[256,256]{1,0:T(8,128)S(1)}, u32[]{:S(2)}, u32[]{:S(2)}) collective-permute-start(f32[256,256]{1,0:T(8,128)S(1)} %shard_map.87.refs_13_), channel_id=1, source_target_pairs={{8,16},{9,17},{10,18},{11,19},{12,20},{13,21},{14,22},{15,23}} | collective-permute-start | bytes 786440 | tf_op jit(solution)/shard_map/ppermute | solution.py:363
  58.8 7.1 %collective-permute-start.23 = (f32[256,256]{1,0:T(8,128)S(1)}, f32[256,256]{1,0:T(8,128)S(1)}, u32[]{:S(2)}, u32[]{:S(2)}) collective-permute-start(f32[256,256]{1,0:T(8,128)S(1)} %shard_map.87.refs_13_), channel_id=1, source_target_pairs={{8,0},{9,1},{10,2},{11,3},{12,4},{13,5},{14,6},{15,7}} | collective-permute-start | bytes 786440 | tf_op jit(solution)/shard_map/ppermute | solution.py:363
  60.1 5.8 %collective-permute-start.21 = (f32[64,512]{1,0:T(8,128)S(1)}, f32[64,512]{1,0:T(8,128)S(1)}, u32[]{:S(2)}, u32[]{:S(2)}) collective-permute-start(f32[64,512]{1,0:T(8,128)S(1)} %collective-permute-done.16.refs_8_), channel_id=1, source_target_pairs={{0,8},{8,0},{16,24},{24,16},{1,9},{9,1},{17,25},{25,17},{2,10},{10... | collective-permute-start | bytes 393224 | tf_op jit(solution)/shard_map/ppermute | solution.py:254
  65.5 1.4 %collective-permute-start.22 = (f32[64,512]{1,0:T(8,128)S(1)}, f32[64,512]{1,0:T(8,128)S(1)}, u32[]{:S(2)}, u32[]{:S(2)}) collective-permute-start(f32[64,512]{1,0:T(8,128)S(1)} %collective-permute-done.17.refs_9_), channel_id=1, source_target_pairs={{0,8},{8,0},{16,24},{24,16},{1,9},{9,1},{17,25},{25,17},{2,10},{10... | collective-permute-start | bytes 393224 | tf_op jit(solution)/shard_map/ppermute | solution.py:254

commit v7 on v5

--- a/solution.py
+++ b/solution.py
@@ -183,7 +183,7 @@
 
 
 def finish(
-    rows_axis, order, own_order, me, target, block, inverses, pivots, couplings, pattern, *refs
+    rows_axis, order, own_order, me, target, block, high, low, pivots, couplings, pattern, *refs
 ):
     *pieces, out, rows, own, corner = refs
     pieces, corners = pieces[:-rows_axis], pieces[-rows_axis:]
@@ -222,7 +222,9 @@
     scaled0 = scale(low0_own, pivots, couplings, pattern, 0)
     matrix = matrix - mm_nt(low0, scaled0)
 
-    update = mm(scale(corner[...], pivots, couplings, pattern, 0).T, inverses[1])
+    parts = split(scale(corner[...], pivots, couplings, pattern, 0).T)
+    both = jnp.dot(jnp.concatenate(parts, axis=0), high[1], preferred_element_type=f32)
+    update = both[:tile] + (both[tile:] + jnp.dot(parts[0], low[1], preferred_element_type=f32))
     low1 = jnp.where(ids >= 2 * tile, second - mm(low0, update), 0.0)
     low1_own = jnp.where(col > 1, own[:, tile : 2 * tile] - mm(low0_own, update), 0.0)
     scaled1 = scale(low1_own, pivots, couplings, pattern, 1)
@@ -372,7 +374,8 @@
         me,
         target,
         block,
-        inverses,
+        high,
+        low,
         pivots,
         couplings,
         pattern,

time: 70.6 us -> 70.5 us (level)
  no operation moved by 1% of the time
where the time goes in v7:
time: 70.5 us; the launch traced here: 70.3 us
  starting transfers between devices  32.2 us (46%)
  waiting for transfers between devices  26.6 us (38%)
  Pallas kernels  9.37 us (13%)
  local copies, waits for them, and re-layouts  1.76 us (2%)
    ppermute x7, starting transfers between devices, shards(): lax.ppermute(pieces[i], 'col', [(c, c ^ i) for c in range(cols_axis)])  11.3 us
    pallas_call x7, Pallas kernels, call(): pl.pallas_call(body, out_shape=[jax.ShapeDtypeStruct(*out) if isinstance(...  9.37 us
    ppermute x5, starting transfers between devices, flip(): return lax.ppermute(value, 'row', [(i, i ^ bit) for i in range(rows_axis)])  8.25 us
    ppermute x4, waiting for transfers between devices, shards(): right = lax.ppermute(right, 'col', after)  7.41 us
    ppermute x5, waiting for transfers between devices, flip(): return lax.ppermute(value, 'row', [(i, i ^ bit) for i in range(rows_axis)])  6.79 us
    ppermute x3, waiting for transfers between devices, shards(): left = lax.ppermute(left, 'col', before)  6.39 us
    ppermute x7, waiting for transfers between devices, shards(): lax.ppermute(pieces[i], 'col', [(c, c ^ i) for c in range(cols_axis)])  5.96 us
    ppermute x4, starting transfers between devices, shards(): right = lax.ppermute(right, 'col', after)  4.59 us
  transfers between devices with their start and end apart: 25, of which 12 were waited for; matrix products, arithmetic and copies ran while one was open for 0% of the time, Pallas kernels for 2%

profile of v7, /device:TPU:0, one launch (start us, length us, event | category | flops | bytes accessed | tf_op | source)
XLA Modules:
  0.0 70.3 jit_solution(4321662915416875503)
XLA Ops:
  0.0 0.1 pad_add_fusion.me
  0.1 0.6 copy-done.3
  0.7 1.0 %copy-done = f32[512,256]{1,0:T(8,128)S(1)} copy-done((f32[512,256]{1,0:T(8,128)S(1)}, f32[512,256]{1,0:T(8,128)}, u32[]{:S(2)}) %copy-start) | copy-done | bytes 524312
  1.7 1.8 %shard_map.83 = (f32[256,256]{1,0:T(8,128)S(1)}, f32[256,256]{1,0:T(8,128)S(1)}) custom-call(s32[3]{0:T(128)S(1)} %pad_add_fusion.me, s32[4,128]{1,0:T(4,128)S(1)} %bitcast.5, f32[512,256]{1,0:T(8,128)S(1)} %copy-done), custom_call_target="tpu_custom_call" | custom-call | tf_op jit(solution)/shard_map/pallas_call | solution.py:59
  3.5 0.5 collective-permute-start
  4.1 1.2 %collective-permute-done = f32[256,256]{1,0:T(8,128)S(1)} collective-permute-done((f32[256,256]{1,0:T(8,128)S(1)}, f32[256,256]{1,0:T(8,128)S(1)}, u32[]{:S(2)}, u32[]{:S(2)}) %collective-permute-start) | collective-permute-done | bytes 262176 | tf_op jit(solution)/shard_map/ppermute | solution.py:256
  5.3 2.9 %collective-permute-start.1 = (f32[128,256]{1,0:T(8,128)S(1)}, f32[128,256]{1,0:T(8,128)S(1)}, u32[]{:S(2)}, u32[]{:S(2)}) collective-permute-start(f32[128,256]{1,0:T(8,128)S(1)} %slice_select_fusion.1), channel_id=1, source_target_pairs={{0,16},{8,24},{16,0},{24,8},{1,17},{9,25},{17,1},{25,9},{2,18},{10... | collective-permute-start | bytes 393224 | tf_op jit(solution)/shard_map/ppermute | solution.py:256
  8.3 3.8 %collective-permute-done.1 = f32[128,256]{1,0:T(8,128)S(1)} collective-permute-done((f32[128,256]{1,0:T(8,128)S(1)}, f32[128,256]{1,0:T(8,128)S(1)}, u32[]{:S(2)}, u32[]{:S(2)}) %collective-permute-start.1) | collective-permute-done | bytes 131104 | tf_op jit(solution)/shard_map/ppermute | solution.py:256
  12.1 0.1 collective-permute-start.2
  12.2 0.4 shard_map.82
  12.6 0.9 %collective-permute-done.2.other = f32[128,256]{1,0:T(8,128)S(1)} collective-permute-done((f32[128,256]{1,0:T(8,128)S(1)}, f32[128,256]{1,0:T(8,128)S(1)}, u32[]{:S(2)}, u32[]{:S(2)}) %collective-permute-start.2) | collective-permute-done | bytes 131104 | tf_op jit(solution)/shard_map/ppermute | solution.py:256
  13.5 1.1 %shard_map.84 = (f32[512,256]{1,0:T(8,128)S(1)}, f32[64,256]{1,0:T(8,128)S(1)}, f32[64,256]{1,0:T(8,128)S(1)}, f32[64,256]{1,0:T(8,128)S(1)}, f32[64,256]{1,0:T(...) custom-call(s32[3]{0:T(128)S(1)} %pad_add_fusion.me, ...), custom_call_target="tpu_custom_call" | custom-call | tf_op jit(solution)/shard_map/pallas_call | solution.py:59
  14.6 1.8 %collective-permute-start.3 = (f32[64,256]{1,0:T(8,128)S(1)}, f32[64,256]{1,0:T(8,128)S(1)}, u32[]{:S(2)}, u32[]{:S(2)}) collective-permute-start(f32[64,256]{1,0:T(8,128)S(1)} %get-tuple-element.36), channel_id=1, source_target_pairs={{0,1},{1,0},{2,3},{3,2},{4,5},{5,4},{6,7},{7,6},{8,9},{9,8},{10,11... | collective-permute-start | bytes 196616 | tf_op jit(solution)/shard_map/ppermute | solution.py:305
  16.4 1.6 %collective-permute-start.4 = (f32[64,256]{1,0:T(8,128)S(1)}, f32[64,256]{1,0:T(8,128)S(1)}, u32[]{:S(2)}, u32[]{:S(2)}) collective-permute-start(f32[64,256]{1,0:T(8,128)S(1)} %get-tuple-element.37), channel_id=1, source_target_pairs={{0,2},{1,3},{2,0},{3,1},{4,6},{5,7},{6,4},{7,5},{8,10},{9,11},{10,... | collective-permute-start | bytes 196616 | tf_op jit(solution)/shard_map/ppermute | solution.py:305
  18.0 0.2 collective-permute-start.5
  18.2 2.8 %collective-permute-start.6 = (f32[64,256]{1,0:T(8,128)S(1)}, f32[64,256]{1,0:T(8,128)S(1)}, u32[]{:S(2)}, u32[]{:S(2)}) collective-permute-start(f32[64,256]{1,0:T(8,128)S(1)} %get-tuple-element.39), channel_id=1, source_target_pairs={{0,4},{1,5},{2,6},{3,7},{4,0},{5,1},{6,2},{7,3},{8,12},{9,13},{10,... | collective-permute-start | bytes 196616 | tf_op jit(solution)/shard_map/ppermute | solution.py:305
  21.0 1.3 %collective-permute-start.7 = (f32[64,256]{1,0:T(8,128)S(1)}, f32[64,256]{1,0:T(8,128)S(1)}, u32[]{:S(2)}, u32[]{:S(2)}) collective-permute-start(f32[64,256]{1,0:T(8,128)S(1)} %get-tuple-element.40), channel_id=1, source_target_pairs={{0,5},{1,4},{2,7},{3,6},{4,1},{5,0},{6,3},{7,2},{8,13},{9,12},{10,... | collective-permute-start | bytes 196616 | tf_op jit(solution)/shard_map/ppermute | solution.py:305
  22.3 3.6 %collective-permute-start.8 = (f32[64,256]{1,0:T(8,128)S(1)}, f32[64,256]{1,0:T(8,128)S(1)}, u32[]{:S(2)}, u32[]{:S(2)}) collective-permute-start(f32[64,256]{1,0:T(8,128)S(1)} %get-tuple-element.41), channel_id=1, source_target_pairs={{0,6},{1,7},{2,4},{3,5},{4,2},{5,3},{6,0},{7,1},{8,14},{9,15},{10,... | collective-permute-start | bytes 196616 | tf_op jit(solution)/shard_map/ppermute | solution.py:305
  25.9 0.0 collective-permute-start.9
  25.9 0.1 slice.19.tiles
  26.0 1.0 %shard_map.85.so_far = f32[128,768]{1,0:T(8,128)S(1)} custom-call(s32[5]{0:T(128)S(1)} %bitcast.7, s32[1,768]{1,0:T(1,128)S(1)} %get-tuple-element.34.source, f32[64,256]{1,0:T(8,128)S(1)} %get-tuple-element.35.refs_0_, f32[64,256]{1,0:T(8,128)S(1)} %collective-permute-done.3.refs_1_, f32[64,256]{1,0:T(8,128)S(1)} %collective-permute-done.4.refs_2_, ...), custom_call_target="tpu_custom_call" | custom-call | tf_op jit(solution)/shard_map/pallas_call | solution.py:59
  27.0 4.5 %collective-permute-done.7.refs_0_ = f32[64,256]{1,0:T(8,128)S(1)} collective-permute-done((f32[64,256]{1,0:T(8,128)S(1)}, f32[64,256]{1,0:T(8,128)S(1)}, u32[]{:S(2)}, u32[]{:S(2)}) %collective-permute-start.7) | collective-permute-done | bytes 65568 | tf_op jit(solution)/shard_map/ppermute | solution.py:305
  31.4 1.5 %collective-permute-done.9.refs_2_ = f32[64,256]{1,0:T(8,128)S(1)} collective-permute-done((f32[64,256]{1,0:T(8,128)S(1)}, f32[64,256]{1,0:T(8,128)S(1)}, u32[]{:S(2)}, u32[]{:S(2)}) %collective-permute-start.9) | collective-permute-done | bytes 65568 | tf_op jit(solution)/shard_map/ppermute | solution.py:305
  32.9 1.1 %shard_map.86 = (f32[64,768]{1,0:T(8,128)S(1)}, f32[64,512]{1,0:T(8,128)S(1)}) custom-call(s32[3]{0:T(128)S(1)} %pad_add_fusion.me, s32[3]{0:T(128)S(1)} %slice.19.tiles, s32[1,768]{1,0:T(1,128)S(1)} %get-tuple-element.34.source, bf16[2,256,256]{2,1,0:T(8,128)(2,1)S(1)} %get-tuple-element.32.high, bf16[2,256,256]{2,1,0:T(8,128)(2,1)S(1)} %get-tuple-element.33.low, ...), custom_call_target="tpu_custom_call" | custom-call | tf_op jit(solution)/shard_map/pallas_call | solution.py:59
  34.0 0.6 collective-permute-start.11
  34.6 1.5 %collective-permute-start.10 = (f32[64,768]{1,0:T(8,128)S(1)}, f32[64,768]{1,0:T(8,128)S(1)}, u32[]{:S(2)}, u32[]{:S(2)}) collective-permute-start(f32[64,768]{1,0:T(8,128)S(1)} %get-tuple-element.43.refs_0_), channel_id=1, source_target_pairs={{0,2},{2,4},{4,6},{6,7},{7,5},{5,3},{3,1},{1,0},{8,10},{10,12},{12... | collective-permute-start | bytes 589832 | tf_op jit(solution)/shard_map/ppermute | solution.py:348
  36.1 4.5 %collective-permute-done.11.refs_2_ = f32[64,768]{1,0:T(8,128)S(1)} collective-permute-done((f32[64,768]{1,0:T(8,128)S(1)}, f32[64,768]{1,0:T(8,128)S(1)}, u32[]{:S(2)}, u32[]{:S(2)}) %collective-permute-start.11) | collective-permute-done | bytes 196640 | tf_op jit(solution)/shard_map/ppermute | solution.py:352
  40.6 0.2 collective-permute-start.13
  40.8 0.5 collective-permute-done.10.refs_1_
  41.3 1.3 %collective-permute-start.12 = (f32[64,768]{1,0:T(8,128)S(1)}, f32[64,768]{1,0:T(8,128)S(1)}, u32[]{:S(2)}, u32[]{:S(2)}) collective-permute-start(f32[64,768]{1,0:T(8,128)S(1)} %collective-permute-done.10.refs_1_), channel_id=1, source_target_pairs={{0,2},{2,4},{4,6},{6,7},{7,5},{5,3},{3,1},{1,0},{8,10},{10,12},{12... | collective-permute-start | bytes 589832 | tf_op jit(solution)/shard_map/ppermute | solution.py:348
  42.6 1.6 %collective-permute-start.16 = (f32[64,512]{1,0:T(8,128)S(1)}, f32[64,512]{1,0:T(8,128)S(1)}, u32[]{:S(2)}, u32[]{:S(2)}) collective-permute-start(f32[64,512]{1,0:T(8,128)S(1)} %get-tuple-element.44), channel_id=1, source_target_pairs={{0,16},{1,24},{2,0},{3,8},{8,17},{9,25},{10,1},{11,9},{16,18},{17,... | collective-permute-start | bytes 393224 | tf_op jit(solution)/shard_map/ppermute | solution.py:330
  44.2 0.7 collective-permute-start.15
  44.8 0.7 collective-permute-start.19
  45.5 1.6 %collective-permute-done.13.refs_4_ = f32[64,768]{1,0:T(8,128)S(1)} collective-permute-done((f32[64,768]{1,0:T(8,128)S(1)}, f32[64,768]{1,0:T(8,128)S(1)}, u32[]{:S(2)}, u32[]{:S(2)}) %collective-permute-start.13) | collective-permute-done | bytes 196640 | tf_op jit(solution)/shard_map/ppermute | solution.py:352
  47.2 1.7 %collective-permute-start.17 = (f32[64,768]{1,0:T(8,128)S(1)}, f32[64,768]{1,0:T(8,128)S(1)}, u32[]{:S(2)}, u32[]{:S(2)}) collective-permute-start(f32[64,768]{1,0:T(8,128)S(1)} %collective-permute-done.13.refs_4_), channel_id=1, source_target_pairs={{2,0},{4,2},{6,4},{7,6},{5,7},{3,5},{1,3},{0,1},{10,8},{12,10},{14... | collective-permute-start | bytes 589832 | tf_op jit(solution)/shard_map/ppermute | solution.py:352
  48.9 1.5 %collective-permute-start.14 = (f32[64,768]{1,0:T(8,128)S(1)}, f32[64,768]{1,0:T(8,128)S(1)}, u32[]{:S(2)}, u32[]{:S(2)}) collective-permute-start(f32[64,768]{1,0:T(8,128)S(1)} %collective-permute-done.12.refs_3_), channel_id=1, source_target_pairs={{0,2},{2,4},{4,6},{6,7},{7,5},{5,3},{3,1},{1,0},{8,10},{10,12},{12... | collective-permute-start | bytes 589832 | tf_op jit(solution)/shard_map/ppermute | solution.py:348
  50.4 5.8 %collective-permute-done.14.refs_5_ = f32[64,768]{1,0:T(8,128)S(1)} collective-permute-done((f32[64,768]{1,0:T(8,128)S(1)}, f32[64,768]{1,0:T(8,128)S(1)}, u32[]{:S(2)}, u32[]{:S(2)}) %collective-permute-start.14) | collective-permute-done | bytes 196640 | tf_op jit(solution)/shard_map/ppermute | solution.py:348
  56.3 0.3 collective-permute-done.17.refs_6_
  56.5 0.6 shard_map.87.refs_13_
  57.2 0.7 collective-permute-start.20
  57.9 0.3 collective-permute-start.18
  58.2 0.7 collective-permute-start.24
  58.8 1.3 %collective-permute-start.23 = (f32[256,256]{1,0:T(8,128)S(1)}, f32[256,256]{1,0:T(8,128)S(1)}, u32[]{:S(2)}, u32[]{:S(2)}) collective-permute-start(f32[256,256]{1,0:T(8,128)S(1)} %shard_map.87.refs_13_), channel_id=1, source_target_pairs={{8,0},{9,1},{10,2},{11,3},{12,4},{13,5},{14,6},{15,7}} | collective-permute-start | bytes 786440 | tf_op jit(solution)/shard_map/ppermute | solution.py:365
  60.1 4.3 %collective-permute-start.21 = (f32[64,512]{1,0:T(8,128)S(1)}, f32[64,512]{1,0:T(8,128)S(1)}, u32[]{:S(2)}, u32[]{:S(2)}) collective-permute-start(f32[64,512]{1,0:T(8,128)S(1)} %collective-permute-done.15.refs_8_), channel_id=1, source_target_pairs={{0,8},{8,0},{16,24},{24,16},{1,9},{9,1},{17,25},{25,17},{2,10},{10... | collective-permute-start | bytes 393224 | tf_op jit(solution)/shard_map/ppermute | solution.py:256
  64.4 1.1 %collective-permute-done.18.refs_7_ = f32[64,768]{1,0:T(8,128)S(1)} collective-permute-done((f32[64,768]{1,0:T(8,128)S(1)}, f32[64,768]{1,0:T(8,128)S(1)}, u32[]{:S(2)}, u32[]{:S(2)}) %collective-permute-start.18) | collective-permute-done | bytes 196640 | tf_op jit(solution)/shard_map/ppermute | solution.py:348
  65.6 0.4 collective-permute-start.22
  66.0 1.0 %collective-permute-done.22.refs_11_ = f32[64,512]{1,0:T(8,128)S(1)} collective-permute-done((f32[64,512]{1,0:T(8,128)S(1)}, f32[64,512]{1,0:T(8,128)S(1)}, u32[]{:S(2)}, u32[]{:S(2)}) %collective-permute-start.22) | collective-permute-done | bytes 131104 | tf_op jit(solution)/shard_map/ppermute | solution.py:256
  67.0 3.3 %shard_map.88 = f32[512,256]{1,0:T(8,128)} custom-call(s32[8]{0:T(128)S(1)} %compare_select_fusion.2.rank.order, s32[4]{0:T(128)S(1)} %broadcast_xor_fusion.own_order, s32[3]{0:T(128)S(1)} %pad_add_fusion.me, s32[1,512]{1,0:T(1,128)S(1)} %get-tuple-element.28.target, f32[512,256]{1,0:T(8,128)S(1)} %get-tuple-element.31.block, ...), custom_call_target="tpu_custom_call" | custom-call | tf_op jit(solution)/shard_map/pallas_call | solution.py:59
  (36 shorter events, 0.2 us)
Async XLA Ops:
  0.0 0.7 copy-start.3
  0.7 1.0 %copy-start = (f32[512,256]{1,0:T(8,128)S(1)}, f32[512,256]{1,0:T(8,128)}, u32[]{:S(2)}) copy-start(f32[512,256]{1,0:T(8,128)} %block.3) | copy-start | bytes 1572868
  3.5 1.7 %collective-permute-start = (f32[256,256]{1,0:T(8,128)S(1)}, f32[256,256]{1,0:T(8,128)S(1)}, u32[]{:S(2)}, u32[]{:S(2)}) collective-permute-start(f32[256,256]{1,0:T(8,128)S(1)} %get-tuple-element.30), channel_id=1, source_target_pairs={{0,8},{8,0},{16,24},{24,16},{1,9},{9,1},{17,25},{25,17},{2,10},{10... | collective-permute-start | bytes 786440 | tf_op jit(solution)/shard_map/ppermute | solution.py:256
  5.3 6.9 %copy-start.2 = (f32[2,256,256]{2,1,0:T(8,128)S(1)}, f32[2,256,256]{2,1,0:T(8,128)}, u32[]{:S(2)}) copy-start(f32[2,256,256]{2,1,0:T(8,128)} %inverses.1) | copy-start | bytes 1572868
  5.3 8.2 %copy-start.1 = (f32[512,256]{1,0:T(8,128)S(1)}, f32[512,256]{1,0:T(8,128)}, u32[]{:S(2)}) copy-start(f32[512,256]{1,0:T(8,128)} %block.3) | copy-start | bytes 1572868
  5.3 6.7 %collective-permute-start.1 = (f32[128,256]{1,0:T(8,128)S(1)}, f32[128,256]{1,0:T(8,128)S(1)}, u32[]{:S(2)}, u32[]{:S(2)}) collective-permute-start(f32[128,256]{1,0:T(8,128)S(1)} %slice_select_fusion.1), channel_id=1, source_target_pairs={{0,16},{8,24},{16,0},{24,8},{1,17},{9,25},{17,1},{25,9},{2,18},{10... | collective-permute-start | bytes 393224 | tf_op jit(solution)/shard_map/ppermute | solution.py:256
  12.1 1.4 %collective-permute-start.2 = (f32[128,256]{1,0:T(8,128)S(1)}, f32[128,256]{1,0:T(8,128)S(1)}, u32[]{:S(2)}, u32[]{:S(2)}) collective-permute-start(f32[128,256]{1,0:T(8,128)S(1)} %get-tuple-element.51.mine), channel_id=1, source_target_pairs={{0,8},{8,0},{16,24},{24,16},{1,9},{9,1},{17,25},{25,17},{2,10},{10... | collective-permute-start | bytes 393224 | tf_op jit(solution)/shard_map/ppermute | solution.py:256
  14.6 7.6 %collective-permute-start.3 = (f32[64,256]{1,0:T(8,128)S(1)}, f32[64,256]{1,0:T(8,128)S(1)}, u32[]{:S(2)}, u32[]{:S(2)}) collective-permute-start(f32[64,256]{1,0:T(8,128)S(1)} %get-tuple-element.36), channel_id=1, source_target_pairs={{0,1},{1,0},{2,3},{3,2},{4,5},{5,4},{6,7},{7,6},{8,9},{9,8},{10,11... | collective-permute-start | bytes 196616 | tf_op jit(solution)/shard_map/ppermute | solution.py:305
  16.4 9.5 %collective-permute-start.4 = (f32[64,256]{1,0:T(8,128)S(1)}, f32[64,256]{1,0:T(8,128)S(1)}, u32[]{:S(2)}, u32[]{:S(2)}) collective-permute-start(f32[64,256]{1,0:T(8,128)S(1)} %get-tuple-element.37), channel_id=1, source_target_pairs={{0,2},{1,3},{2,0},{3,1},{4,6},{5,7},{6,4},{7,5},{8,10},{9,11},{10,... | collective-permute-start | bytes 196616 | tf_op jit(solution)/shard_map/ppermute | solution.py:305
  18.0 8.0 %collective-permute-start.5 = (f32[64,256]{1,0:T(8,128)S(1)}, f32[64,256]{1,0:T(8,128)S(1)}, u32[]{:S(2)}, u32[]{:S(2)}) collective-permute-start(f32[64,256]{1,0:T(8,128)S(1)} %get-tuple-element.38), channel_id=1, source_target_pairs={{0,3},{1,2},{2,1},{3,0},{4,7},{5,6},{6,5},{7,4},{8,11},{9,10},{10,... | collective-permute-start | bytes 196616 | tf_op jit(solution)/shard_map/ppermute | solution.py:305
  18.2 7.8 %collective-permute-start.6 = (f32[64,256]{1,0:T(8,128)S(1)}, f32[64,256]{1,0:T(8,128)S(1)}, u32[]{:S(2)}, u32[]{:S(2)}) collective-permute-start(f32[64,256]{1,0:T(8,128)S(1)} %get-tuple-element.39), channel_id=1, source_target_pairs={{0,4},{1,5},{2,6},{3,7},{4,0},{5,1},{6,2},{7,3},{8,12},{9,13},{10,... | collective-permute-start | bytes 196616 | tf_op jit(solution)/shard_map/ppermute | solution.py:305
  21.0 10.5 %collective-permute-start.7 = (f32[64,256]{1,0:T(8,128)S(1)}, f32[64,256]{1,0:T(8,128)S(1)}, u32[]{:S(2)}, u32[]{:S(2)}) collective-permute-start(f32[64,256]{1,0:T(8,128)S(1)} %get-tuple-element.40), channel_id=1, source_target_pairs={{0,5},{1,4},{2,7},{3,6},{4,1},{5,0},{6,3},{7,2},{8,13},{9,12},{10,... | collective-permute-start | bytes 196616 | tf_op jit(solution)/shard_map/ppermute | solution.py:305
  22.3 9.2 %collective-permute-start.8 = (f32[64,256]{1,0:T(8,128)S(1)}, f32[64,256]{1,0:T(8,128)S(1)}, u32[]{:S(2)}, u32[]{:S(2)}) collective-permute-start(f32[64,256]{1,0:T(8,128)S(1)} %get-tuple-element.41), channel_id=1, source_target_pairs={{0,6},{1,7},{2,4},{3,5},{4,2},{5,3},{6,0},{7,1},{8,14},{9,15},{10,... | collective-permute-start | bytes 196616 | tf_op jit(solution)/shard_map/ppermute | solution.py:305
  25.9 7.1 %collective-permute-start.9 = (f32[64,256]{1,0:T(8,128)S(1)}, f32[64,256]{1,0:T(8,128)S(1)}, u32[]{:S(2)}, u32[]{:S(2)}) collective-permute-start(f32[64,256]{1,0:T(8,128)S(1)} %get-tuple-element.42), channel_id=1, source_target_pairs={{0,7},{1,6},{2,5},{3,4},{4,3},{5,2},{6,1},{7,0},{8,15},{9,14},{10,... | collective-permute-start | bytes 196616 | tf_op jit(solution)/shard_map/ppermute | solution.py:305
  34.0 6.5 %collective-permute-start.11 = (f32[64,768]{1,0:T(8,128)S(1)}, f32[64,768]{1,0:T(8,128)S(1)}, u32[]{:S(2)}, u32[]{:S(2)}) collective-permute-start(f32[64,768]{1,0:T(8,128)S(1)} %get-tuple-element.43.refs_0_), channel_id=1, source_target_pairs={{2,0},{4,2},{6,4},{7,6},{5,7},{3,5},{1,3},{0,1},{10,8},{12,10},{14... | collective-permute-start | bytes 589832 | tf_op jit(solution)/shard_map/ppermute | solution.py:352
  34.6 6.7 %collective-permute-start.10 = (f32[64,768]{1,0:T(8,128)S(1)}, f32[64,768]{1,0:T(8,128)S(1)}, u32[]{:S(2)}, u32[]{:S(2)}) collective-permute-start(f32[64,768]{1,0:T(8,128)S(1)} %get-tuple-element.43.refs_0_), channel_id=1, source_target_pairs={{0,2},{2,4},{4,6},{6,7},{7,5},{5,3},{3,1},{1,0},{8,10},{10,12},{12... | collective-permute-start | bytes 589832 | tf_op jit(solution)/shard_map/ppermute | solution.py:348
  40.6 6.6 %collective-permute-start.13 = (f32[64,768]{1,0:T(8,128)S(1)}, f32[64,768]{1,0:T(8,128)S(1)}, u32[]{:S(2)}, u32[]{:S(2)}) collective-permute-start(f32[64,768]{1,0:T(8,128)S(1)} %collective-permute-done.11.refs_2_), channel_id=1, source_target_pairs={{2,0},{4,2},{6,4},{7,6},{5,7},{3,5},{1,3},{0,1},{10,8},{12,10},{14... | collective-permute-start | bytes 589832 | tf_op jit(solution)/shard_map/ppermute | solution.py:352
  41.3 7.6 %collective-permute-start.12 = (f32[64,768]{1,0:T(8,128)S(1)}, f32[64,768]{1,0:T(8,128)S(1)}, u32[]{:S(2)}, u32[]{:S(2)}) collective-permute-start(f32[64,768]{1,0:T(8,128)S(1)} %collective-permute-done.10.refs_1_), channel_id=1, source_target_pairs={{0,2},{2,4},{4,6},{6,7},{7,5},{5,3},{3,1},{1,0},{8,10},{10,12},{12... | collective-permute-start | bytes 589832 | tf_op jit(solution)/shard_map/ppermute | solution.py:348
  42.6 7.8 %copy-start.8 = (s32[8]{0:T(128)S(1)}, s32[8]{0:T(128)}, u32[]{:S(2)}) copy-start(s32[8]{0:T(128)} %constant.63.clone) | copy-start | bytes 100
  42.6 7.8 %collective-permute-start.16 = (f32[64,512]{1,0:T(8,128)S(1)}, f32[64,512]{1,0:T(8,128)S(1)}, u32[]{:S(2)}, u32[]{:S(2)}) collective-permute-start(f32[64,512]{1,0:T(8,128)S(1)} %get-tuple-element.44), channel_id=1, source_target_pairs={{0,16},{1,24},{2,0},{3,8},{8,17},{9,25},{10,1},{11,9},{16,18},{17,... | collective-permute-start | bytes 393224 | tf_op jit(solution)/shard_map/ppermute | solution.py:330
  44.2 6.2 %collective-permute-start.15 = (f32[64,512]{1,0:T(8,128)S(1)}, f32[64,512]{1,0:T(8,128)S(1)}, u32[]{:S(2)}, u32[]{:S(2)}) collective-permute-start(f32[64,512]{1,0:T(8,128)S(1)} %get-tuple-element.44), channel_id=1, source_target_pairs={{0,0},{1,8},{2,16},{3,24},{8,1},{9,9},{10,17},{11,25},{16,2},{17,1... | collective-permute-start | bytes 393224 | tf_op jit(solution)/shard_map/ppermute | solution.py:330
  44.8 11.4 %collective-permute-start.19 = (f32[64,256]{1,0:T(8,128)S(1)}, f32[64,256]{1,0:T(8,128)S(1)}, u32[]{:S(2)}, u32[]{:S(2)}) collective-permute-start(f32[64,256]{1,0:T(8,128)S(1)} %slice.21), channel_id=1, source_target_pairs={{8,15},{9,14},{10,13},{11,12}} | collective-permute-start | bytes 196616 | tf_op jit(solution)/shard_map/ppermute | solution.py:363
  47.2 9.4 %collective-permute-start.17 = (f32[64,768]{1,0:T(8,128)S(1)}, f32[64,768]{1,0:T(8,128)S(1)}, u32[]{:S(2)}, u32[]{:S(2)}) collective-permute-start(f32[64,768]{1,0:T(8,128)S(1)} %collective-permute-done.13.refs_4_), channel_id=1, source_target_pairs={{2,0},{4,2},{6,4},{7,6},{5,7},{3,5},{1,3},{0,1},{10,8},{12,10},{14... | collective-permute-start | bytes 589832 | tf_op jit(solution)/shard_map/ppermute | solution.py:352
  48.9 7.4 %collective-permute-start.14 = (f32[64,768]{1,0:T(8,128)S(1)}, f32[64,768]{1,0:T(8,128)S(1)}, u32[]{:S(2)}, u32[]{:S(2)}) collective-permute-start(f32[64,768]{1,0:T(8,128)S(1)} %collective-permute-done.12.refs_3_), channel_id=1, source_target_pairs={{0,2},{2,4},{4,6},{6,7},{7,5},{5,3},{3,1},{1,0},{8,10},{10,12},{12... | collective-permute-start | bytes 589832 | tf_op jit(solution)/shard_map/ppermute | solution.py:348
  50.4 15.6 %copy-start.7 = (s32[4]{0:T(128)S(1)}, s32[4]{0:T(128)}, u32[]{:S(2)}) copy-start(s32[4]{0:T(128)} %constant.64.clone) | copy-start | bytes 52
  56.5 10.4 %copy-start.5 = (f32[2,256]{1,0:T(2,128)S(1)}, f32[2,256]{1,0:T(2,128)}, u32[]{:S(2)}) copy-start(f32[2,256]{1,0:T(2,128)} %couplings.1) | copy-start | bytes 6148
  56.5 10.4 %copy-start.6 = (s32[2,256]{1,0:T(2,128)S(1)}, s32[2,256]{1,0:T(2,128)}, u32[]{:S(2)}) copy-start(s32[2,256]{1,0:T(2,128)} %pattern.1) | copy-start | bytes 6148
  57.2 9.8 %copy-start.4 = (f32[2,256]{1,0:T(2,128)S(1)}, f32[2,256]{1,0:T(2,128)}, u32[]{:S(2)}) copy-start(f32[2,256]{1,0:T(2,128)} %pivots.1) | copy-start | bytes 6148
  57.2 8.4 %collective-permute-start.20 = (f32[256,256]{1,0:T(8,128)S(1)}, f32[256,256]{1,0:T(8,128)S(1)}, u32[]{:S(2)}, u32[]{:S(2)}) collective-permute-start(f32[256,256]{1,0:T(8,128)S(1)} %shard_map.87.refs_13_), channel_id=1, source_target_pairs={{8,24},{9,25},{10,26},{11,27},{12,28},{13,29},{14,30},{15,31}} | collective-permute-start | bytes 786440 | tf_op jit(solution)/shard_map/ppermute | solution.py:365
  57.9 7.7 %collective-permute-start.18 = (f32[64,768]{1,0:T(8,128)S(1)}, f32[64,768]{1,0:T(8,128)S(1)}, u32[]{:S(2)}, u32[]{:S(2)}) collective-permute-start(f32[64,768]{1,0:T(8,128)S(1)} %collective-permute-done.14.refs_5_), channel_id=1, source_target_pairs={{0,2},{2,4},{4,6},{6,7},{7,5},{5,3},{3,1},{1,0},{8,10},{10,12},{12... | collective-permute-start | bytes 589832 | tf_op jit(solution)/shard_map/ppermute | solution.py:348
  58.2 7.8 %collective-permute-start.24 = (f32[256,256]{1,0:T(8,128)S(1)}, f32[256,256]{1,0:T(8,128)S(1)}, u32[]{:S(2)}, u32[]{:S(2)}) collective-permute-start(f32[256,256]{1,0:T(8,128)S(1)} %shard_map.87.refs_13_), channel_id=1, source_target_pairs={{8,16},{9,17},{10,18},{11,19},{12,20},{13,21},{14,22},{15,23}} | collective-permute-start | bytes 786440 | tf_op jit(solution)/shard_map/ppermute | solution.py:365
  58.8 7.2 %collective-permute-start.23 = (f32[256,256]{1,0:T(8,128)S(1)}, f32[256,256]{1,0:T(8,128)S(1)}, u32[]{:S(2)}, u32[]{:S(2)}) collective-permute-start(f32[256,256]{1,0:T(8,128)S(1)} %shard_map.87.refs_13_), channel_id=1, source_target_pairs={{8,0},{9,1},{10,2},{11,3},{12,4},{13,5},{14,6},{15,7}} | collective-permute-start | bytes 786440 | tf_op jit(solution)/shard_map/ppermute | solution.py:365
  60.1 5.8 %collective-permute-start.21 = (f32[64,512]{1,0:T(8,128)S(1)}, f32[64,512]{1,0:T(8,128)S(1)}, u32[]{:S(2)}, u32[]{:S(2)}) collective-permute-start(f32[64,512]{1,0:T(8,128)S(1)} %collective-permute-done.15.refs_8_), channel_id=1, source_target_pairs={{0,8},{8,0},{16,24},{24,16},{1,9},{9,1},{17,25},{25,17},{2,10},{10... | collective-permute-start | bytes 393224 | tf_op jit(solution)/shard_map/ppermute | solution.py:256
  65.6 1.4 %collective-permute-start.22 = (f32[64,512]{1,0:T(8,128)S(1)}, f32[64,512]{1,0:T(8,128)S(1)}, u32[]{:S(2)}, u32[]{:S(2)}) collective-permute-start(f32[64,512]{1,0:T(8,128)S(1)} %collective-permute-done.16.refs_9_), channel_id=1, source_target_pairs={{0,8},{8,0},{16,24},{24,16},{1,9},{9,1},{17,25},{25,17},{2,10},{10... | collective-permute-start | bytes 393224 | tf_op jit(solution)/shard_map/ppermute | solution.py:256

commit v8 on v5

--- a/solution.py
+++ b/solution.py
@@ -362,7 +362,7 @@
     (corner,) = call(collect, [(tile, tile)], order, *parts[:-1], extra, smem=1)
     corners = [corner if r == 1 else lax.ppermute(corner, "row", [(1, r)]) for r in range(rows_axis)]
     free = [flip(near_part, 1) for near_part in near_parts[:-1]]
-    parts[-1], corners[3], tied = lax.optimization_barrier((parts[-1], corners[3], near_parts[-1]))
+    parts[-1], corners[2], tied = lax.optimization_barrier((parts[-1], corners[2], near_parts[-1]))
     own_parts = near_parts + free + [flip(tied, 1)]
     (out,) = call(
         functools.partial(finish, rows_axis),

time: 70.6 us -> 70.6 us (level)
  no operation moved by 1% of the time
where the time goes in v8:
time: 70.6 us; the launch traced here: 70.3 us
  starting transfers between devices  32.5 us (46%)
  waiting for transfers between devices  26.3 us (37%)
  Pallas kernels  9.39 us (13%)
  local copies, waits for them, and re-layouts  1.76 us (2%)
    ppermute x7, starting transfers between devices, shards(): lax.ppermute(pieces[i], 'col', [(c, c ^ i) for c in range(cols_axis)])  11.3 us
    pallas_call x7, Pallas kernels, call(): pl.pallas_call(body, out_shape=[jax.ShapeDtypeStruct(*out) if isinstance(...  9.39 us
    ppermute x5, starting transfers between devices, flip(): return lax.ppermute(value, 'row', [(i, i ^ bit) for i in range(rows_axis)])  8.58 us
    ppermute x4, waiting for transfers between devices, shards(): right = lax.ppermute(right, 'col', after)  7.09 us
    ppermute x5, waiting for transfers between devices, flip(): return lax.ppermute(value, 'row', [(i, i ^ bit) for i in range(rows_axis)])  6.8 us
    ppermute x3, waiting for transfers between devices, shards(): left = lax.ppermute(left, 'col', before)  6.41 us
    ppermute x7, waiting for transfers between devices, shards(): lax.ppermute(pieces[i], 'col', [(c, c ^ i) for c in range(cols_axis)])  5.96 us
    ppermute x4, starting transfers between devices, shards(): right = lax.ppermute(right, 'col', after)  4.57 us
  transfers between devices with their start and end apart: 25, of which 12 were waited for; matrix products, arithmetic and copies ran while one was open for 0% of the time, Pallas kernels for 2%

profile of v8, /device:TPU:0, one launch (start us, length us, event | category | flops | bytes accessed | tf_op | source)
XLA Modules:
  0.0 70.3 jit_solution(7071469601392496318)
XLA Ops:
  0.0 0.1 pad_add_fusion.me
  0.1 0.6 copy-done.3
  0.7 1.0 %copy-done = f32[512,256]{1,0:T(8,128)S(1)} copy-done((f32[512,256]{1,0:T(8,128)S(1)}, f32[512,256]{1,0:T(8,128)}, u32[]{:S(2)}) %copy-start) | copy-done | bytes 524312
  1.7 1.8 %shard_map.83 = (f32[256,256]{1,0:T(8,128)S(1)}, f32[256,256]{1,0:T(8,128)S(1)}) custom-call(s32[3]{0:T(128)S(1)} %pad_add_fusion.me, s32[4,128]{1,0:T(4,128)S(1)} %bitcast.5, f32[512,256]{1,0:T(8,128)S(1)} %copy-done), custom_call_target="tpu_custom_call" | custom-call | tf_op jit(solution)/shard_map/pallas_call | solution.py:59
  3.5 0.5 collective-permute-start
  4.1 1.2 %collective-permute-done = f32[256,256]{1,0:T(8,128)S(1)} collective-permute-done((f32[256,256]{1,0:T(8,128)S(1)}, f32[256,256]{1,0:T(8,128)S(1)}, u32[]{:S(2)}, u32[]{:S(2)}) %collective-permute-start) | collective-permute-done | bytes 262176 | tf_op jit(solution)/shard_map/ppermute | solution.py:254
  5.3 2.9 %collective-permute-start.1 = (f32[128,256]{1,0:T(8,128)S(1)}, f32[128,256]{1,0:T(8,128)S(1)}, u32[]{:S(2)}, u32[]{:S(2)}) collective-permute-start(f32[128,256]{1,0:T(8,128)S(1)} %slice_select_fusion.1), channel_id=1, source_target_pairs={{0,16},{8,24},{16,0},{24,8},{1,17},{9,25},{17,1},{25,9},{2,18},{10... | collective-permute-start | bytes 393224 | tf_op jit(solution)/shard_map/ppermute | solution.py:254
  8.3 3.8 %collective-permute-done.1 = f32[128,256]{1,0:T(8,128)S(1)} collective-permute-done((f32[128,256]{1,0:T(8,128)S(1)}, f32[128,256]{1,0:T(8,128)S(1)}, u32[]{:S(2)}, u32[]{:S(2)}) %collective-permute-start.1) | collective-permute-done | bytes 131104 | tf_op jit(solution)/shard_map/ppermute | solution.py:254
  12.1 0.1 collective-permute-start.2
  12.2 0.4 shard_map.82
  12.6 0.9 %collective-permute-done.2.other = f32[128,256]{1,0:T(8,128)S(1)} collective-permute-done((f32[128,256]{1,0:T(8,128)S(1)}, f32[128,256]{1,0:T(8,128)S(1)}, u32[]{:S(2)}, u32[]{:S(2)}) %collective-permute-start.2) | collective-permute-done | bytes 131104 | tf_op jit(solution)/shard_map/ppermute | solution.py:254
  13.5 1.1 %shard_map.84 = (f32[512,256]{1,0:T(8,128)S(1)}, f32[64,256]{1,0:T(8,128)S(1)}, f32[64,256]{1,0:T(8,128)S(1)}, f32[64,256]{1,0:T(8,128)S(1)}, f32[64,256]{1,0:T(...) custom-call(s32[3]{0:T(128)S(1)} %pad_add_fusion.me, ...), custom_call_target="tpu_custom_call" | custom-call | tf_op jit(solution)/shard_map/pallas_call | solution.py:59
  14.6 1.8 %collective-permute-start.3 = (f32[64,256]{1,0:T(8,128)S(1)}, f32[64,256]{1,0:T(8,128)S(1)}, u32[]{:S(2)}, u32[]{:S(2)}) collective-permute-start(f32[64,256]{1,0:T(8,128)S(1)} %get-tuple-element.36), channel_id=1, source_target_pairs={{0,1},{1,0},{2,3},{3,2},{4,5},{5,4},{6,7},{7,6},{8,9},{9,8},{10,11... | collective-permute-start | bytes 196616 | tf_op jit(solution)/shard_map/ppermute | solution.py:303
  16.4 1.6 %collective-permute-start.4 = (f32[64,256]{1,0:T(8,128)S(1)}, f32[64,256]{1,0:T(8,128)S(1)}, u32[]{:S(2)}, u32[]{:S(2)}) collective-permute-start(f32[64,256]{1,0:T(8,128)S(1)} %get-tuple-element.37), channel_id=1, source_target_pairs={{0,2},{1,3},{2,0},{3,1},{4,6},{5,7},{6,4},{7,5},{8,10},{9,11},{10,... | collective-permute-start | bytes 196616 | tf_op jit(solution)/shard_map/ppermute | solution.py:303
  18.0 0.2 collective-permute-start.5
  18.2 2.8 %collective-permute-start.6 = (f32[64,256]{1,0:T(8,128)S(1)}, f32[64,256]{1,0:T(8,128)S(1)}, u32[]{:S(2)}, u32[]{:S(2)}) collective-permute-start(f32[64,256]{1,0:T(8,128)S(1)} %get-tuple-element.39), channel_id=1, source_target_pairs={{0,4},{1,5},{2,6},{3,7},{4,0},{5,1},{6,2},{7,3},{8,12},{9,13},{10,... | collective-permute-start | bytes 196616 | tf_op jit(solution)/shard_map/ppermute | solution.py:303
  21.0 1.3 %collective-permute-start.7 = (f32[64,256]{1,0:T(8,128)S(1)}, f32[64,256]{1,0:T(8,128)S(1)}, u32[]{:S(2)}, u32[]{:S(2)}) collective-permute-start(f32[64,256]{1,0:T(8,128)S(1)} %get-tuple-element.40), channel_id=1, source_target_pairs={{0,5},{1,4},{2,7},{3,6},{4,1},{5,0},{6,3},{7,2},{8,13},{9,12},{10,... | collective-permute-start | bytes 196616 | tf_op jit(solution)/shard_map/ppermute | solution.py:303
  22.3 3.6 %collective-permute-start.8 = (f32[64,256]{1,0:T(8,128)S(1)}, f32[64,256]{1,0:T(8,128)S(1)}, u32[]{:S(2)}, u32[]{:S(2)}) collective-permute-start(f32[64,256]{1,0:T(8,128)S(1)} %get-tuple-element.41), channel_id=1, source_target_pairs={{0,6},{1,7},{2,4},{3,5},{4,2},{5,3},{6,0},{7,1},{8,14},{9,15},{10,... | collective-permute-start | bytes 196616 | tf_op jit(solution)/shard_map/ppermute | solution.py:303
  25.9 0.0 collective-permute-start.9
  25.9 0.1 slice.19.tiles
  26.0 1.0 %shard_map.85.so_far = f32[128,768]{1,0:T(8,128)S(1)} custom-call(s32[5]{0:T(128)S(1)} %bitcast.7, s32[1,768]{1,0:T(1,128)S(1)} %get-tuple-element.32.source, f32[64,256]{1,0:T(8,128)S(1)} %get-tuple-element.35.refs_0_, f32[64,256]{1,0:T(8,128)S(1)} %collective-permute-done.3.refs_1_, f32[64,256]{1,0:T(8,128)S(1)} %collective-permute-done.4.refs_2_, ...), custom_call_target="tpu_custom_call" | custom-call | tf_op jit(solution)/shard_map/pallas_call | solution.py:59
  27.0 4.5 %collective-permute-done.7.refs_0_ = f32[64,256]{1,0:T(8,128)S(1)} collective-permute-done((f32[64,256]{1,0:T(8,128)S(1)}, f32[64,256]{1,0:T(8,128)S(1)}, u32[]{:S(2)}, u32[]{:S(2)}) %collective-permute-start.7) | collective-permute-done | bytes 65568 | tf_op jit(solution)/shard_map/ppermute | solution.py:303
  31.4 1.5 %collective-permute-done.9.refs_2_ = f32[64,256]{1,0:T(8,128)S(1)} collective-permute-done((f32[64,256]{1,0:T(8,128)S(1)}, f32[64,256]{1,0:T(8,128)S(1)}, u32[]{:S(2)}, u32[]{:S(2)}) %collective-permute-start.9) | collective-permute-done | bytes 65568 | tf_op jit(solution)/shard_map/ppermute | solution.py:303
  32.9 1.1 %shard_map.86 = (f32[64,768]{1,0:T(8,128)S(1)}, f32[64,512]{1,0:T(8,128)S(1)}) custom-call(s32[3]{0:T(128)S(1)} %pad_add_fusion.me, s32[3]{0:T(128)S(1)} %slice.19.tiles, s32[1,768]{1,0:T(1,128)S(1)} %get-tuple-element.32.source, bf16[2,256,256]{2,1,0:T(8,128)(2,1)S(1)} %get-tuple-element.33.high, bf16[2,256,256]{2,1,0:T(8,128)(2,1)S(1)} %get-tuple-element.34.low, ...), custom_call_target="tpu_custom_call" | custom-call | tf_op jit(solution)/shard_map/pallas_call | solution.py:59
  34.0 0.6 collective-permute-start.11
  34.6 1.5 %collective-permute-start.10 = (f32[64,768]{1,0:T(8,128)S(1)}, f32[64,768]{1,0:T(8,128)S(1)}, u32[]{:S(2)}, u32[]{:S(2)}) collective-permute-start(f32[64,768]{1,0:T(8,128)S(1)} %get-tuple-element.43.refs_0_), channel_id=1, source_target_pairs={{0,2},{2,4},{4,6},{6,7},{7,5},{5,3},{3,1},{1,0},{8,10},{10,12},{12... | collective-permute-start | bytes 589832 | tf_op jit(solution)/shard_map/ppermute | solution.py:346
  36.1 4.5 %collective-permute-done.11.refs_2_ = f32[64,768]{1,0:T(8,128)S(1)} collective-permute-done((f32[64,768]{1,0:T(8,128)S(1)}, f32[64,768]{1,0:T(8,128)S(1)}, u32[]{:S(2)}, u32[]{:S(2)}) %collective-permute-start.11) | collective-permute-done | bytes 196640 | tf_op jit(solution)/shard_map/ppermute | solution.py:350
  40.6 0.3 collective-permute-start.13
  40.8 0.5 collective-permute-done.10.refs_1_
  41.3 1.3 %collective-permute-start.12 = (f32[64,768]{1,0:T(8,128)S(1)}, f32[64,768]{1,0:T(8,128)S(1)}, u32[]{:S(2)}, u32[]{:S(2)}) collective-permute-start(f32[64,768]{1,0:T(8,128)S(1)} %collective-permute-done.10.refs_1_), channel_id=1, source_target_pairs={{0,2},{2,4},{4,6},{6,7},{7,5},{5,3},{3,1},{1,0},{8,10},{10,12},{12... | collective-permute-start | bytes 589832 | tf_op jit(solution)/shard_map/ppermute | solution.py:346
  42.6 1.6 %collective-permute-start.16 = (f32[64,512]{1,0:T(8,128)S(1)}, f32[64,512]{1,0:T(8,128)S(1)}, u32[]{:S(2)}, u32[]{:S(2)}) collective-permute-start(f32[64,512]{1,0:T(8,128)S(1)} %get-tuple-element.44), channel_id=1, source_target_pairs={{0,16},{1,24},{2,0},{3,8},{8,17},{9,25},{10,1},{11,9},{16,18},{17,... | collective-permute-start | bytes 393224 | tf_op jit(solution)/shard_map/ppermute | solution.py:328
  44.2 0.7 collective-permute-start.15
  44.8 0.7 collective-permute-start.19
  45.5 1.7 %collective-permute-done.13.refs_4_ = f32[64,768]{1,0:T(8,128)S(1)} collective-permute-done((f32[64,768]{1,0:T(8,128)S(1)}, f32[64,768]{1,0:T(8,128)S(1)}, u32[]{:S(2)}, u32[]{:S(2)}) %collective-permute-start.13) | collective-permute-done | bytes 196640 | tf_op jit(solution)/shard_map/ppermute | solution.py:350
  47.2 1.7 %collective-permute-start.17 = (f32[64,768]{1,0:T(8,128)S(1)}, f32[64,768]{1,0:T(8,128)S(1)}, u32[]{:S(2)}, u32[]{:S(2)}) collective-permute-start(f32[64,768]{1,0:T(8,128)S(1)} %collective-permute-done.13.refs_4_), channel_id=1, source_target_pairs={{2,0},{4,2},{6,4},{7,6},{5,7},{3,5},{1,3},{0,1},{10,8},{12,10},{14... | collective-permute-start | bytes 589832 | tf_op jit(solution)/shard_map/ppermute | solution.py:350
  48.9 1.5 %collective-permute-start.14 = (f32[64,768]{1,0:T(8,128)S(1)}, f32[64,768]{1,0:T(8,128)S(1)}, u32[]{:S(2)}, u32[]{:S(2)}) collective-permute-start(f32[64,768]{1,0:T(8,128)S(1)} %collective-permute-done.12.refs_3_), channel_id=1, source_target_pairs={{0,2},{2,4},{4,6},{6,7},{7,5},{5,3},{3,1},{1,0},{8,10},{10,12},{12... | collective-permute-start | bytes 589832 | tf_op jit(solution)/shard_map/ppermute | solution.py:346
  50.4 5.8 %collective-permute-done.14.refs_5_ = f32[64,768]{1,0:T(8,128)S(1)} collective-permute-done((f32[64,768]{1,0:T(8,128)S(1)}, f32[64,768]{1,0:T(8,128)S(1)}, u32[]{:S(2)}, u32[]{:S(2)}) %collective-permute-start.14) | collective-permute-done | bytes 196640 | tf_op jit(solution)/shard_map/ppermute | solution.py:346
  56.3 0.3 collective-permute-done.17.refs_6_
  56.5 0.6 shard_map.87.refs_13_
  57.2 0.7 collective-permute-start.20
  57.9 0.3 collective-permute-start.18
  58.2 0.7 collective-permute-start.24
  58.8 1.3 %collective-permute-start.23 = (f32[256,256]{1,0:T(8,128)S(1)}, f32[256,256]{1,0:T(8,128)S(1)}, u32[]{:S(2)}, u32[]{:S(2)}) collective-permute-start(f32[256,256]{1,0:T(8,128)S(1)} %shard_map.87.refs_13_), channel_id=1, source_target_pairs={{8,0},{9,1},{10,2},{11,3},{12,4},{13,5},{14,6},{15,7}} | collective-permute-start | bytes 786440 | tf_op jit(solution)/shard_map/ppermute | solution.py:363
  60.1 4.7 %collective-permute-start.21 = (f32[64,512]{1,0:T(8,128)S(1)}, f32[64,512]{1,0:T(8,128)S(1)}, u32[]{:S(2)}, u32[]{:S(2)}) collective-permute-start(f32[64,512]{1,0:T(8,128)S(1)} %collective-permute-done.15.refs_8_), channel_id=1, source_target_pairs={{0,8},{8,0},{16,24},{24,16},{1,9},{9,1},{17,25},{25,17},{2,10},{10... | collective-permute-start | bytes 393224 | tf_op jit(solution)/shard_map/ppermute | solution.py:254
  64.8 0.8 %collective-permute-done.18.refs_7_ = f32[64,768]{1,0:T(8,128)S(1)} collective-permute-done((f32[64,768]{1,0:T(8,128)S(1)}, f32[64,768]{1,0:T(8,128)S(1)}, u32[]{:S(2)}, u32[]{:S(2)}) %collective-permute-start.18) | collective-permute-done | bytes 196640 | tf_op jit(solution)/shard_map/ppermute | solution.py:346
  65.6 0.4 collective-permute-start.22
  66.0 1.0 %collective-permute-done.22.refs_11_ = f32[64,512]{1,0:T(8,128)S(1)} collective-permute-done((f32[64,512]{1,0:T(8,128)S(1)}, f32[64,512]{1,0:T(8,128)S(1)}, u32[]{:S(2)}, u32[]{:S(2)}) %collective-permute-start.22) | collective-permute-done | bytes 131104 | tf_op jit(solution)/shard_map/ppermute | solution.py:254
  67.0 3.3 %shard_map.88 = f32[512,256]{1,0:T(8,128)} custom-call(s32[8]{0:T(128)S(1)} %compare_select_fusion.2.rank.order, s32[4]{0:T(128)S(1)} %broadcast_xor_fusion.own_order, s32[3]{0:T(128)S(1)} %pad_add_fusion.me, s32[1,512]{1,0:T(1,128)S(1)} %get-tuple-element.28.target, f32[512,256]{1,0:T(8,128)S(1)} %get-tuple-element.31.block, f32[2,256,256]{2,1,0:T(8,128)S(1)} %copy-done.2, ...), custom_call_target="tpu_custom_call" | custom-call | tf_op jit(solution)/shard_map/pallas_call | solution.py:59
  (36 shorter events, 0.2 us)
Async XLA Ops:
  0.0 0.7 copy-start.3
  0.7 1.0 %copy-start = (f32[512,256]{1,0:T(8,128)S(1)}, f32[512,256]{1,0:T(8,128)}, u32[]{:S(2)}) copy-start(f32[512,256]{1,0:T(8,128)} %block.3) | copy-start | bytes 1572868
  3.5 1.7 %collective-permute-start = (f32[256,256]{1,0:T(8,128)S(1)}, f32[256,256]{1,0:T(8,128)S(1)}, u32[]{:S(2)}, u32[]{:S(2)}) collective-permute-start(f32[256,256]{1,0:T(8,128)S(1)} %get-tuple-element.30), channel_id=1, source_target_pairs={{0,8},{8,0},{16,24},{24,16},{1,9},{9,1},{17,25},{25,17},{2,10},{10... | collective-permute-start | bytes 786440 | tf_op jit(solution)/shard_map/ppermute | solution.py:254
  5.3 6.9 %copy-start.2 = (f32[2,256,256]{2,1,0:T(8,128)S(1)}, f32[2,256,256]{2,1,0:T(8,128)}, u32[]{:S(2)}) copy-start(f32[2,256,256]{2,1,0:T(8,128)} %inverses.3) | copy-start | bytes 1572868
  5.3 8.2 %copy-start.1 = (f32[512,256]{1,0:T(8,128)S(1)}, f32[512,256]{1,0:T(8,128)}, u32[]{:S(2)}) copy-start(f32[512,256]{1,0:T(8,128)} %block.3) | copy-start | bytes 1572868
  5.3 6.7 %collective-permute-start.1 = (f32[128,256]{1,0:T(8,128)S(1)}, f32[128,256]{1,0:T(8,128)S(1)}, u32[]{:S(2)}, u32[]{:S(2)}) collective-permute-start(f32[128,256]{1,0:T(8,128)S(1)} %slice_select_fusion.1), channel_id=1, source_target_pairs={{0,16},{8,24},{16,0},{24,8},{1,17},{9,25},{17,1},{25,9},{2,18},{10... | collective-permute-start | bytes 393224 | tf_op jit(solution)/shard_map/ppermute | solution.py:254
  12.1 1.4 %collective-permute-start.2 = (f32[128,256]{1,0:T(8,128)S(1)}, f32[128,256]{1,0:T(8,128)S(1)}, u32[]{:S(2)}, u32[]{:S(2)}) collective-permute-start(f32[128,256]{1,0:T(8,128)S(1)} %get-tuple-element.51.mine), channel_id=1, source_target_pairs={{0,8},{8,0},{16,24},{24,16},{1,9},{9,1},{17,25},{25,17},{2,10},{10... | collective-permute-start | bytes 393224 | tf_op jit(solution)/shard_map/ppermute | solution.py:254
  14.6 7.6 %collective-permute-start.3 = (f32[64,256]{1,0:T(8,128)S(1)}, f32[64,256]{1,0:T(8,128)S(1)}, u32[]{:S(2)}, u32[]{:S(2)}) collective-permute-start(f32[64,256]{1,0:T(8,128)S(1)} %get-tuple-element.36), channel_id=1, source_target_pairs={{0,1},{1,0},{2,3},{3,2},{4,5},{5,4},{6,7},{7,6},{8,9},{9,8},{10,11... | collective-permute-start | bytes 196616 | tf_op jit(solution)/shard_map/ppermute | solution.py:303
  16.4 9.5 %collective-permute-start.4 = (f32[64,256]{1,0:T(8,128)S(1)}, f32[64,256]{1,0:T(8,128)S(1)}, u32[]{:S(2)}, u32[]{:S(2)}) collective-permute-start(f32[64,256]{1,0:T(8,128)S(1)} %get-tuple-element.37), channel_id=1, source_target_pairs={{0,2},{1,3},{2,0},{3,1},{4,6},{5,7},{6,4},{7,5},{8,10},{9,11},{10,... | collective-permute-start | bytes 196616 | tf_op jit(solution)/shard_map/ppermute | solution.py:303
  18.0 8.0 %collective-permute-start.5 = (f32[64,256]{1,0:T(8,128)S(1)}, f32[64,256]{1,0:T(8,128)S(1)}, u32[]{:S(2)}, u32[]{:S(2)}) collective-permute-start(f32[64,256]{1,0:T(8,128)S(1)} %get-tuple-element.38), channel_id=1, source_target_pairs={{0,3},{1,2},{2,1},{3,0},{4,7},{5,6},{6,5},{7,4},{8,11},{9,10},{10,... | collective-permute-start | bytes 196616 | tf_op jit(solution)/shard_map/ppermute | solution.py:303
  18.2 7.8 %collective-permute-start.6 = (f32[64,256]{1,0:T(8,128)S(1)}, f32[64,256]{1,0:T(8,128)S(1)}, u32[]{:S(2)}, u32[]{:S(2)}) collective-permute-start(f32[64,256]{1,0:T(8,128)S(1)} %get-tuple-element.39), channel_id=1, source_target_pairs={{0,4},{1,5},{2,6},{3,7},{4,0},{5,1},{6,2},{7,3},{8,12},{9,13},{10,... | collective-permute-start | bytes 196616 | tf_op jit(solution)/shard_map/ppermute | solution.py:303
  21.0 10.5 %collective-permute-start.7 = (f32[64,256]{1,0:T(8,128)S(1)}, f32[64,256]{1,0:T(8,128)S(1)}, u32[]{:S(2)}, u32[]{:S(2)}) collective-permute-start(f32[64,256]{1,0:T(8,128)S(1)} %get-tuple-element.40), channel_id=1, source_target_pairs={{0,5},{1,4},{2,7},{3,6},{4,1},{5,0},{6,3},{7,2},{8,13},{9,12},{10,... | collective-permute-start | bytes 196616 | tf_op jit(solution)/shard_map/ppermute | solution.py:303
  22.3 9.2 %collective-permute-start.8 = (f32[64,256]{1,0:T(8,128)S(1)}, f32[64,256]{1,0:T(8,128)S(1)}, u32[]{:S(2)}, u32[]{:S(2)}) collective-permute-start(f32[64,256]{1,0:T(8,128)S(1)} %get-tuple-element.41), channel_id=1, source_target_pairs={{0,6},{1,7},{2,4},{3,5},{4,2},{5,3},{6,0},{7,1},{8,14},{9,15},{10,... | collective-permute-start | bytes 196616 | tf_op jit(solution)/shard_map/ppermute | solution.py:303
  25.9 7.1 %collective-permute-start.9 = (f32[64,256]{1,0:T(8,128)S(1)}, f32[64,256]{1,0:T(8,128)S(1)}, u32[]{:S(2)}, u32[]{:S(2)}) collective-permute-start(f32[64,256]{1,0:T(8,128)S(1)} %get-tuple-element.42), channel_id=1, source_target_pairs={{0,7},{1,6},{2,5},{3,4},{4,3},{5,2},{6,1},{7,0},{8,15},{9,14},{10,... | collective-permute-start | bytes 196616 | tf_op jit(solution)/shard_map/ppermute | solution.py:303
  34.0 6.5 %collective-permute-start.11 = (f32[64,768]{1,0:T(8,128)S(1)}, f32[64,768]{1,0:T(8,128)S(1)}, u32[]{:S(2)}, u32[]{:S(2)}) collective-permute-start(f32[64,768]{1,0:T(8,128)S(1)} %get-tuple-element.43.refs_0_), channel_id=1, source_target_pairs={{2,0},{4,2},{6,4},{7,6},{5,7},{3,5},{1,3},{0,1},{10,8},{12,10},{14... | collective-permute-start | bytes 589832 | tf_op jit(solution)/shard_map/ppermute | solution.py:350
  34.6 6.7 %collective-permute-start.10 = (f32[64,768]{1,0:T(8,128)S(1)}, f32[64,768]{1,0:T(8,128)S(1)}, u32[]{:S(2)}, u32[]{:S(2)}) collective-permute-start(f32[64,768]{1,0:T(8,128)S(1)} %get-tuple-element.43.refs_0_), channel_id=1, source_target_pairs={{0,2},{2,4},{4,6},{6,7},{7,5},{5,3},{3,1},{1,0},{8,10},{10,12},{12... | collective-permute-start | bytes 589832 | tf_op jit(solution)/shard_map/ppermute | solution.py:346
  40.6 6.6 %collective-permute-start.13 = (f32[64,768]{1,0:T(8,128)S(1)}, f32[64,768]{1,0:T(8,128)S(1)}, u32[]{:S(2)}, u32[]{:S(2)}) collective-permute-start(f32[64,768]{1,0:T(8,128)S(1)} %collective-permute-done.11.refs_2_), channel_id=1, source_target_pairs={{2,0},{4,2},{6,4},{7,6},{5,7},{3,5},{1,3},{0,1},{10,8},{12,10},{14... | collective-permute-start | bytes 589832 | tf_op jit(solution)/shard_map/ppermute | solution.py:350
  41.3 7.6 %collective-permute-start.12 = (f32[64,768]{1,0:T(8,128)S(1)}, f32[64,768]{1,0:T(8,128)S(1)}, u32[]{:S(2)}, u32[]{:S(2)}) collective-permute-start(f32[64,768]{1,0:T(8,128)S(1)} %collective-permute-done.10.refs_1_), channel_id=1, source_target_pairs={{0,2},{2,4},{4,6},{6,7},{7,5},{5,3},{3,1},{1,0},{8,10},{10,12},{12... | collective-permute-start | bytes 589832 | tf_op jit(solution)/shard_map/ppermute | solution.py:346
  42.6 7.8 %copy-start.8 = (s32[8]{0:T(128)S(1)}, s32[8]{0:T(128)}, u32[]{:S(2)}) copy-start(s32[8]{0:T(128)} %constant.63.clone) | copy-start | bytes 100
  42.6 7.8 %collective-permute-start.16 = (f32[64,512]{1,0:T(8,128)S(1)}, f32[64,512]{1,0:T(8,128)S(1)}, u32[]{:S(2)}, u32[]{:S(2)}) collective-permute-start(f32[64,512]{1,0:T(8,128)S(1)} %get-tuple-element.44), channel_id=1, source_target_pairs={{0,16},{1,24},{2,0},{3,8},{8,17},{9,25},{10,1},{11,9},{16,18},{17,... | collective-permute-start | bytes 393224 | tf_op jit(solution)/shard_map/ppermute | solution.py:328
  44.2 6.2 %collective-permute-start.15 = (f32[64,512]{1,0:T(8,128)S(1)}, f32[64,512]{1,0:T(8,128)S(1)}, u32[]{:S(2)}, u32[]{:S(2)}) collective-permute-start(f32[64,512]{1,0:T(8,128)S(1)} %get-tuple-element.44), channel_id=1, source_target_pairs={{0,0},{1,8},{2,16},{3,24},{8,1},{9,9},{10,17},{11,25},{16,2},{17,1... | collective-permute-start | bytes 393224 | tf_op jit(solution)/shard_map/ppermute | solution.py:328
  44.8 11.4 %collective-permute-start.19 = (f32[64,256]{1,0:T(8,128)S(1)}, f32[64,256]{1,0:T(8,128)S(1)}, u32[]{:S(2)}, u32[]{:S(2)}) collective-permute-start(f32[64,256]{1,0:T(8,128)S(1)} %slice.21), channel_id=1, source_target_pairs={{8,15},{9,14},{10,13},{11,12}} | collective-permute-start | bytes 196616 | tf_op jit(solution)/shard_map/ppermute | solution.py:361
  47.2 9.4 %collective-permute-start.17 = (f32[64,768]{1,0:T(8,128)S(1)}, f32[64,768]{1,0:T(8,128)S(1)}, u32[]{:S(2)}, u32[]{:S(2)}) collective-permute-start(f32[64,768]{1,0:T(8,128)S(1)} %collective-permute-done.13.refs_4_), channel_id=1, source_target_pairs={{2,0},{4,2},{6,4},{7,6},{5,7},{3,5},{1,3},{0,1},{10,8},{12,10},{14... | collective-permute-start | bytes 589832 | tf_op jit(solution)/shard_map/ppermute | solution.py:350
  48.9 7.4 %collective-permute-start.14 = (f32[64,768]{1,0:T(8,128)S(1)}, f32[64,768]{1,0:T(8,128)S(1)}, u32[]{:S(2)}, u32[]{:S(2)}) collective-permute-start(f32[64,768]{1,0:T(8,128)S(1)} %collective-permute-done.12.refs_3_), channel_id=1, source_target_pairs={{0,2},{2,4},{4,6},{6,7},{7,5},{5,3},{3,1},{1,0},{8,10},{10,12},{12... | collective-permute-start | bytes 589832 | tf_op jit(solution)/shard_map/ppermute | solution.py:346
  50.4 15.6 %copy-start.7 = (s32[4]{0:T(128)S(1)}, s32[4]{0:T(128)}, u32[]{:S(2)}) copy-start(s32[4]{0:T(128)} %constant.64.clone) | copy-start | bytes 52
  56.5 10.4 %copy-start.5 = (f32[2,256]{1,0:T(2,128)S(1)}, f32[2,256]{1,0:T(2,128)}, u32[]{:S(2)}) copy-start(f32[2,256]{1,0:T(2,128)} %couplings.1) | copy-start | bytes 6148
  56.5 10.4 %copy-start.6 = (s32[2,256]{1,0:T(2,128)S(1)}, s32[2,256]{1,0:T(2,128)}, u32[]{:S(2)}) copy-start(s32[2,256]{1,0:T(2,128)} %pattern.1) | copy-start | bytes 6148
  57.2 9.8 %copy-start.4 = (f32[2,256]{1,0:T(2,128)S(1)}, f32[2,256]{1,0:T(2,128)}, u32[]{:S(2)}) copy-start(f32[2,256]{1,0:T(2,128)} %pivots.1) | copy-start | bytes 6148
  57.2 8.4 %collective-permute-start.20 = (f32[256,256]{1,0:T(8,128)S(1)}, f32[256,256]{1,0:T(8,128)S(1)}, u32[]{:S(2)}, u32[]{:S(2)}) collective-permute-start(f32[256,256]{1,0:T(8,128)S(1)} %shard_map.87.refs_13_), channel_id=1, source_target_pairs={{8,16},{9,17},{10,18},{11,19},{12,20},{13,21},{14,22},{15,23}} | collective-permute-start | bytes 786440 | tf_op jit(solution)/shard_map/ppermute | solution.py:363
  57.9 7.7 %collective-permute-start.18 = (f32[64,768]{1,0:T(8,128)S(1)}, f32[64,768]{1,0:T(8,128)S(1)}, u32[]{:S(2)}, u32[]{:S(2)}) collective-permute-start(f32[64,768]{1,0:T(8,128)S(1)} %collective-permute-done.14.refs_5_), channel_id=1, source_target_pairs={{0,2},{2,4},{4,6},{6,7},{7,5},{5,3},{3,1},{1,0},{8,10},{10,12},{12... | collective-permute-start | bytes 589832 | tf_op jit(solution)/shard_map/ppermute | solution.py:346
  58.2 7.8 %collective-permute-start.24 = (f32[256,256]{1,0:T(8,128)S(1)}, f32[256,256]{1,0:T(8,128)S(1)}, u32[]{:S(2)}, u32[]{:S(2)}) collective-permute-start(f32[256,256]{1,0:T(8,128)S(1)} %shard_map.87.refs_13_), channel_id=1, source_target_pairs={{8,24},{9,25},{10,26},{11,27},{12,28},{13,29},{14,30},{15,31}} | collective-permute-start | bytes 786440 | tf_op jit(solution)/shard_map/ppermute | solution.py:363
  58.8 7.2 %collective-permute-start.23 = (f32[256,256]{1,0:T(8,128)S(1)}, f32[256,256]{1,0:T(8,128)S(1)}, u32[]{:S(2)}, u32[]{:S(2)}) collective-permute-start(f32[256,256]{1,0:T(8,128)S(1)} %shard_map.87.refs_13_), channel_id=1, source_target_pairs={{8,0},{9,1},{10,2},{11,3},{12,4},{13,5},{14,6},{15,7}} | collective-permute-start | bytes 786440 | tf_op jit(solution)/shard_map/ppermute | solution.py:363
  60.1 5.9 %collective-permute-start.21 = (f32[64,512]{1,0:T(8,128)S(1)}, f32[64,512]{1,0:T(8,128)S(1)}, u32[]{:S(2)}, u32[]{:S(2)}) collective-permute-start(f32[64,512]{1,0:T(8,128)S(1)} %collective-permute-done.15.refs_8_), channel_id=1, source_target_pairs={{0,8},{8,0},{16,24},{24,16},{1,9},{9,1},{17,25},{25,17},{2,10},{10... | collective-permute-start | bytes 393224 | tf_op jit(solution)/shard_map/ppermute | solution.py:254
  65.6 1.4 %collective-permute-start.22 = (f32[64,512]{1,0:T(8,128)S(1)}, f32[64,512]{1,0:T(8,128)S(1)}, u32[]{:S(2)}, u32[]{:S(2)}) collective-permute-start(f32[64,512]{1,0:T(8,128)S(1)} %collective-permute-done.16.refs_9_), channel_id=1, source_target_pairs={{0,8},{8,0},{16,24},{24,16},{1,9},{9,1},{17,25},{25,17},{2,10},{10... | collective-permute-start | bytes 393224 | tf_op jit(solution)/shard_map/ppermute | solution.py:254
